TPU v7x, 512 devices: a whole 4x8x8 slice. The times are simulated.
512 devices in a mesh: dp: 64 (over z, y_lo, core), mp: 8 (over y_hi, x).
Axes of the slice: x: 4, y: 8 (y_hi: 2, y_lo: 4; y = y_hi * 4 + y_lo), z: 8, core: 2. Of those that a mesh axis runs over, the one named last changes fastest.
Arguments:
- residual: bfloat16 [16384, 4608], P('dp', 'mp'), may hold values from -6 to 6
- out_grad: bfloat16 [16384, 4608], P('dp', 'mp'), may hold values from -6 to 6
- ffn_weights: bfloat16 [3, 256, 4608], P(None, 'mp'), may hold values from -0.09375 to 0.09375
- norm_gain: float32 [4608], replicated, may hold values from 0.1 to 1.9
- exponents: int32 [3], replicated, may hold values from 3 to 6, as said below
- sign_bits: int32 [4608], replicated, may hold values from 0 to 1
Outputs:
- resid_grad: bfloat16 [16384, 4608], P('dp', 'mp')
- weight_grads: bfloat16 [3, 256, 4608], P(None, 'mp')
Inputs may be any that keep to these rules, and one draw needn't show every extreme that they name: `exponents`: one exponent for each of the gate, up and down gradients; every draw holds both 3 and 6. `sign_bits`: one bit per feature.
All inputs are finite; a program needn't handle non-finite values.
Results may differ from a plain program's by a relative error of at most 0.01.
Values may be sent and summed in bfloat16 or wider, within the bound.
No kernel may reach another device: no remote copies, remote signals or barrier semaphores. Data moves between devices by JAX's collectives and lax.ppermute only.
A program may use at most 64 MiB of HBM per device.

v0:
```python
import math

import jax
import jax.numpy as jnp
from jax import lax
from jax.sharding import PartitionSpec as P


def hadamard():
    indices = jnp.arange(128, dtype=jnp.int32)
    anded = jnp.bitwise_and(indices[:, None], indices[None, :])
    parity = jnp.zeros((128, 128), jnp.int32)
    for offset in range(7):
        parity = parity + jnp.bitwise_and(jnp.right_shift(anded, offset), 1)
    return (1 - 2 * (parity % 2)).astype(jnp.float32) / math.sqrt(128.0)


def gelu_parts(values):
    tanh_input = 0.7978845608 * (values + 0.044715 * values * values * values)
    tanhed = jnp.tanh(tanh_input)
    forward = 0.5 * values * (1.0 + tanhed)
    gelu_slope = 0.5 * (1.0 + tanhed) + 0.5 * values * (1.0 - tanhed * tanhed) * 0.7978845608 * (
        1.0 + 3.0 * 0.044715 * values * values
    )
    return (forward, gelu_slope)


def restore(summed, factors, sign_table, hadamard_table):
    block_count = sign_table.shape[0]
    widened = lax.optimization_barrier(summed).astype(jnp.float32).reshape(3, -1, block_count, 128)
    scaled = widened * factors[:, None, None, None]
    restored = (
        jnp.einsum("kubj,jc->kubc", scaled, hadamard_table, precision=lax.Precision.HIGHEST)
        * sign_table
    )
    return restored.astype(jnp.bfloat16).reshape(3, -1, block_count * 128)


def per_device(residual, out_grad, ffn_weights, norm_gain, exponents, sign_bits):
    full_rows, grads_in = (
        lax.all_gather(residual, "mp", axis=1, tiled=True),
        lax.all_gather(out_grad, "mp", axis=1, tiled=True),
    )
    feature_count = full_rows.shape[1]
    col_count = residual.shape[1]
    col_start = lax.axis_index("mp") * col_count
    bucket_rows = ffn_weights.shape[1]
    rows_wide = full_rows.astype(jnp.float32)
    inverse = lax.rsqrt(jnp.mean(rows_wide * rows_wide, axis=1, keepdims=True) + 1e-06)
    unit_rows = rows_wide * inverse
    normed = (unit_rows * norm_gain).astype(jnp.bfloat16)
    pair_weights = ffn_weights[:2]
    gate_up = jnp.einsum("td,khd->tkh", normed, pair_weights, preferred_element_type=jnp.float32)
    gate_pre = gate_up[:, 0]
    up_proj = gate_up[:, 1]
    activated, gelu_slope = gelu_parts(gate_pre)
    hidden = (activated * up_proj).astype(jnp.bfloat16)
    hidden_grad = lax.dot_general(
        grads_in, ffn_weights[2], (((1,), (1,)), ((), ())), preferred_element_type=jnp.float32
    )
    gate_grad = (hidden_grad * up_proj * gelu_slope).astype(jnp.bfloat16)
    up_grad = (hidden_grad * activated).astype(jnp.bfloat16)
    pair_grad = jnp.stack([gate_grad, up_grad], axis=1)
    partial_value = jnp.einsum(
        "tkh,khd->td", pair_grad, pair_weights, preferred_element_type=jnp.float32
    )
    own_unit = lax.dynamic_slice_in_dim(unit_rows, col_start, col_count, 1)
    normed_grad = lax.psum(partial_value.astype(jnp.bfloat16), "mp").astype(jnp.float32)
    feature_grad = normed_grad * norm_gain
    row_mean = jnp.sum(feature_grad * unit_rows, axis=1, keepdims=True) / feature_count
    own_grad = lax.dynamic_slice_in_dim(feature_grad, col_start, col_count, 1)
    resid_grad = (out_grad.astype(jnp.float32) + inverse * (own_grad - own_unit * row_mean)).astype(
        jnp.bfloat16
    )
    pair_wgrad = jnp.einsum("tkh,td->khd", pair_grad, normed, preferred_element_type=jnp.float32)
    down_wgrad = lax.dot_general(
        hidden, grads_in, (((0,), (0,)), ((), ())), preferred_element_type=jnp.float32
    )
    stacked = jnp.concatenate([pair_wgrad, down_wgrad[None]], axis=0)
    block_count = feature_count // 128
    sign_table = (2 * sign_bits - 1).astype(jnp.float32).reshape(block_count, 128)
    hadamard_table = hadamard()
    shaped = stacked.reshape(3, bucket_rows, block_count, 128) * sign_table
    rotated = jnp.einsum("kubj,jc->kubc", shaped, hadamard_table, precision=lax.Precision.HIGHEST)
    scales = jnp.exp2(exponents.astype(jnp.float32))
    quantized = jnp.clip(rotated * scales[:, None, None, None], -127.0, 127.0).astype(jnp.bfloat16)
    flat_terms = lax.optimization_barrier(quantized).astype(jnp.float32).reshape(-1, 128)
    factors = jnp.exp2(-exponents.astype(jnp.float32)) / float(lax.axis_size("dp"))
    own_share = lax.psum_scatter(flat_terms, "dp", scatter_dimension=0, tiled=True).astype(
        jnp.bfloat16
    )
    gathered = lax.all_gather(own_share, "dp", axis=0, tiled=True)
    weight_grads = restore(gathered, factors, sign_table, hadamard_table)
    return (resid_grad, weight_grads)


def solution(mesh):
    placed = (P("dp", "mp"), P("dp", "mp"), P(None, "mp", None), P(), P(), P())
    return jax.shard_map(
        per_device,
        mesh=mesh,
        in_specs=placed,
        out_specs=(P("dp", "mp"), P(None, "mp", None)),
        check_vma=False,
    )
```

profile of v0, /device:TPU:1, one launch (start us, length us, event | category | flops | bytes accessed | tf_op | source)
XLA Modules:
  0.0 517.4 jit_solution(12886427552994358560)
XLA Ops:
  9.4 1.3 convert_bitcast_fusion
  10.7 88.5 %all-gather.4.cloned.1.call-done = bf16[256,4608]{0,1:T(8,128)(2,1)} async-done(((bf16[256,576]{0,1:T(8,128)(2,1)}), bf16[256,4608]{0,1:T(8,128)(2,1)}) %all-gather.4.cloned.1.call-update) | async-done | bytes 2359312 | tf_op jit(solution)/shard_map/all_gather | solution.py:41
  99.2 2.8 copy.17
  103.2 0.9 fusion.14
  104.2 79.4 %all-gather.6.cloned.1.call-done = bf16[256,4608]{0,1:T(8,128)(2,1)} async-done(((bf16[256,576]{0,1:T(8,128)(2,1)}), bf16[256,4608]{0,1:T(8,128)(2,1)}) %all-gather.6.cloned.1.call-update) | async-done | bytes 2359312 | tf_op jit(solution)/shard_map/all_gather | solution.py:42
  183.6 2.2 fusion.65
  187.0 2.2 fusion.1
  189.2 1.3 concatenate.6
  190.4 2.6 convolution_bitcast_fusion.1
  193.4 1.8 clamp_convert_fusion
  195.2 1.4 reshape.51
  196.6 178.1 %fusion = f32[64,128]{1,0:T(8,128)S(1)} fusion(f32[3456,128]{1,0:T(8,128)} %reshape.51), kind=kCustom, calls=%all-reduce-scatter | all-reduce-scatter fusion | flops 524289 | bytes 1804288
  374.7 3.5 collective-permute-start
  378.2 1.3 collective-permute-start.1
  379.5 1.3 collective-permute-start.2
  380.8 1.3 collective-permute-start.3
  382.2 1.3 collective-permute-start.9
  384.3 1.3 collective-permute-start.4
  385.6 19.8 %collective-permute-start.5 = (bf16[64,128]{1,0:T(8,128)(2,1)S(1)}, bf16[64,128]{1,0:T(8,128)(2,1)S(1)}, u32[]{:S(2)}, u32[]{:S(2)}) collective-permute-start(bf16[64,128]{1,0:T(8,128)(2,1)S(1)} %convert.20), channel_id=1, source_target_pairs={{0,48},{8,56},{16,64},{24,72},{32,80},{40,88},{48,96},{56,104},{64... | collective-permute-start | bytes 49160
  405.4 1.9 collective-permute-start.6
  407.4 4.2 collective-permute-start.7
  411.6 3.7 collective-permute-start.8
  415.3 0.9 copy.16
  416.3 1.3 dynamic-slice.4
  418.2 1.8 concatenate.8
  420.0 78.4 %all-gather = bf16[64,54,128]{2,1,0:T(8,128)(2,1)S(1)} all-gather(bf16[1,54,128]{2,1,0:T(8,128)(2,1)S(1)} %fusion.66), channel_id=1, replica_groups=mesh['dp'=64,'mp'=8] {'dp'}, dimensions={0}, use_global_device_ids=true | all-gather | bytes 898560 | tf_op jit(solution)/shard_map/all_gather | solution.py:92
  498.4 1.1 reshape.55
  499.5 2.5 reshape.53
  502.0 3.3 multiply_convert_fusion.1
  505.3 1.4 reshape.49
  506.7 2.8 multiply_reduce_fusion
  510.0 0.9 copy.19
  (47 shorter events, 6.3 us)
Async XLA Ops:
  7.2 92.1 %all-gather.4.cloned.1.call-start = ((), (), s32[]{:S(2)}) async-start(), calls=%async_computation | async-start | bytes 2654208 | tf_op jit(solution)/shard_map/all_gather | solution.py:41
  7.9 175.7 %all-gather.6.cloned.1.call-start = ((), (), s32[]{:S(2)}) async-start(), calls=%async_computation.1 | async-start | bytes 2654208 | tf_op jit(solution)/shard_map/all_gather | solution.py:42
  8.6 498.0 %all-reduce.4.cloned.1.call-start = ((), (), s32[]{:S(2)}) async-start(), calls=%async_computation.2 | async-start | bytes 4718592 | tf_op jit(solution)/shard_map/psum | solution.py:68
  102.1 1.2 copy-start.3
  102.1 1.2 copy-start.7
  104.2 81.6 %copy-start.6 = (f32[256,2,32]{0,2,1:T(8,128)}, f32[256,2,32]{0,2,1:T(8,128)S(1)}, u32[]{:S(2)}) copy-start(f32[256,2,32]{0,2,1:T(8,128)S(1)} %fusion.14) | copy-start | bytes 196612
  183.6 2.2 copy-start.8
  185.8 1.2 copy-start.4
  190.4 3.0 copy-start.1
  190.4 3.0 copy-start.5
  196.6 218.7 %copy-start.2 = (bf16[256,576]{0,1:T(8,128)(2,1)S(1)}, bf16[256,576]{0,1:T(8,128)(2,1)}, u32[]{:S(2)}) copy-start(bf16[256,576]{0,1:T(8,128)(2,1)} %param.7) | copy-start | bytes 884740
  374.7 10.8 %collective-permute-start = (bf16[64,128]{1,0:T(8,128)(2,1)S(1)}, bf16[64,128]{1,0:T(8,128)(2,1)S(1)}, u32[]{:S(2)}, u32[]{:S(2)}) collective-permute-start(bf16[64,128]{1,0:T(8,128)(2,1)S(1)} %convert.20), channel_id=1, source_target_pairs={{0,8},{8,16},{16,24},{24,32},{32,40},{40,48},{48,56},{56,64},{64,7... | collective-permute-start | bytes 49160
  378.2 27.2 %collective-permute-start.1 = (bf16[64,128]{1,0:T(8,128)(2,1)S(1)}, bf16[64,128]{1,0:T(8,128)(2,1)S(1)}, u32[]{:S(2)}, u32[]{:S(2)}) collective-permute-start(bf16[64,128]{1,0:T(8,128)(2,1)S(1)} %convert.20), channel_id=1, source_target_pairs={{0,16},{8,24},{16,32},{24,40},{32,48},{40,56},{48,64},{56,72},{64,... | collective-permute-start | bytes 49160
  379.5 27.8 %collective-permute-start.2 = (bf16[64,128]{1,0:T(8,128)(2,1)S(1)}, bf16[64,128]{1,0:T(8,128)(2,1)S(1)}, u32[]{:S(2)}, u32[]{:S(2)}) collective-permute-start(bf16[64,128]{1,0:T(8,128)(2,1)S(1)} %convert.20), channel_id=1, source_target_pairs={{0,24},{8,32},{16,40},{24,48},{32,56},{40,64},{48,72},{56,80},{64,... | collective-permute-start | bytes 49160
  380.8 30.7 %collective-permute-start.3 = (bf16[64,128]{1,0:T(8,128)(2,1)S(1)}, bf16[64,128]{1,0:T(8,128)(2,1)S(1)}, u32[]{:S(2)}, u32[]{:S(2)}) collective-permute-start(bf16[64,128]{1,0:T(8,128)(2,1)S(1)} %convert.20), channel_id=1, source_target_pairs={{0,32},{8,40},{16,48},{24,56},{32,64},{40,72},{48,80},{56,88},{64,... | collective-permute-start | bytes 49160
  382.2 2.1 collective-permute-start.9
  384.3 33.9 %collective-permute-start.4 = (bf16[64,128]{1,0:T(8,128)(2,1)S(1)}, bf16[64,128]{1,0:T(8,128)(2,1)S(1)}, u32[]{:S(2)}, u32[]{:S(2)}) collective-permute-start(bf16[64,128]{1,0:T(8,128)(2,1)S(1)} %convert.20), channel_id=1, source_target_pairs={{0,40},{8,48},{16,56},{24,64},{32,72},{40,80},{48,88},{56,96},{64,... | collective-permute-start | bytes 49160
  385.6 32.6 %collective-permute-start.5 = (bf16[64,128]{1,0:T(8,128)(2,1)S(1)}, bf16[64,128]{1,0:T(8,128)(2,1)S(1)}, u32[]{:S(2)}, u32[]{:S(2)}) collective-permute-start(bf16[64,128]{1,0:T(8,128)(2,1)S(1)} %convert.20), channel_id=1, source_target_pairs={{0,48},{8,56},{16,64},{24,72},{32,80},{40,88},{48,96},{56,104},{64... | collective-permute-start | bytes 49160
  405.4 12.8 %collective-permute-start.6 = (bf16[64,128]{1,0:T(8,128)(2,1)S(1)}, bf16[64,128]{1,0:T(8,128)(2,1)S(1)}, u32[]{:S(2)}, u32[]{:S(2)}) collective-permute-start(bf16[64,128]{1,0:T(8,128)(2,1)S(1)} %convert.20), channel_id=1, source_target_pairs={{0,56},{8,64},{16,72},{24,80},{32,88},{40,96},{48,104},{56,112},{6... | collective-permute-start | bytes 49160
  407.4 10.8 %collective-permute-start.7 = (bf16[64,128]{1,0:T(8,128)(2,1)S(1)}, bf16[64,128]{1,0:T(8,128)(2,1)S(1)}, u32[]{:S(2)}, u32[]{:S(2)}) collective-permute-start(bf16[64,128]{1,0:T(8,128)(2,1)S(1)} %convert.20), channel_id=1, source_target_pairs={{0,64},{8,72},{16,80},{24,88},{32,96},{40,104},{48,112},{56,120},{... | collective-permute-start | bytes 49160
  411.6 6.6 %collective-permute-start.8 = (bf16[64,128]{1,0:T(8,128)(2,1)S(1)}, bf16[64,128]{1,0:T(8,128)(2,1)S(1)}, u32[]{:S(2)}, u32[]{:S(2)}) collective-permute-start(bf16[64,128]{1,0:T(8,128)(2,1)S(1)} %convert.20), channel_id=1, source_target_pairs={{0,72},{8,80},{16,88},{24,96},{32,104},{40,112},{48,120},{56,128},... | collective-permute-start | bytes 49160
  502.0 4.7 copy-start.9
  506.7 2.8 copy-start
Sparse Core Ops, SparseCore 0:
  11.2 88.0 all-gather.3
  102.4 81.1 all-gather.5
  196.8 152.8 all-reduce.3
where the time goes:
time: 518 us; the launch traced here: 517 us
  blocking collectives  256 us (49%)
  waiting for transfers between devices  170 us (33%)
  starting transfers between devices  39.7 us (8%)
  local copies, waits for them, and re-layouts  16.6 us (3%)
  between operations  14.7 us (3%)
  matrix products  13.8 us (3%)
  other arithmetic  5.85 us (1%)
    unnamed x1, blocking collectives  178 us
    all_gather x1, waiting for transfers between devices, per_device(): lax.all_gather(residual, 'mp', axis=1, tiled=True)  88.5 us
    all_gather x1, waiting for transfers between devices, per_device(): lax.all_gather(out_grad, 'mp', axis=1, tiled=True)  79.4 us
    all_gather x1, blocking collectives, per_device(): gathered = lax.all_gather(own_share, 'dp', axis=0, tiled=True)  78.4 us
    unnamed x10, starting transfers between devices  39.6 us
  transfers between devices with their start and end apart: 13, of which 3 were waited for; matrix products, arithmetic and copies ran while one was open for 38% of the time, Pallas kernels for 0%

commit v1 on v0

v1 whole, which is shorter than its diff:
```python
import functools

import jax
import jax.numpy as jnp
import numpy as np
from jax import lax
from jax.experimental import pallas as pl
from jax.experimental.pallas import tpu as pltpu
from jax.sharding import Mesh
from jax.sharding import PartitionSpec as P

F32 = jnp.float32
BF16 = jnp.bfloat16
DP = ("z", "yl", "c")
MP = ("yh", "x")
VMEM_LIMIT = 40 * 1024 * 1024
FEATURES = 4608
CONTRACT_LAST = (((1,), (1,)), ((), ()))
CONTRACT_FIRST = (((0,), (0,)), ((), ()))


def signed_hadamard():
    table = np.array([[1.0]], np.float32)
    for _ in range(7):
        table = np.block([[table, table], [table, -table]])
    return table


def gelu_parts(values):
    tanh_input = 0.7978845608 * (values + 0.044715 * values * values * values)
    tanhed = jnp.tanh(tanh_input)
    forward = 0.5 * values * (1.0 + tanhed)
    gelu_slope = 0.5 * (1.0 + tanhed) + 0.5 * values * (1.0 - tanhed * tanhed) * 0.7978845608 * (
        1.0 + 3.0 * 0.044715 * values * values
    )
    return (forward, gelu_slope)


def pieces(values):
    high = values.astype(BF16)
    rest = values - high.astype(F32)
    middle = rest.astype(BF16)
    low = (rest - middle.astype(F32)).astype(BF16)
    return (high, middle, low)


def dot(left, right, dims=(((1,), (0,)), ((), ()))):
    return lax.dot_general(left, right, dims, preferred_element_type=F32)


def places():
    odd = lax.axis_index("x") % 2
    pair = lax.axis_index("yh") * 2 + lax.axis_index("x") // 2
    return (lax.axis_index("c"), odd, pair * 9)


def local_rows(table_ref, first, odd):
    rows = [table_ref[pl.ds(first + 5 * odd + b, 1), :] for b in range(4)]
    return jnp.concatenate(rows + [table_ref[pl.ds(first + 4, 1), :]], axis=1)


def forward_kernel(recv_ref, both_ref, x_ref, xh_ref, g_ref, gh_ref, gain_ref, part_ref, w_ref, inv_ref):
    core, odd, first = places()
    for near in range(2):
        side = core if near == 0 else 1 - core
        for j in range(8):
            for b in range(5):
                for k in range(3):
                    w_ref[pl.ds(k * 256 + near * 128 + j * 16, 16), pl.ds(b * 128, 128)] = both_ref[
                        side, j, pl.ds(b * 48 + k * 16, 16), :
                    ]
    sums = jnp.sum(recv_ref[:, 240:256, :].astype(F32), axis=0)
    total = sums[0:2] + sums[2:4] + sums[4:6]
    diagonal = lax.broadcasted_iota(jnp.int32, (128, 128), 0) == lax.broadcasted_iota(jnp.int32, (128, 128), 1)
    columns = [
        jnp.sum(jnp.where(diagonal, total[i : i + 1], 0.0), axis=1, keepdims=True) for i in range(2)
    ]
    inverse = lax.rsqrt(jnp.concatenate(columns, axis=0) / FEATURES + 1e-06)
    inv_ref[...] = jnp.broadcast_to(inverse, (256, 128))
    gain = local_rows(gain_ref, first, odd)
    own_half = (lax.broadcasted_iota(jnp.int32, (256, 128), 1) >= 64) == (odd == 1)

    def widened(main_ref, half_ref):
        half = jnp.where(own_half, half_ref[...].astype(F32), 0.0)
        return jnp.concatenate([main_ref[...].astype(F32), half], axis=1)

    normed = (widened(x_ref, xh_ref) * inverse * gain).astype(BF16)
    grads = widened(g_ref, gh_ref).astype(BF16)
    part_ref[:, 0:512] = dot(normed, w_ref[0:512], CONTRACT_LAST).astype(BF16)
    part_ref[:, 512:768] = dot(grads, w_ref[512:768], CONTRACT_LAST).astype(BF16)


def activation_kernel(parts_ref, out_ref):
    total = parts_ref[0].astype(F32)
    for i in range(1, 8):
        total = total + parts_ref[i].astype(F32)
    gate_pre, up_proj, hidden_grad = total[:, 0:256], total[:, 256:512], total[:, 512:768]
    activated, slope = gelu_parts(gate_pre)
    hidden = (activated * up_proj).astype(BF16)
    gate_grad = (hidden_grad * up_proj * slope).astype(BF16)
    up_grad = (hidden_grad * activated).astype(BF16)
    products = gate_grad.astype(F32) * gate_pre + up_grad.astype(F32) * up_proj
    row_mean = jnp.sum(products, axis=1, keepdims=True) / FEATURES
    high, middle, low = pieces(jnp.broadcast_to(row_mean, (32, 128)))
    lane = lax.broadcasted_iota(jnp.int32, (32, 128), 1)
    tail = jnp.where(lane == 0, high.astype(F32), jnp.where(lane == 1, middle.astype(F32), low.astype(F32)))
    tail = jnp.where(lane < 3, tail, 0.0).astype(BF16)
    message = jnp.concatenate([gate_grad, up_grad, hidden, tail], axis=1)
    for i in range(8):
        out_ref[i] = message


def gradient_kernel(
    acts_ref, w_ref, x_ref, xh_ref, g_ref, gh_ref, inv_ref, gain_ref, sign_ref, table_ref, exps_ref, resid_ref, keep_ref, send_ref
):
    _, odd, first = places()
    gain = local_rows(gain_ref, first, odd)
    sign = (2 * local_rows(sign_ref, first, odd) - 1).astype(F32)
    inverse = inv_ref[:, 0:1]
    acts = acts_ref[...].reshape(256, 896)
    gate_grad, up_grad, hidden = acts[:, 0:256], acts[:, 256:512], acts[:, 512:768]
    row_mean = jnp.sum(acts[:, 768:896].astype(F32), axis=1, keepdims=True)
    unit = jnp.concatenate([x_ref[...], xh_ref[...]], axis=1).astype(F32) * inverse
    grads = jnp.concatenate([g_ref[...], gh_ref[...]], axis=1)
    normed = (unit * gain).astype(BF16)
    normed_grad = dot(gate_grad, w_ref[0:256]) + dot(up_grad, w_ref[256:512])
    resid = grads.astype(F32) + inverse * (normed_grad * gain - unit * row_mean)
    resid_ref[...] = resid.astype(BF16)
    table = table_ref[...]
    for k, (left, right) in enumerate(((gate_grad, normed), (up_grad, normed), (hidden, grads))):
        term = dot(left, right, CONTRACT_FIRST) * sign
        scale = jnp.left_shift(1, exps_ref[k]).astype(F32) * float(128.0**-0.5)
        for b in range(5):
            high, middle, low = pieces(term[:, b * 128 : (b + 1) * 128])
            rotated = (dot(low, table) + dot(middle, table)) + dot(high, table)
            values = jnp.clip(rotated * scale, -127.0, 127.0)
            for near, out_ref in enumerate((keep_ref, send_ref)):
                half = values[near * 128 : near * 128 + 128].reshape(8, 2, 8, 128)
                if b < 4:
                    out_ref[k * 8 + b] = half[:, 0].reshape(64, 128).astype(BF16)
                    out_ref[k * 8 + 4 + b] = half[:, 1].reshape(64, 128).astype(BF16)
                else:
                    chosen = jnp.where(odd == 1, half[:, 1], half[:, 0])
                    out_ref[24 + k] = chosen.reshape(64, 128).astype(BF16)
    for out_ref in (keep_ref, send_ref):
        for s in range(27, 32):
            out_ref[s] = jnp.zeros((64, 128), BF16)


def pair_kernel(keep_ref, other_ref, out_ref):
    out_ref[...] = (keep_ref[...].astype(F32) + other_ref[...].astype(F32)).astype(BF16)


def total_kernel(terms_ref, out_ref):
    total = terms_ref[0].astype(F32)
    for i in range(1, 32):
        total = total + terms_ref[i].astype(F32)
    rounded = total.astype(BF16)
    for i in range(32):
        out_ref[i] = rounded


def restore_kernel(share_ref, sign_ref, table_ref, exps_ref, out_ref):
    table = table_ref[...]
    for k in range(3):
        e = exps_ref[k]
        factor = jnp.where(e == 3, 2.0**-9, jnp.where(e == 4, 2.0**-10, jnp.where(e == 5, 2.0**-11, 2.0**-12)))
        factor = factor.astype(F32) * float(128.0**-0.5)
        for q in range(2):
            rows = pl.ds(16 * q, 16)

            def put(block, low_half, high_half):
                sign = (2 * sign_ref[block : block + 1, :] - 1).astype(F32) * factor
                both = jnp.concatenate([low_half, high_half], axis=0) * sign
                out_ref[k, rows, block * 128 : (block + 1) * 128] = both.astype(BF16)

            for b in range(4):
                halves = [dot(share_ref[q, k * 8 + 4 * i + b], table) for i in range(2)]
                for m in range(8):
                    put(
                        9 * (m // 2) + 5 * (m % 2) + b,
                        halves[0][m * 8 : m * 8 + 8],
                        halves[1][m * 8 : m * 8 + 8],
                    )
            shared = dot(share_ref[q, 24 + k], table)
            for p in range(4):
                put(9 * p + 4, shared[16 * p : 16 * p + 8], shared[16 * p + 8 : 16 * p + 16])


def call(kernel, outs, scalars=0):
    def run(*operands):
        count = len(operands)
        spaces = [pltpu.SMEM if i >= count - scalars else pltpu.VMEM for i in range(count)]
        return pl.pallas_call(
            kernel,
            out_shape=[jax.ShapeDtypeStruct(shape, dtype) for shape, dtype in outs],
            in_specs=[pl.BlockSpec(memory_space=space) for space in spaces],
            out_specs=[pl.BlockSpec(memory_space=pltpu.VMEM) for _ in outs],
            compiler_params=pltpu.CompilerParams(vmem_limit_bytes=VMEM_LIMIT),
            name=kernel.__name__,
        )(*operands)

    return run


def aligned(values, odd):
    return (
        jnp.where(odd == 1, values[:, 64:576], values[:, 0:512]),
        jnp.where(odd == 1, values[:, 0:64], values[:, 512:576]),
    )


def per_device(residual, out_grad, ffn_weights, norm_gain, exponents, sign_bits):
    core, odd, _ = places()
    x_main, x_half = aligned(residual, odd)
    g_main, g_half = aligned(out_grad, odd)
    swapped = lax.ppermute(
        jnp.concatenate([x_half, g_half], axis=1), "x", [(0, 1), (1, 0), (2, 3), (3, 2)]
    )

    def shared(own, other):
        return jnp.where(
            odd == 1, jnp.concatenate([other, own], axis=1), jnp.concatenate([own, other], axis=1)
        )

    x_shared = shared(x_half, swapped[:, 0:64])
    g_shared = shared(g_half, swapped[:, 64:128])

    wide = residual.astype(F32)
    squares = jnp.stack(pieces(jnp.sum(wide * wide, axis=1))).reshape(6, 128)
    squares = jnp.concatenate([squares, jnp.zeros((10, 128), BF16)], axis=0)
    mine = lax.dynamic_slice_in_dim(ffn_weights, core * 16, 16, 1).reshape(48, 36, 128)
    chunks = []
    for m in range(8):
        start = 9 * (m // 2)
        blocks = [start + 5 * (m % 2) + b for b in range(4)] + [start + 4]
        chunks.append(jnp.concatenate([mine[:, b] for b in blocks] + [squares], axis=0))
    received = lax.all_to_all(jnp.stack(chunks), MP, 0, 0)
    both = lax.all_gather(received, "c", axis=0)

    gain = norm_gain.reshape(36, 128)
    signs = sign_bits.reshape(36, 128)
    table = jnp.asarray(signed_hadamard(), BF16)
    parts, weights, inverse = call(
        forward_kernel, [((256, 768), BF16), ((768, 640), BF16), ((256, 128), F32)]
    )(received, both, x_main, x_shared, g_main, g_shared, gain)
    parts = lax.all_to_all(parts.reshape(8, 32, 768), MP, 0, 0)
    (message,) = call(activation_kernel, [((8, 32, 896), BF16)])(parts)
    acts = lax.all_to_all(message, MP, 0, 0)
    resid, keep, send = call(
        gradient_kernel,
        [((256, 640), BF16), ((32, 64, 128), BF16), ((32, 64, 128), BF16)],
        scalars=1,
    )(acts, weights, x_main, x_shared, g_main, g_shared, inverse, gain, signs, table, exponents)
    other = lax.ppermute(send, "c", [(0, 1), (1, 0)])
    (terms,) = call(pair_kernel, [((32, 64, 128), BF16)])(keep, other)
    terms = lax.all_to_all(terms, ("z", "yl"), 0, 0)
    (share,) = call(total_kernel, [((32, 64, 128), BF16)])(terms)
    gathered = lax.all_to_all(share.reshape(256, 8, 128), ("z", "yl", "yh", "x"), 0, 0)
    gathered = lax.all_gather(gathered, "c", axis=0).reshape(2, 32, 64, 128)
    (weight_grads,) = call(restore_kernel, [((3, 32, 4608), BF16)], scalars=1)(
        gathered, signs, table, exponents
    )
    resid_grad = jnp.where(
        odd == 1,
        jnp.concatenate([resid[:, 576:640], resid[:, 0:512]], axis=1),
        resid[:, 0:576],
    )
    return (resid_grad, weight_grads)


def solution(mesh):
    axes = ("z", "yl", "c", "yh", "x")
    fine = Mesh(mesh.devices.reshape(8, 4, 2, 2, 4), axes)
    rows = P(DP, MP)
    return jax.shard_map(
        per_device,
        mesh=fine,
        in_specs=(rows, rows, P(None, MP, None), P(), P(), P()),
        out_specs=(rows, P(None, MP, None)),
        check_vma=False,
    )
```

time: 518 us -> 192 us (0.37)
  blocking collectives: 256 us -> 91.5 us
  waiting for transfers between devices: 170 us -> 42 us
  starting transfers between devices: 39.7 us -> 21.3 us
  matrix products: 13.8 us -> 0 us
  Pallas kernels: 0 us -> 5.35 us
    unnamed x1 -> x0, blocking collectives: 178 us -> none
    all_gather x2, waiting for transfers between devices: 168 us -> 32.5 us  [the longest x1 22.4 us: per_device(): both = lax.all_gather(received, 'c', axis=0)]
    all_to_all x0 -> x4, blocking collectives: none -> 91.5 us  [the longest x1 30.4 us: per_device(): lax.all_to_all(share.reshape(256, 8, 128), ('z', 'yl', 'yh', 'x'), 0, 0)]
    all_gather x1 -> x0, blocking collectives: 78.4 us -> none  [per_device(): gathered = lax.all_gather(own_share, 'dp', axis=0, tiled=True)]
    unnamed x10 -> x0, starting transfers between devices: 39.6 us -> none
    dot_general x7 -> x0, matrix products: 13.8 us -> none  [the longest x1 3.32 us: restore(): jnp.einsum('kubj,jc->kubc', scaled, hadamard_table, precision=lax.Precisi...]
    ppermute x0 -> x2, starting transfers between devices: none -> 10.9 us  [the longest x1 7.56 us: per_device(): other = lax.ppermute(send, 'c', [(0, 1), (1, 0)])]
    all_to_all x0 -> x1, starting transfers between devices: none -> 10.2 us  [per_device(): received = lax.all_to_all(jnp.stack(chunks), MP, 0, 0)]
  transfers between devices with their start and end apart: 13 -> 5, of which waited for: 3 -> 4; matrix products, arithmetic and copies ran while one was open for 38% -> 1% of each run, Pallas kernels for 0% -> 0%
where the time goes in v1:
time: 192 us; the launch traced here: 191 us
  blocking collectives  91.5 us (48%)
  waiting for transfers between devices  42 us (22%)
  starting transfers between devices  21.3 us (11%)
  local copies, waits for them, and re-layouts  14.6 us (8%)
  between operations  14.5 us (8%)
  Pallas kernels  5.35 us (3%)
    all_to_all x1, blocking collectives, per_device(): lax.all_to_all(share.reshape(256, 8, 128), ('z', 'yl', 'yh', 'x'), 0, 0)  30.4 us
    all_to_all x1, blocking collectives, per_device(): terms = lax.all_to_all(terms, ('z', 'yl'), 0, 0)  26.3 us
    all_gather x1, waiting for transfers between devices, per_device(): both = lax.all_gather(received, 'c', axis=0)  22.4 us
    all_to_all x1, blocking collectives, per_device(): parts = lax.all_to_all(parts.reshape(8, 32, 768), MP, 0, 0)  19.7 us
    all_to_all x1, blocking collectives, per_device(): acts = lax.all_to_all(message, MP, 0, 0)  15.2 us
    unnamed x40, local copies, waits for them, and re-layouts  11 us
    all_to_all x1, starting transfers between devices, per_device(): received = lax.all_to_all(jnp.stack(chunks), MP, 0, 0)  10.2 us
    all_gather x1, waiting for transfers between devices, per_device(): gathered = lax.all_gather(gathered, 'c', axis=0).reshape(2, 32, 64, 128)  10.1 us
  transfers between devices with their start and end apart: 5, of which 4 were waited for; matrix products, arithmetic and copies ran while one was open for 1% of the time, Pallas kernels for 0%

profile of v1, /device:TPU:1, one launch (start us, length us, event | category | flops | bytes accessed | tf_op | source)
XLA Modules:
  0.0 190.9 jit_solution(5233313211355377630)
XLA Ops:
  7.2 1.1 multiply_reduce_fusion
  8.5 0.2 reshape.58
  8.7 0.3 fusion.2
  9.0 0.4 fusion.1
  9.7 0.6 bitcast_dynamic-update-slice_fusion.7
  10.8 0.6 bitcast_dynamic-update-slice_fusion.6
  11.6 0.6 bitcast_dynamic-update-slice_fusion.5
  12.4 0.6 bitcast_dynamic-update-slice_fusion.4
  13.3 0.6 bitcast_dynamic-update-slice_fusion.3
  14.1 0.6 bitcast_dynamic-update-slice_fusion.2
  14.9 0.6 bitcast_dynamic-update-slice_fusion.1
  15.8 0.6 bitcast_dynamic-update-slice_fusion
  16.4 10.2 %all-to-all-start = ((bf16[8,256,128]{2,1,0:T(8,128)(2,1)}), bf16[8,256,128]{2,1,0:T(8,128)(2,1)S(1)}, u32[]{:S(2)}, u32[]{:S(2)}) async-start(bf16[8,256,128]{2,1,0:T(8,128)(2,1)} %bitcast_dynamic-update-slice_fusion), calls=%async_computation | async-start | bytes 1048576 | tf_op jit(solution)/shard_map/all_to_all | solution.py:238
  27.0 0.6 copy-done.9
  28.0 3.4 %collective-permute-start = (bf16[256,128]{1,0:T(8,128)(2,1)S(1)}, bf16[256,128]{1,0:T(8,128)(2,1)S(1)}, u32[]{:S(2)}, u32[]{:S(2)}) collective-permute-start(bf16[256,128]{1,0:T(8,128)(2,1)S(1)} %pad_maximum_fusion), channel_id=1, source_target_pairs={{0,1},{1,0},{2,3},{3,2},{4,5},{5,4},{6,7},{7,6},{8,9},{9,8},{10,11... | collective-permute-start | bytes 196616 | tf_op jit(solution)/shard_map/ppermute | solution.py:217
  31.4 8.0 %all-to-all-done.recv_ref = bf16[8,256,128]{2,1,0:T(8,128)(2,1)S(1)} async-done(((bf16[8,256,128]{2,1,0:T(8,128)(2,1)}), bf16[8,256,128]{2,1,0:T(8,128)(2,1)S(1)}, u32[]{:S(2)}, u32[]{:S(2)}) %all-to-all-start) | async-done | bytes 524320 | tf_op jit(solution)/shard_map/all_to_all | solution.py:238
  39.3 0.8 copy-done.1
  41.2 22.4 %all-gather.5.cloned.1.call-done = bf16[16,256,128]{2,1,0:T(8,128)(2,1)} async-done(((bf16[8,256,128]{2,1,0:T(8,128)(2,1)}), bf16[16,256,128]{2,1,0:T(8,128)(2,1)}) %all-gather.5.cloned.1.call-update) | async-done | bytes 1048592 | tf_op jit(solution)/shard_map/all_gather | solution.py:239
  63.7 1.2 copy-done.3
  64.9 0.8 forward_kernel.1
  65.6 19.7 %all_to_all.25.parts_ref = bf16[8,32,768]{2,1,0:T(8,128)(2,1)S(1)} all-to-all(bf16[8,32,768]{2,1,0:T(8,128)(2,1)S(1)} %bitcast.100), channel_id=1, replica_groups=mesh['z'=8,'yl'=4,'c'=2,'yh'=2,'x'=4] {'yh','x'}, dimensions={0} | all-to-all | bytes 786432 | tf_op jit(solution)/shard_map/all_to_all | solution.py:247
  85.5 15.2 %all_to_all.26.acts_ref = bf16[8,32,896]{2,1,0:T(8,128)(2,1)S(1)} all-to-all(bf16[8,32,896]{2,1,0:T(8,128)(2,1)S(1)} %activation_kernel.1), channel_id=1, replica_groups=mesh['z'=8,'yl'=4,'c'=2,'yh'=2,'x'=4] {'yh','x'}, dimensions={0} | all-to-all | bytes 917504 | tf_op jit(solution)/shard_map/all_to_all | solution.py:249
  100.7 0.6 copy-done.8
  101.3 2.1 %gradient_kernel.1 = (bf16[256,640]{1,0:T(8,128)(2,1)S(1)}, bf16[32,64,128]{2,1,0:T(8,128)(2,1)S(1)}, bf16[32,64,128]{2,1,0:T(8,128)(2,1)S(1)}) custom-call(bf16[8,32,896]{2,1,0:T(8,128)(2,1)S(1)} %all_to_all.26.acts_ref, bf16[768,640]{1,0:T(8,128)(2,1)S(1)} %get-tuple-element.9.w_ref, bf16[256,512]{1,0:T(8,128)(2,1)S(1)} %get-tuple-element.103.x_ref, ...), custom_call_target="tpu_custom_call" | custom-call | tf_op jit(solution)/shard_map/gradient_kernel/pallas_call | solution.py:194
  103.5 7.6 %collective-permute-start.1 = (bf16[32,64,128]{2,1,0:T(8,128)(2,1)S(1)}, bf16[32,64,128]{2,1,0:T(8,128)(2,1)S(1)}, u32[]{:S(2)}, u32[]{:S(2)}) collective-permute-start(bf16[32,64,128]{2,1,0:T(8,128)(2,1)S(1)} %get-tuple-element.13), channel_id=1, source_target_pairs={{0,8},{8,0},{1,9},{9,1},{2,10},{10,2},{3,11},{11,3},{4,12},{12,4},... | collective-permute-start | bytes 1572872 | tf_op jit(solution)/shard_map/ppermute | solution.py:255
  111.0 1.5 collective-permute-done.1.other_ref
  112.7 26.3 %all_to_all.27.terms_ref = bf16[32,64,128]{2,1,0:T(8,128)(2,1)S(1)} all-to-all(bf16[32,64,128]{2,1,0:T(8,128)(2,1)S(1)} %pair_kernel.1), channel_id=1, replica_groups=mesh['z'=8,'yl'=4,'c'=2,'yh'=2,'x'=4] {'z','yl'}, dimensions={0} | all-to-all | bytes 1048576 | tf_op jit(solution)/shard_map/all_to_all | solution.py:257
  139.1 30.4 %all_to_all.28 = bf16[256,8,128]{2,1,0:T(8,128)(2,1)} all-to-all(bf16[256,8,128]{2,1,0:T(8,128)(2,1)S(1)} %bitcast.97), channel_id=1, replica_groups=mesh['z'=8,'yl'=4,'c'=2,'yh'=2,'x'=4] {'z','yl','yh','x'}, dimensions={0} | all-to-all | bytes 1048576 | tf_op jit(solution)/shard_map/all_to_all | solution.py:259
  169.8 0.9 copy.107
  170.7 10.1 %all-gather.7.cloned.1.call-done = bf16[512,8,128]{2,1,0:T(8,128)(2,1)} async-done(((bf16[256,8,128]{2,1,0:T(8,128)(2,1)}), bf16[512,8,128]{2,1,0:T(8,128)(2,1)}) %all-gather.7.cloned.1.call-update) | async-done | bytes 1048592 | tf_op jit(solution)/shard_map/all_gather | solution.py:260
  180.8 1.2 copy-done.4
  182.0 2.1 %restore_kernel.1 = bf16[3,32,4608]{2,1,0:T(8,128)(2,1)} custom-call(bf16[2,32,64,128]{3,2,1,0:T(8,128)(2,1)S(1)} %bitcast.99, s32[36,128]{1,0:T(8,128)S(1)} %bitcast.104, bf16[128,128]{1,0:T(8,128)(2,1)S(1)} %copy-done.5, s32[3]{0:T(128)S(1)} %copy-done.8), custom_call_target="tpu_custom_call" | custom-call | tf_op jit(solution)/shard_map/restore_kernel/pallas_call | solution.py:194
  (79 shorter events, 4.1 us)
Async XLA Ops:
  7.2 1.3 copy-start
  16.4 10.3 %copy-start.10 = (bf16[256,576]{0,1:T(8,128)(2,1)S(1)}, bf16[256,576]{0,1:T(8,128)(2,1)}, u32[]{:S(2)}) copy-start(bf16[256,576]{0,1:T(8,128)(2,1)} %param.8) | copy-start | bytes 884740
  16.4 22.9 %all-to-all-start = ((bf16[8,256,128]{2,1,0:T(8,128)(2,1)}), bf16[8,256,128]{2,1,0:T(8,128)(2,1)S(1)}, u32[]{:S(2)}, u32[]{:S(2)}) async-start(bf16[8,256,128]{2,1,0:T(8,128)(2,1)} %bitcast_dynamic-update-slice_fusion), calls=%async_computation | async-start | bytes 1048576 | tf_op jit(solution)/shard_map/all_to_all | solution.py:238
  26.7 1.0 copy-start.9
  26.7 37.0 %all-gather.5.cloned.1.call-start = ((), (), s32[]{:S(2)}) async-start(), calls=%async_computation.5 | async-start | bytes 1572864 | tf_op jit(solution)/shard_map/all_gather | solution.py:239
  28.0 13.0 %collective-permute-start = (bf16[256,128]{1,0:T(8,128)(2,1)S(1)}, bf16[256,128]{1,0:T(8,128)(2,1)S(1)}, u32[]{:S(2)}, u32[]{:S(2)}) collective-permute-start(bf16[256,128]{1,0:T(8,128)(2,1)S(1)} %pad_maximum_fusion), channel_id=1, source_target_pairs={{0,1},{1,0},{2,3},{3,2},{4,5},{5,4},{6,7},{7,6},{8,9},{9,8},{10,11... | collective-permute-start | bytes 196616 | tf_op jit(solution)/shard_map/ppermute | solution.py:217
  39.3 0.8 copy-start.1
  40.2 140.6 %all-gather.7.cloned.1.call-start = ((), (), s32[]{:S(2)}) async-start(), calls=%async_computation.6 | async-start | bytes 1572864 | tf_op jit(solution)/shard_map/all_gather | solution.py:260
  41.0 22.7 %copy-start.2 = (bf16[8,256,128]{2,1,0:T(8,128)(2,1)S(1)}, bf16[8,256,128]{2,1,0:T(8,128)(2,1)}, u32[]{:S(2)}) copy-start(bf16[8,256,128]{2,1,0:T(8,128)(2,1)} %copy-done.1) | copy-start | bytes 1572868
  41.1 22.6 %copy-start.6 = (f32[4608]{0:T(1024)S(1)}, f32[4608]{0:T(1024)}, u32[]{:S(2)}) copy-start(f32[4608]{0:T(1024)} %param.10) | copy-start | bytes 55300
  63.7 1.2 copy-start.3
  85.5 15.2 %copy-start.5 = (bf16[128,128]{1,0:T(8,128)(2,1)S(1)}, bf16[128,128]{1,0:T(8,128)(2,1)}, u32[]{:S(2)}) copy-start(bf16[128,128]{1,0:T(8,128)(2,1)} %constant.34.clone.table_ref) | copy-start | bytes 98308
  85.5 15.2 %copy-start.7 = (s32[4608]{0:T(1024)S(1)}, s32[4608]{0:T(1024)}, u32[]{:S(2)}) copy-start(s32[4608]{0:T(1024)} %param.12) | copy-start | bytes 55300
  100.7 0.7 copy-start.8
  103.5 9.1 %collective-permute-start.1 = (bf16[32,64,128]{2,1,0:T(8,128)(2,1)S(1)}, bf16[32,64,128]{2,1,0:T(8,128)(2,1)S(1)}, u32[]{:S(2)}, u32[]{:S(2)}) collective-permute-start(bf16[32,64,128]{2,1,0:T(8,128)(2,1)S(1)} %get-tuple-element.13), channel_id=1, source_target_pairs={{0,8},{8,0},{1,9},{9,1},{2,10},{10,2},{3,11},{11,3},{4,12},{12,4},... | collective-permute-start | bytes 1572872 | tf_op jit(solution)/shard_map/ppermute | solution.py:255
  180.8 1.2 copy-start.4
Sparse Core Ops, SparseCore 0:
  40.3 23.3 all-gather.4
  169.6 11.0 all-gather.6

commit v2 on v1

v2 whole, which is shorter than its diff:
```python
import functools

import jax
import jax.numpy as jnp
import numpy as np
from jax import lax
from jax.experimental import pallas as pl
from jax.experimental.pallas import tpu as pltpu
from jax.sharding import Mesh
from jax.sharding import PartitionSpec as P

F32 = jnp.float32
BF16 = jnp.bfloat16
DP = ("z", "yl", "c")
MP = ("yh", "x")
VMEM_LIMIT = 40 * 1024 * 1024
FEATURES = 4608
CONTRACT_LAST = (((1,), (1,)), ((), ()))
CONTRACT_FIRST = (((0,), (0,)), ((), ()))


def signed_hadamard():
    table = np.array([[1.0]], np.float32)
    for _ in range(7):
        table = np.block([[table, table], [table, -table]])
    return table


def gelu_parts(values):
    tanh_input = 0.7978845608 * (values + 0.044715 * values * values * values)
    tanhed = jnp.tanh(tanh_input)
    forward = 0.5 * values * (1.0 + tanhed)
    gelu_slope = 0.5 * (1.0 + tanhed) + 0.5 * values * (1.0 - tanhed * tanhed) * 0.7978845608 * (
        1.0 + 3.0 * 0.044715 * values * values
    )
    return (forward, gelu_slope)


def pieces(values):
    high = values.astype(BF16)
    rest = values - high.astype(F32)
    middle = rest.astype(BF16)
    low = (rest - middle.astype(F32)).astype(BF16)
    return (high, middle, low)


def dot(left, right, dims=(((1,), (0,)), ((), ()))):
    return lax.dot_general(left, right, dims, preferred_element_type=F32)


def places():
    odd = lax.axis_index("x") % 2
    pair = lax.axis_index("yh") * 2 + lax.axis_index("x") // 2
    return (lax.axis_index("c"), odd, pair * 9)


def local_rows(table_ref, first, odd):
    rows = [table_ref[pl.ds(first + 5 * odd + b, 1), :] for b in range(4)]
    return jnp.concatenate(rows + [table_ref[pl.ds(first + 4, 1), :]], axis=1)


def prepare_kernel(x_ref, g_ref, w_ref, send_ref, half_ref):
    core, odd, _ = places()
    rows = pl.ds(pl.multiple_of(core * 16, 16), 16)
    for m in range(8):
        start = 9 * (m // 2)
        for b, block in enumerate([start + 5 * (m % 2) + b for b in range(4)] + [start + 4]):
            for k in range(3):
                send_ref[m, pl.ds(b * 48 + k * 16, 16), :] = w_ref[k, rows, block * 128 : (block + 1) * 128]
    halves = [
        jnp.where(odd == 1, ref[:, 0:64].astype(F32), ref[:, 512:576].astype(F32)) for ref in (x_ref, g_ref)
    ]
    half_ref[...] = jnp.concatenate(halves, axis=1).astype(BF16)


def aligned(ref, odd):
    values = ref[...].astype(F32)
    zeros = jnp.zeros((256, 64), F32)
    return jnp.where(
        odd == 1,
        jnp.concatenate([values[:, 64:576], zeros, values[:, 0:64]], axis=1),
        jnp.concatenate([values, zeros], axis=1),
    )


def forward_kernel(recv_ref, x_ref, g_ref, far_x_ref, far_g_ref, gain_ref, part_ref, w_ref, xa_ref, ga_ref):
    _, odd, first = places()
    for j in range(8):
        for b in range(5):
            for k in range(3):
                w_ref[k * 128 + j * 16 : k * 128 + j * 16 + 16, b * 128 : (b + 1) * 128] = recv_ref[
                    j, b * 48 + k * 16 : b * 48 + k * 16 + 16, :
                ]
    wide = jnp.concatenate([aligned(x_ref, odd), aligned(far_x_ref, odd)], axis=0)
    grads = jnp.concatenate([aligned(g_ref, odd), aligned(far_g_ref, odd)], axis=0).astype(BF16)
    xa_ref[...] = wide.astype(BF16)
    ga_ref[...] = grads
    gained = wide * local_rows(gain_ref, first, odd)
    high = gained.astype(BF16)
    low = (gained - high.astype(F32)).astype(BF16)
    pair = w_ref[0:256]
    gate_up = (dot(low, pair, CONTRACT_LAST) + dot(high, pair, CONTRACT_LAST)).astype(BF16)
    down = dot(grads, w_ref[256:384], CONTRACT_LAST).astype(BF16)
    squares = wide * wide
    ones = jnp.ones((8, 640), BF16)
    square_high = squares.astype(BF16)
    square_low = (squares - square_high.astype(F32)).astype(BF16)
    sums = dot(ones, square_low, CONTRACT_LAST) + dot(ones, square_high, CONTRACT_LAST)
    row = lax.broadcasted_iota(jnp.int32, (8, 256), 0)
    tail = jnp.zeros((8, 256), F32)
    for i, piece in enumerate(pieces(sums)):
        for side in range(2):
            tail = jnp.where(row == 2 * i + side, piece[:, side * 256 : side * 256 + 256].astype(F32), tail)
    tail = jnp.concatenate([tail, jnp.zeros((8, 128), F32)], axis=1)
    for i in range(8):
        near, far = slice(32 * i, 32 * i + 32), slice(256 + 32 * i, 256 + 32 * i + 32)
        part_ref[i, 0:32, 0:256] = gate_up[near]
        part_ref[i, 0:32, 256:384] = down[near]
        part_ref[i, 32:64, 0:256] = gate_up[far]
        part_ref[i, 32:64, 256:384] = down[far]
        part_ref[i, 64:72, :] = tail.astype(BF16)


def activation_kernel(parts_ref, out_ref, inv_ref):
    total = parts_ref[0].astype(F32)
    for i in range(1, 8):
        total = total + parts_ref[i].astype(F32)
    sums = total[64:72, 0:256]
    inverse_rows = lax.rsqrt((sums[0:2] + sums[2:4] + sums[4:6]) / FEATURES + 1e-06)
    inv_ref[0:2, :] = inverse_rows
    inv_ref[2:8, :] = jnp.zeros((6, 256), F32)
    mine = 32 * (lax.axis_index("yh") * 4 + lax.axis_index("x"))
    place = lax.broadcasted_iota(jnp.int32, (32, 256), 1) == lax.broadcasted_iota(jnp.int32, (32, 256), 0) + mine
    columns = [
        jnp.sum(jnp.where(place, inverse_rows[i : i + 1], 0.0), axis=1, keepdims=True) for i in range(2)
    ]
    inverse = jnp.concatenate(columns, axis=0)
    gate_pre, up_proj, hidden_grad = (
        total[0:64, 0:128] * inverse,
        total[0:64, 128:256] * inverse,
        total[0:64, 256:384],
    )
    activated, slope = gelu_parts(gate_pre)
    hidden = (activated * up_proj).astype(BF16)
    gate_grad = (hidden_grad * up_proj * slope).astype(BF16)
    up_grad = (hidden_grad * activated).astype(BF16)
    products = gate_grad.astype(F32) * gate_pre + up_grad.astype(F32) * up_proj
    row_mean = jnp.sum(products, axis=1, keepdims=True) / FEATURES
    diagonal = lax.broadcasted_iota(jnp.int32, (64, 128), 0) == lax.broadcasted_iota(jnp.int32, (64, 128), 1)
    mean_row = jnp.sum(jnp.where(diagonal, row_mean, 0.0), axis=0, keepdims=True)
    row = lax.broadcasted_iota(jnp.int32, (8, 128), 0)
    tail = jnp.zeros((8, 128), F32)
    for i, piece in enumerate(pieces(mean_row)):
        tail = jnp.where(row == i, piece.astype(F32), tail)
    tail = jnp.concatenate([tail, jnp.zeros((8, 256), F32)], axis=1).astype(BF16)
    acts = jnp.concatenate([gate_grad, up_grad, hidden], axis=1)
    for i in range(8):
        out_ref[i, 0:64, :] = acts
        out_ref[i, 64:72, :] = tail


def gradient_kernel(
    acts_ref, w_ref, xa_ref, ga_ref, near_half_ref, far_half_ref, inv_ref, gain_ref, sign_ref, table_ref, exps_ref,
    term_ref, near_ref, far_ref,
):
    _, odd, first = places()
    gain = local_rows(gain_ref, first, odd)
    sign = (2 * local_rows(sign_ref, first, odd) - 1).astype(F32)
    table = table_ref[...]
    lane = lax.broadcasted_iota(jnp.int32, (256, 128), 1)
    theirs = (lane >= 64) == (odd == 0)
    square = lax.broadcasted_iota(jnp.int32, (256, 256), 0) == lax.broadcasted_iota(jnp.int32, (256, 256), 1)
    diagonal = lax.broadcasted_iota(jnp.int32, (64, 128), 0) == lax.broadcasted_iota(jnp.int32, (64, 128), 1)
    means = []
    for i in range(8):
        tail = acts_ref[i, 64:72, 0:128].astype(F32)
        mean_row = tail[0:1] + tail[1:2] + tail[2:3]
        means.append(jnp.sum(jnp.where(diagonal, mean_row, 0.0), axis=1, keepdims=True))
    sides = []
    for side, half_ref in enumerate((near_half_ref, far_half_ref)):
        tokens = slice(side * 256, side * 256 + 256)
        inverse = jnp.sum(jnp.where(square, inv_ref[side : side + 1, :], 0.0), axis=1, keepdims=True)
        row_mean = jnp.concatenate([mean[side * 32 : side * 32 + 32] for mean in means], axis=0)
        acts = jnp.concatenate([acts_ref[i, side * 32 : side * 32 + 32, :] for i in range(8)], axis=0)
        halves = half_ref[...].astype(F32)
        turned = pltpu.roll(halves, 64, 1)
        x_half = jnp.where(theirs, jnp.where(odd == 1, halves, turned), xa_ref[tokens, 512:640].astype(F32))
        g_half = jnp.where(theirs, jnp.where(odd == 1, turned, halves), ga_ref[tokens, 512:640].astype(F32))
        unit = jnp.concatenate([xa_ref[tokens, 0:512].astype(F32), x_half], axis=1) * inverse
        grads = jnp.concatenate([ga_ref[tokens, 0:512], g_half.astype(BF16)], axis=1)
        normed = (unit * gain).astype(BF16)
        gate_grad, up_grad, hidden = acts[:, 0:128], acts[:, 128:256], acts[:, 256:384]
        normed_grad = dot(acts[:, 0:256], w_ref[0:256])
        resid = inverse * (normed_grad * gain - unit * row_mean)
        if side == 0:
            near_ref[...] = resid
        else:
            far_ref[...] = resid.astype(BF16)
        sides.append(((gate_grad, normed), (up_grad, normed), (hidden, grads)))
    for k in range(3):
        scale = jnp.left_shift(1, exps_ref[k]).astype(F32) * float(128.0**-0.5)
        terms = [dot(*sides[side][k], CONTRACT_FIRST) * sign for side in range(2)]
        for b in range(5):
            total = None
            for term in terms:
                high, middle, low = pieces(term[:, b * 128 : (b + 1) * 128])
                rotated = (dot(low, table) + dot(middle, table)) + dot(high, table)
                quantized = jnp.clip(rotated * scale, -127.0, 127.0).astype(BF16).astype(F32)
                total = quantized if total is None else total + quantized
            half = total.reshape(8, 2, 8, 128)
            if b < 4:
                term_ref[k * 8 + b] = half[:, 0].reshape(64, 128).astype(BF16)
                term_ref[k * 8 + 4 + b] = half[:, 1].reshape(64, 128).astype(BF16)
            else:
                chosen = jnp.where(odd == 1, half[:, 1], half[:, 0])
                term_ref[24 + k] = chosen.reshape(64, 128).astype(BF16)
    for s in range(27, 32):
        term_ref[s] = jnp.zeros((64, 128), BF16)


def resid_kernel(g_ref, near_ref, far_ref, out_ref):
    _, odd, _ = places()
    total = near_ref[...] + far_ref[...].astype(F32)
    own = jnp.where(
        odd == 1, jnp.concatenate([total[:, 576:640], total[:, 0:512]], axis=1), total[:, 0:576]
    )
    out_ref[...] = (g_ref[...].astype(F32) + own).astype(BF16)


def total_kernel(terms_ref, out_ref):
    total = terms_ref[0].astype(F32)
    for i in range(1, 32):
        total = total + terms_ref[i].astype(F32)
    rounded = total.astype(BF16)
    for i in range(32):
        out_ref[i] = rounded


def restore_kernel(near_ref, far_ref, sign_ref, table_ref, exps_ref, out_ref):
    table = table_ref[...]
    core, _, _ = places()
    for k in range(3):
        e = exps_ref[k]
        factor = jnp.where(e == 3, 2.0**-9, jnp.where(e == 4, 2.0**-10, jnp.where(e == 5, 2.0**-11, 2.0**-12)))
        factor = factor.astype(F32) * float(128.0**-0.5)
        for q, share_ref in ((core, near_ref), (1 - core, far_ref)):
            rows = pl.ds(pl.multiple_of(16 * q, 16), 16)

            def put(block, low_half, high_half):
                sign = (2 * sign_ref[block : block + 1, :] - 1).astype(F32) * factor
                both = jnp.concatenate([low_half, high_half], axis=0) * sign
                out_ref[k, rows, block * 128 : (block + 1) * 128] = both.astype(BF16)

            for b in range(4):
                halves = [dot(share_ref[k * 8 + 4 * i + b], table) for i in range(2)]
                for m in range(8):
                    put(
                        9 * (m // 2) + 5 * (m % 2) + b,
                        halves[0][m * 8 : m * 8 + 8],
                        halves[1][m * 8 : m * 8 + 8],
                    )
            shared = dot(share_ref[24 + k], table)
            for p in range(4):
                put(9 * p + 4, shared[16 * p : 16 * p + 8], shared[16 * p + 8 : 16 * p + 16])


def call(kernel, outs, scalars=0):
    def run(*operands):
        count = len(operands)
        spaces = [pltpu.SMEM if i >= count - scalars else pltpu.VMEM for i in range(count)]
        return pl.pallas_call(
            kernel,
            out_shape=[jax.ShapeDtypeStruct(shape, dtype) for shape, dtype in outs],
            in_specs=[pl.BlockSpec(memory_space=space) for space in spaces],
            out_specs=[pl.BlockSpec(memory_space=pltpu.VMEM) for _ in outs],
            compiler_params=pltpu.CompilerParams(vmem_limit_bytes=VMEM_LIMIT),
            name=kernel.__name__,
        )(*operands)

    return run


def per_device(residual, out_grad, ffn_weights, norm_gain, exponents, sign_bits):
    gain = norm_gain.reshape(36, 128)
    signs = sign_bits.reshape(36, 128)
    table = jnp.asarray(signed_hadamard(), BF16)
    cores = [(0, 1), (1, 0)]

    send, half = call(prepare_kernel, [((8, 240, 128), BF16), ((256, 128), BF16)])(residual, out_grad, ffn_weights)
    received = lax.all_to_all(send, MP, 0, 0)
    near_x, near_g, half = lax.optimization_barrier((residual, out_grad, half))
    far_x = lax.ppermute(near_x, "c", cores)
    far_g = lax.ppermute(near_g, "c", cores)
    near_half = lax.ppermute(half, "x", [(0, 1), (1, 0), (2, 3), (3, 2)])
    far_half = lax.ppermute(near_half, "c", cores)

    parts, weights, x_aligned, g_aligned = call(
        forward_kernel,
        [((8, 72, 384), BF16), ((384, 640), BF16), ((512, 640), BF16), ((512, 640), BF16)],
    )(received, residual, out_grad, far_x, far_g, gain)
    parts = lax.all_to_all(parts, MP, 0, 0)
    message, inverse = call(activation_kernel, [((8, 72, 384), BF16), ((8, 256), F32)])(parts)
    acts = lax.all_to_all(message, MP, 0, 0)
    terms, near_resid, far_resid = call(
        gradient_kernel,
        [((32, 64, 128), BF16), ((256, 640), F32), ((256, 640), BF16)],
        scalars=1,
    )(acts, weights, x_aligned, g_aligned, near_half, far_half, inverse, gain, signs, table, exponents)
    terms = lax.all_to_all(terms, ("z", "yl"), 0, 0)
    far_resid = lax.ppermute(far_resid, "c", cores)
    (resid_grad,) = call(resid_kernel, [((256, 576), BF16)])(out_grad, near_resid, far_resid)
    (share,) = call(total_kernel, [((32, 64, 128), BF16)])(terms)
    share = lax.all_to_all(share.reshape(256, 8, 128), ("z", "yl", "yh", "x"), 0, 0).reshape(32, 64, 128)
    other = lax.ppermute(share, "c", cores)
    (weight_grads,) = call(restore_kernel, [((3, 32, 4608), BF16)], scalars=1)(
        share, other, signs, table, exponents
    )
    return (resid_grad, weight_grads)


def solution(mesh):
    axes = ("z", "yl", "c", "yh", "x")
    fine = Mesh(mesh.devices.reshape(8, 4, 2, 2, 4), axes)
    rows = P(DP, MP)
    return jax.shard_map(
        per_device,
        mesh=fine,
        in_specs=(rows, rows, P(None, MP, None), P(), P(), P()),
        out_specs=(rows, P(None, MP, None)),
        check_vma=False,
    )
```

time: 192 us -> 145 us (0.76)
  waiting for transfers between devices: 42 us -> 10.6 us
  starting transfers between devices: 21.3 us -> 38.3 us
  between operations: 14.5 us -> 0.79 us
  blocking collectives: 91.5 us -> 81.4 us
  local copies, waits for them, and re-layouts: 14.6 us -> 5.11 us
  Pallas kernels: 5.35 us -> 8.39 us
    all_gather x2 -> x0, waiting for transfers between devices: 32.5 us -> none  [the longest x1 22.4 us: per_device(): both = lax.all_gather(received, 'c', axis=0)]
    all_to_all x2 -> x1, blocking collectives: 34.8 us -> 15.4 us  [per_device(): parts = lax.all_to_all(parts, MP, 0, 0)]
    ppermute x2 -> x6, starting transfers between devices: 10.9 us -> 24.5 us  [the longest x1 8.7 us: per_device(): far_half = lax.ppermute(near_half, 'c', cores)]
    all_to_all x1, blocking collectives: 26.3 us -> 33.2 us  [per_device(): terms = lax.all_to_all(terms, ('z', 'yl'), 0, 0)]
    unnamed x40 -> x21, local copies, waits for them, and re-layouts: 11 us -> 4.7 us
    ppermute x2 -> x6, waiting for transfers between devices: 1.52 us -> 5.81 us  [the longest x1 1.75 us: per_device(): near_half = lax.ppermute(half, 'x', [(0, 1), (1, 0), (2, 3), (3, 2)])]
    all_to_all x1 -> x2, starting transfers between devices: 10.2 us -> 13.8 us  [the longest x1 10.2 us: per_device(): received = lax.all_to_all(send, MP, 0, 0)]
    all_to_all x1 -> x2, waiting for transfers between devices: 7.96 us -> 4.79 us  [the longest x1 4.79 us: per_device(): received = lax.all_to_all(send, MP, 0, 0)]
  transfers between devices with their start and end apart: 5 -> 8, of which waited for: 4 -> 5; matrix products, arithmetic and copies ran while one was open for 1% -> 1% of each run, Pallas kernels for 0% -> 0%
where the time goes in v2:
time: 145 us
  blocking collectives  81.4 us (56%)
  starting transfers between devices  38.3 us (26%)
  waiting for transfers between devices  10.6 us (7%)
  Pallas kernels  8.39 us (6%)
  local copies, waits for them, and re-layouts  5.11 us (4%)
    all_to_all x1, blocking collectives, per_device(): terms = lax.all_to_all(terms, ('z', 'yl'), 0, 0)  33.2 us
    all_to_all x1, blocking collectives, per_device(): lax.all_to_all(share.reshape(256, 8, 128), ('z', 'yl', 'yh', 'x'), 0, 0)  32.7 us
    all_to_all x1, blocking collectives, per_device(): parts = lax.all_to_all(parts, MP, 0, 0)  15.4 us
    all_to_all x1, starting transfers between devices, per_device(): received = lax.all_to_all(send, MP, 0, 0)  10.2 us
    ppermute x1, starting transfers between devices, per_device(): far_half = lax.ppermute(near_half, 'c', cores)  8.7 us
    pallas_call x7, Pallas kernels, run(): pl.pallas_call(kernel, out_shape=[jax.ShapeDtypeStruct(shape, dtype) for...  8.39 us
    ppermute x1, starting transfers between devices, per_device(): other = lax.ppermute(share, 'c', cores)  5.79 us
    all_to_all x1, waiting for transfers between devices, per_device(): received = lax.all_to_all(send, MP, 0, 0)  4.79 us
  transfers between devices with their start and end apart: 8, of which 5 were waited for; matrix products, arithmetic and copies ran while one was open for 1% of the time, Pallas kernels for 0%

profile of v2, /device:TPU:1, one launch (start us, length us, event | category | flops | bytes accessed | tf_op | source)
XLA Modules:
  0.0 144.6 jit_solution(3684445317363228614)
XLA Ops:
  0.6 1.3 copy.15.g_ref
  1.9 0.2 copy.9.x_ref
  2.1 0.9 prepare_kernel.1
  3.0 10.2 %all-to-all-start = ((bf16[8,240,128]{2,1,0:T(8,128)(2,1)}), bf16[8,240,128]{2,1,0:T(8,128)(2,1)S(1)}, u32[]{:S(2)}, u32[]{:S(2)}) async-start(bf16[8,240,128]{2,1,0:T(8,128)(2,1)} %get-tuple-element.16), calls=%async_computation | async-start | bytes 983040 | tf_op jit(solution)/shard_map/all_to_all | solution.py:290
  13.3 0.2 copy.12
  13.5 0.0 copy-start.4
  13.5 2.9 %collective-permute-start.1 = (bf16[256,576]{1,0:T(8,128)(2,1)S(1)}, bf16[256,576]{1,0:T(8,128)(2,1)S(1)}, u32[]{:S(2)}, u32[]{:S(2)}) collective-permute-start(bf16[256,576]{1,0:T(8,128)(2,1)S(1)} %copy.12), channel_id=1, source_target_pairs={{0,8},{8,0},{1,9},{9,1},{2,10},{10,2},{3,11},{11,3},{4,12},{12,4},... | collective-permute-start | bytes 884744 | tf_op jit(solution)/shard_map/ppermute | solution.py:293
  16.4 0.2 copy.11
  16.6 1.9 %collective-permute-start = (bf16[256,576]{1,0:T(8,128)(2,1)S(1)}, bf16[256,576]{1,0:T(8,128)(2,1)S(1)}, u32[]{:S(2)}, u32[]{:S(2)}) collective-permute-start(bf16[256,576]{1,0:T(8,128)(2,1)S(1)} %copy.11), channel_id=1, source_target_pairs={{0,8},{8,0},{1,9},{9,1},{2,10},{10,2},{3,11},{11,3},{4,12},{12,4},... | collective-permute-start | bytes 884744 | tf_op jit(solution)/shard_map/ppermute | solution.py:292
  18.5 1.6 %collective-permute-done.far_x_ref = bf16[256,576]{1,0:T(8,128)(2,1)S(1)} collective-permute-done((bf16[256,576]{1,0:T(8,128)(2,1)S(1)}, bf16[256,576]{1,0:T(8,128)(2,1)S(1)}, u32[]{:S(2)}, u32[]{:S(2)}) %collective-permute-start) | collective-permute-done | bytes 294944 | tf_op jit(solution)/shard_map/ppermute | solution.py:292
  20.1 0.7 copy-done.1
  20.8 4.8 %all-to-all-done.recv_ref = bf16[8,240,128]{2,1,0:T(8,128)(2,1)S(1)} async-done(((bf16[8,240,128]{2,1,0:T(8,128)(2,1)}), bf16[8,240,128]{2,1,0:T(8,128)(2,1)S(1)}, u32[]{:S(2)}, u32[]{:S(2)}) %all-to-all-start) | async-done | bytes 491552 | tf_op jit(solution)/shard_map/all_to_all | solution.py:290
  25.6 1.0 copy-done.2
  26.6 1.5 %forward_kernel.1 = (bf16[8,72,384]{2,1,0:T(8,128)(2,1)S(1)}, bf16[384,640]{1,0:T(8,128)(2,1)S(1)}, bf16[512,640]{1,0:T(8,128)(2,1)S(1)}, bf16[512,640]{1,0:T(8,128)(2,1)S(1)}) custom-call(bf16[8,240,128]{2,1,0:T(8,128)(2,1)S(1)} %all-to-all-done.recv_ref, bf16[256,576]{1,0:T(8,128)(2,1)S(1)} %copy.9.x_ref, bf16[256,576]{1,0:T(8,128)(2,1)S(1)} %copy.15.g_ref, ...), custom_call_target="tpu_custom_call" | custom-call | tf_op jit(solution)/shard_map/forward_kernel/pallas_call | solution.py:271
  28.1 15.4 %all_to_all.25.parts_ref = bf16[8,72,384]{2,1,0:T(8,128)(2,1)S(1)} all-to-all(bf16[8,72,384]{2,1,0:T(8,128)(2,1)S(1)} %get-tuple-element.20), channel_id=1, replica_groups=mesh['z'=8,'yl'=4,'c'=2,'yh'=2,'x'=4] {'yh','x'}, dimensions={0} | all-to-all | bytes 884736 | tf_op jit(solution)/shard_map/all_to_all | solution.py:301
  43.5 1.1 activation_kernel.1
  44.5 3.6 %all-to-all-start.2 = ((bf16[8,72,384]{2,1,0:T(8,128)(2,1)}), bf16[8,72,384]{2,1,0:T(8,128)(2,1)S(1)}, u32[]{:S(2)}, u32[]{:S(2)}) async-start(bf16[8,72,384]{2,1,0:T(8,128)(2,1)} %get-tuple-element.21), calls=%async_computation.2 | async-start | bytes 884736 | tf_op jit(solution)/shard_map/all_to_all | solution.py:303
  48.1 3.3 %collective-permute-start.2 = (bf16[256,128]{1,0:T(8,128)(2,1)S(1)}, bf16[256,128]{1,0:T(8,128)(2,1)S(1)}, u32[]{:S(2)}, u32[]{:S(2)}) collective-permute-start(bf16[256,128]{1,0:T(8,128)(2,1)S(1)} %get-tuple-element.25), channel_id=1, source_target_pairs={{0,1},{1,0},{2,3},{3,2},{4,5},{5,4},{6,7},{7,6},{8,9},{9,8},{10,11... | collective-permute-start | bytes 196616 | tf_op jit(solution)/shard_map/ppermute | solution.py:294
  51.4 1.7 %collective-permute-done.2.near_half_ref = bf16[256,128]{1,0:T(8,128)(2,1)S(1)} collective-permute-done((bf16[256,128]{1,0:T(8,128)(2,1)S(1)}, bf16[256,128]{1,0:T(8,128)(2,1)S(1)}, u32[]{:S(2)}, u32[]{:S(2)}) %collective-permute-start.2) | collective-permute-done | bytes 65568 | tf_op jit(solution)/shard_map/ppermute | solution.py:294
  53.2 8.7 %collective-permute-start.3 = (bf16[256,128]{1,0:T(8,128)(2,1)S(1)}, bf16[256,128]{1,0:T(8,128)(2,1)S(1)}, u32[]{:S(2)}, u32[]{:S(2)}) collective-permute-start(bf16[256,128]{1,0:T(8,128)(2,1)S(1)} %collective-permute-done.2.near_half_ref), channel_id=1, source_target_pairs={{0,8},{8,0},{1,9},{9,1},{2,10},{10,2},{3,11},{11,3},{4,12},{12,4},... | collective-permute-start | bytes 196616 | tf_op jit(solution)/shard_map/ppermute | solution.py:295
  61.9 0.9 collective-permute-done.3.far_half_ref
  62.8 0.6 copy-done.6
  63.4 2.5 %gradient_kernel.1 = (bf16[32,64,128]{2,1,0:T(8,128)(2,1)S(1)}, f32[256,640]{1,0:T(8,128)S(1)}, bf16[256,640]{1,0:T(8,128)(2,1)S(1)}) custom-call(bf16[8,72,384]{2,1,0:T(8,128)(2,1)S(1)} %all-to-all-done.2.acts_ref, bf16[384,640]{1,0:T(8,128)(2,1)S(1)} %get-tuple-element.22.w_ref, bf16[512,640]{1,0:T(8,128)(2,1)S(1)} %get-tuple-element.23.xa_ref, ...), custom_call_target="tpu_custom_call" | custom-call | tf_op jit(solution)/shard_map/gradient_kernel/pallas_call | solution.py:271
  66.0 33.2 %all_to_all.26.terms_ref = bf16[32,64,128]{2,1,0:T(8,128)(2,1)S(1)} all-to-all(bf16[32,64,128]{2,1,0:T(8,128)(2,1)S(1)} %get-tuple-element.29), channel_id=1, replica_groups=mesh['z'=8,'yl'=4,'c'=2,'yh'=2,'x'=4] {'z','yl'}, dimensions={0} | all-to-all | bytes 1048576 | tf_op jit(solution)/shard_map/all_to_all | solution.py:309
  99.2 0.1 total_kernel.1
  99.3 32.7 %all_to_all.27 = bf16[256,8,128]{2,1,0:T(8,128)(2,1)S(1)} all-to-all(bf16[256,8,128]{2,1,0:T(8,128)(2,1)S(1)} %bitcast.6), channel_id=1, replica_groups=mesh['z'=8,'yl'=4,'c'=2,'yh'=2,'x'=4] {'z','yl','yh','x'}, dimensions={0} | all-to-all | bytes 1048576 | tf_op jit(solution)/shard_map/all_to_all | solution.py:313
  132.1 5.8 %collective-permute-start.5 = (bf16[32,64,128]{2,1,0:T(8,128)(2,1)S(1)}, bf16[32,64,128]{2,1,0:T(8,128)(2,1)S(1)}, u32[]{:S(2)}, u32[]{:S(2)}) collective-permute-start(bf16[32,64,128]{2,1,0:T(8,128)(2,1)S(1)} %bitcast.4), channel_id=1, source_target_pairs={{0,8},{8,0},{1,9},{9,1},{2,10},{10,2},{3,11},{11,3},{4,12},{12,4},... | collective-permute-start | bytes 1572872 | tf_op jit(solution)/shard_map/ppermute | solution.py:314
  137.9 1.9 %collective-permute-start.4 = (bf16[256,640]{1,0:T(8,128)(2,1)S(1)}, bf16[256,640]{1,0:T(8,128)(2,1)S(1)}, u32[]{:S(2)}, u32[]{:S(2)}) collective-permute-start(bf16[256,640]{1,0:T(8,128)(2,1)S(1)} %get-tuple-element.28), channel_id=1, source_target_pairs={{0,8},{8,0},{1,9},{9,1},{2,10},{10,2},{3,11},{11,3},{4,12},{12,4},... | collective-permute-start | bytes 983048 | tf_op jit(solution)/shard_map/ppermute | solution.py:310
  139.8 1.6 %collective-permute-done.4.far_ref = bf16[256,640]{1,0:T(8,128)(2,1)S(1)} collective-permute-done((bf16[256,640]{1,0:T(8,128)(2,1)S(1)}, bf16[256,640]{1,0:T(8,128)(2,1)S(1)}, u32[]{:S(2)}, u32[]{:S(2)}) %collective-permute-start.4) | collective-permute-done | bytes 327712 | tf_op jit(solution)/shard_map/ppermute | solution.py:310
  141.4 0.3 resid_kernel.1
  141.6 0.9 copy.16
  142.5 2.0 %restore_kernel.1 = bf16[3,32,4608]{2,1,0:T(8,128)(2,1)} custom-call(bf16[32,64,128]{2,1,0:T(8,128)(2,1)S(1)} %bitcast.5, bf16[32,64,128]{2,1,0:T(8,128)(2,1)S(1)} %collective-permute-done.5.far_ref, s32[36,128]{1,0:T(8,128)S(1)} %bitcast.10, bf16[128,128]{1,0:T(8,128)(2,1)S(1)} %copy-done.3, s32[3]{0:T(128)S(1)} %copy-done.6), custom_call_target="tpu_custom_call" | custom-call | tf_op jit(solution)/shard_map/restore_kernel/pallas_call | solution.py:271
  (17 shorter events, 0.0 us)
Async XLA Ops:
  0.6 1.3 copy-start.8
  0.6 1.5 %copy-start = (bf16[3,32,4608]{2,1,0:T(8,128)(2,1)S(1)}, bf16[3,32,4608]{2,1,0:T(8,128)(2,1)}, u32[]{:S(2)}) copy-start(bf16[3,32,4608]{2,1,0:T(8,128)(2,1)} %w_ref.1) | copy-start | bytes 2654212
  3.0 10.2 %copy-start.7 = (bf16[256,576]{0,1:T(8,128)(2,1)S(1)}, bf16[256,576]{0,1:T(8,128)(2,1)}, u32[]{:S(2)}) copy-start(bf16[256,576]{0,1:T(8,128)(2,1)} %param.8) | copy-start | bytes 884740
  3.0 22.6 %all-to-all-start = ((bf16[8,240,128]{2,1,0:T(8,128)(2,1)}), bf16[8,240,128]{2,1,0:T(8,128)(2,1)S(1)}, u32[]{:S(2)}, u32[]{:S(2)}) async-start(bf16[8,240,128]{2,1,0:T(8,128)(2,1)} %get-tuple-element.16), calls=%async_computation | async-start | bytes 983040 | tf_op jit(solution)/shard_map/all_to_all | solution.py:290
  13.5 12.1 %copy-start.4 = (f32[4608]{0:T(1024)S(1)}, f32[4608]{0:T(1024)}, u32[]{:S(2)}) copy-start(f32[4608]{0:T(1024)} %param.10) | copy-start | bytes 55300
  13.5 5.0 %collective-permute-start.1 = (bf16[256,576]{1,0:T(8,128)(2,1)S(1)}, bf16[256,576]{1,0:T(8,128)(2,1)S(1)}, u32[]{:S(2)}, u32[]{:S(2)}) collective-permute-start(bf16[256,576]{1,0:T(8,128)(2,1)S(1)} %copy.12), channel_id=1, source_target_pairs={{0,8},{8,0},{1,9},{9,1},{2,10},{10,2},{3,11},{11,3},{4,12},{12,4},... | collective-permute-start | bytes 884744 | tf_op jit(solution)/shard_map/ppermute | solution.py:293
  16.6 3.5 %collective-permute-start = (bf16[256,576]{1,0:T(8,128)(2,1)S(1)}, bf16[256,576]{1,0:T(8,128)(2,1)S(1)}, u32[]{:S(2)}, u32[]{:S(2)}) collective-permute-start(bf16[256,576]{1,0:T(8,128)(2,1)S(1)} %copy.11), channel_id=1, source_target_pairs={{0,8},{8,0},{1,9},{9,1},{2,10},{10,2},{3,11},{11,3},{4,12},{12,4},... | collective-permute-start | bytes 884744 | tf_op jit(solution)/shard_map/ppermute | solution.py:292
  20.1 0.7 copy-start.1
  25.6 1.0 copy-start.2
  44.5 18.2 %copy-start.3 = (bf16[128,128]{1,0:T(8,128)(2,1)S(1)}, bf16[128,128]{1,0:T(8,128)(2,1)}, u32[]{:S(2)}) copy-start(bf16[128,128]{1,0:T(8,128)(2,1)} %constant.2.clone.table_ref) | copy-start | bytes 98308
  44.5 18.2 %copy-start.5 = (s32[4608]{0:T(1024)S(1)}, s32[4608]{0:T(1024)}, u32[]{:S(2)}) copy-start(s32[4608]{0:T(1024)} %param.12) | copy-start | bytes 55300
  44.5 18.2 %all-to-all-start.2 = ((bf16[8,72,384]{2,1,0:T(8,128)(2,1)}), bf16[8,72,384]{2,1,0:T(8,128)(2,1)S(1)}, u32[]{:S(2)}, u32[]{:S(2)}) async-start(bf16[8,72,384]{2,1,0:T(8,128)(2,1)} %get-tuple-element.21), calls=%async_computation.2 | async-start | bytes 884736 | tf_op jit(solution)/shard_map/all_to_all | solution.py:303
  48.1 5.0 %collective-permute-start.2 = (bf16[256,128]{1,0:T(8,128)(2,1)S(1)}, bf16[256,128]{1,0:T(8,128)(2,1)S(1)}, u32[]{:S(2)}, u32[]{:S(2)}) collective-permute-start(bf16[256,128]{1,0:T(8,128)(2,1)S(1)} %get-tuple-element.25), channel_id=1, source_target_pairs={{0,1},{1,0},{2,3},{3,2},{4,5},{5,4},{6,7},{7,6},{8,9},{9,8},{10,11... | collective-permute-start | bytes 196616 | tf_op jit(solution)/shard_map/ppermute | solution.py:294
  53.2 9.6 %collective-permute-start.3 = (bf16[256,128]{1,0:T(8,128)(2,1)S(1)}, bf16[256,128]{1,0:T(8,128)(2,1)S(1)}, u32[]{:S(2)}, u32[]{:S(2)}) collective-permute-start(bf16[256,128]{1,0:T(8,128)(2,1)S(1)} %collective-permute-done.2.near_half_ref), channel_id=1, source_target_pairs={{0,8},{8,0},{1,9},{9,1},{2,10},{10,2},{3,11},{11,3},{4,12},{12,4},... | collective-permute-start | bytes 196616 | tf_op jit(solution)/shard_map/ppermute | solution.py:295
  62.7 0.7 copy-start.6
  132.1 10.5 %collective-permute-start.5 = (bf16[32,64,128]{2,1,0:T(8,128)(2,1)S(1)}, bf16[32,64,128]{2,1,0:T(8,128)(2,1)S(1)}, u32[]{:S(2)}, u32[]{:S(2)}) collective-permute-start(bf16[32,64,128]{2,1,0:T(8,128)(2,1)S(1)} %bitcast.4), channel_id=1, source_target_pairs={{0,8},{8,0},{1,9},{9,1},{2,10},{10,2},{3,11},{11,3},{4,12},{12,4},... | collective-permute-start | bytes 1572872 | tf_op jit(solution)/shard_map/ppermute | solution.py:314
  137.9 3.5 %collective-permute-start.4 = (bf16[256,640]{1,0:T(8,128)(2,1)S(1)}, bf16[256,640]{1,0:T(8,128)(2,1)S(1)}, u32[]{:S(2)}, u32[]{:S(2)}) collective-permute-start(bf16[256,640]{1,0:T(8,128)(2,1)S(1)} %get-tuple-element.28), channel_id=1, source_target_pairs={{0,8},{8,0},{1,9},{9,1},{2,10},{10,2},{3,11},{11,3},{4,12},{12,4},... | collective-permute-start | bytes 983048 | tf_op jit(solution)/shard_map/ppermute | solution.py:310

commit v3 on v2

v3 whole, which is shorter than its diff:
```python
import functools

import jax
import jax.numpy as jnp
import numpy as np
from jax import lax
from jax.experimental import pallas as pl
from jax.experimental.pallas import tpu as pltpu
from jax.sharding import Mesh
from jax.sharding import PartitionSpec as P

F32 = jnp.float32
BF16 = jnp.bfloat16
AXES = ("z", "yl", "c", "yh", "x")
DP = ("z", "yl", "c")
MP = ("yh", "x")
VMEM_LIMIT = 40 * 1024 * 1024
FEATURES = 4608
CONTRACT_LAST = (((1,), (1,)), ((), ()))
CONTRACT_FIRST = (((0,), (0,)), ((), ()))


def signed_hadamard():
    table = np.array([[1.0]], np.float32)
    for _ in range(7):
        table = np.block([[table, table], [table, -table]])
    return table


def gelu_parts(values):
    tanh_input = 0.7978845608 * (values + 0.044715 * values * values * values)
    tanhed = jnp.tanh(tanh_input)
    forward = 0.5 * values * (1.0 + tanhed)
    gelu_slope = 0.5 * (1.0 + tanhed) + 0.5 * values * (1.0 - tanhed * tanhed) * 0.7978845608 * (
        1.0 + 3.0 * 0.044715 * values * values
    )
    return (forward, gelu_slope)


def pieces(values):
    high = values.astype(BF16)
    rest = values - high.astype(F32)
    middle = rest.astype(BF16)
    low = (rest - middle.astype(F32)).astype(BF16)
    return (high, middle, low)


def dot(left, right, dims=(((1,), (0,)), ((), ()))):
    return lax.dot_general(left, right, dims, preferred_element_type=F32)


def places():
    odd = lax.axis_index("x") % 2
    pair = lax.axis_index("yh") * 2 + lax.axis_index("x") // 2
    return (lax.axis_index("c"), odd, pair * 9)


def local_rows(table_ref, first, odd):
    return [table_ref[pl.ds(first + 5 * odd + b, 1), :] for b in range(4)] + [table_ref[pl.ds(first + 4, 1), :]]


def own_rows(odd):
    return (
        pl.ds(pl.multiple_of(odd * 64, 64), 512),
        pl.ds(pl.multiple_of((1 - odd) * 512, 64), 64),
    )


def prepare_kernel(w_ref, send_ref, sems):
    core, _, _ = places()
    rows = pl.ds(pl.multiple_of(core * 16, 16), 16)
    copies = []
    for m in range(8):
        start = 9 * (m // 2)
        for b, block in enumerate([start + 5 * (m % 2) + b for b in range(4)] + [start + 4]):
            copies.append(
                pltpu.make_async_copy(
                    w_ref.at[:, rows, pl.ds(block * 128, 128)], send_ref.at[m, b], sems.at[m * 5 + b]
                )
            )
    for copy in copies:
        copy.start()
    for copy in copies:
        copy.wait()


def forward_kernel(recv_ref, x_ref, g_ref, far_x_ref, far_g_ref, gain_ref, part_ref, w_ref, xa_ref, ga_ref, half_ref):
    _, odd, first = places()
    for j in range(8):
        for b in range(5):
            for k in range(3):
                w_ref[k * 128 + j * 16 : k * 128 + j * 16 + 16, b * 128 : (b + 1) * 128] = recv_ref[j, b, k]
    main, half = own_rows(odd)
    mine = pl.ds(pl.multiple_of(512 + odd * 64, 64), 64)
    theirs = pl.ds(pl.multiple_of(576 - odd * 64, 64), 64)
    for part, (to_ref, refs) in enumerate(((xa_ref, (x_ref, far_x_ref)), (ga_ref, (g_ref, far_g_ref)))):
        for side, ref in enumerate(refs):
            tokens = pl.ds(side * 256, 256)
            to_ref[0:512, tokens] = ref[main, :]
            to_ref[mine, tokens] = ref[half, :]
            to_ref[theirs, tokens] = jnp.zeros((64, 256), BF16)
            half_ref[pl.ds(64 * part, 64), tokens] = ref[half, :]
    gained = w_ref[0:256].astype(F32) * jnp.concatenate(local_rows(gain_ref, first, odd), axis=1)
    high = gained.astype(BF16)
    low = (gained - high.astype(F32)).astype(BF16)
    gate_up = (dot(low, xa_ref[...]) + dot(high, xa_ref[...])).astype(BF16)
    down = dot(w_ref[256:384], ga_ref[...]).astype(BF16)
    wide = xa_ref[...].astype(F32)
    sums = jnp.sum(wide * wide, axis=0, keepdims=True)
    tail = stacked_pieces(sums)
    for j in range(8):
        x, yh = j % 4, j // 4
        part_ref[x, yh, 0:16, :] = gate_up[j * 16 : j * 16 + 16]
        part_ref[x, yh, 16:32, :] = gate_up[128 + j * 16 : 128 + j * 16 + 16]
        part_ref[x, yh, 32:48, :] = down[j * 16 : j * 16 + 16]
        part_ref[x, yh, 48:56, :] = tail


def stacked_pieces(row):
    place = lax.broadcasted_iota(jnp.int32, (8, 512), 0)
    tail = jnp.zeros((8, 512), F32)
    for i, piece in enumerate(pieces(row)):
        tail = jnp.where(place == i, piece.astype(F32), tail)
    return tail.astype(BF16)


def sum_kernel(parts_ref, out_ref):
    for yh in range(2):
        total = parts_ref[0, yh].astype(F32)
        for i in range(1, 4):
            total = total + parts_ref[i, yh].astype(F32)
        out_ref[yh, 0:48, :] = total[0:48].astype(BF16)
        out_ref[yh, 48:56, :] = stacked_pieces(total[48:49] + total[49:50] + total[50:51])


def activation_kernel(parts_ref, out_ref, inv_ref):
    for yh in range(2):
        total = parts_ref[0, yh].astype(F32) + parts_ref[1, yh].astype(F32)
        sums = total[48:49] + total[49:50] + total[50:51]
        inverse = lax.rsqrt(sums / FEATURES + 1e-06)
        inv_ref[...] = jnp.broadcast_to(inverse, (8, 512))
        gate_pre, up_proj, hidden_grad = total[0:16] * inverse, total[16:32] * inverse, total[32:48]
        activated, slope = gelu_parts(gate_pre)
        hidden = (activated * up_proj).astype(BF16)
        gate_grad = (hidden_grad * up_proj * slope).astype(BF16)
        up_grad = (hidden_grad * activated).astype(BF16)
        products = gate_grad.astype(F32) * gate_pre + up_grad.astype(F32) * up_proj
        tail = stacked_pieces(jnp.sum(products, axis=0, keepdims=True) / FEATURES)
        for i in range(4):
            out_ref[i, yh, 0:16, :] = gate_grad
            out_ref[i, yh, 16:32, :] = up_grad
            out_ref[i, yh, 32:48, :] = hidden
            out_ref[i, yh, 48:56, :] = tail


def gradient_kernel(
    acts_ref, w_ref, xa_ref, ga_ref, half_ref, inv_ref, gain_ref, sign_ref, table_ref, exps_ref,
    term_ref, near_ref, far_ref,
):
    _, odd, first = places()
    table = table_ref[...]
    sign = (2 * jnp.concatenate(local_rows(sign_ref, first, odd), axis=1) - 1).astype(F32)
    diagonal = lax.broadcasted_iota(jnp.int32, (128, 128), 0) == lax.broadcasted_iota(jnp.int32, (128, 128), 1)
    gain = jnp.concatenate(
        [
            jnp.sum(jnp.where(diagonal, row, 0.0), axis=1, keepdims=True)
            for row in local_rows(gain_ref, first, odd)
        ],
        axis=0,
    )
    acts = [
        jnp.concatenate([acts_ref[j % 4, j // 4, k * 16 : k * 16 + 16, :] for j in range(8)], axis=0)
        for k in range(3)
    ]
    tails = acts_ref[0, 0, 48:56, :].astype(F32)
    for j in range(1, 8):
        tails = tails + acts_ref[j % 4, j // 4, 48:56, :].astype(F32)
    row_mean = tails[0:1] + tails[1:2] + tails[2:3]
    inverse = inv_ref[0:1, :]
    theirs = (lax.broadcasted_iota(jnp.int32, (128, 512), 0) >= 64) == (odd == 0)
    shared = []
    for part, ref in enumerate((xa_ref, ga_ref)):
        other = half_ref[part * 64 : part * 64 + 64, :].astype(F32)
        shared.append(
            jnp.where(theirs, jnp.concatenate([other, other], axis=0), ref[512:640, :].astype(F32))
        )
    unit = jnp.concatenate([xa_ref[0:512, :].astype(F32), shared[0]], axis=0) * inverse
    normed = (unit * gain).astype(BF16)
    grads = jnp.concatenate([ga_ref[0:512, :], shared[1].astype(BF16)], axis=0)
    rights = (normed, normed, grads)
    for k in range(3):
        scale = jnp.left_shift(1, exps_ref[k]).astype(F32) * float(128.0**-0.5)
        terms = [
            dot(acts[k][:, s * 256 : s * 256 + 256], rights[k][:, s * 256 : s * 256 + 256], CONTRACT_LAST) * sign
            for s in range(2)
        ]
        for b in range(5):
            total = None
            for term in terms:
                high, middle, low = pieces(term[:, b * 128 : (b + 1) * 128])
                rotated = (dot(low, table) + dot(middle, table)) + dot(high, table)
                quantized = jnp.clip(rotated * scale, -127.0, 127.0).astype(BF16).astype(F32)
                total = quantized if total is None else total + quantized
            half = total.reshape(8, 2, 8, 128)
            if b < 4:
                term_ref[k * 8 + b] = half[:, 0].reshape(64, 128).astype(BF16)
                term_ref[k * 8 + 4 + b] = half[:, 1].reshape(64, 128).astype(BF16)
            else:
                chosen = jnp.where(odd == 1, half[:, 1], half[:, 0])
                term_ref[24 + k] = chosen.reshape(64, 128).astype(BF16)
    for s in range(27, 32):
        term_ref[s] = jnp.zeros((64, 128), BF16)
    normed_grad = dot(w_ref[0:256], jnp.concatenate(acts[0:2], axis=0), CONTRACT_FIRST)
    resid = inverse * (normed_grad * gain - unit * row_mean)
    main, half = own_rows(odd)
    shared_half = jnp.where(odd == 1, resid[576:640], resid[512:576])
    near_ref[main, :] = resid[0:512, 0:256]
    near_ref[half, :] = shared_half[:, 0:256]
    far_ref[main, :] = resid[0:512, 256:512].astype(BF16)
    far_ref[half, :] = shared_half[:, 256:512].astype(BF16)


def total_kernel(terms_ref, g_ref, near_ref, far_ref, share_ref, resid_ref):
    total = terms_ref[0].astype(F32)
    for i in range(1, 32):
        total = total + terms_ref[i].astype(F32)
    rounded = total.astype(BF16)
    for i in range(32):
        share_ref[i] = rounded
    resid_ref[...] = (g_ref[...].astype(F32) + (near_ref[...] + far_ref[...].astype(F32))).astype(BF16)


def restore_kernel(near_ref, far_ref, sign_ref, table_ref, exps_ref, out_ref):
    table = table_ref[...]
    core, _, _ = places()
    for k in range(3):
        e = exps_ref[k]
        factor = jnp.where(e == 3, 2.0**-9, jnp.where(e == 4, 2.0**-10, jnp.where(e == 5, 2.0**-11, 2.0**-12)))
        factor = factor.astype(F32) * float(128.0**-0.5)
        for q, share_ref in ((core, near_ref), (1 - core, far_ref)):
            rows = pl.ds(pl.multiple_of(16 * q, 16), 16)

            def put(block, low_half, high_half):
                sign = (2 * sign_ref[block : block + 1, :] - 1).astype(F32) * factor
                both = jnp.concatenate([low_half, high_half], axis=0) * sign
                out_ref[k, rows, block * 128 : (block + 1) * 128] = both.astype(BF16)

            for b in range(4):
                halves = [dot(share_ref[k * 8 + 4 * i + b], table) for i in range(2)]
                for m in range(8):
                    put(
                        9 * (m // 2) + 5 * (m % 2) + b,
                        halves[0][m * 8 : m * 8 + 8],
                        halves[1][m * 8 : m * 8 + 8],
                    )
            shared = dot(share_ref[24 + k], table)
            for p in range(4):
                put(9 * p + 4, shared[16 * p : 16 * p + 8], shared[16 * p + 8 : 16 * p + 16])


def call(kernel, outs, scalars=0, scratch=(), space=pltpu.VMEM):
    def run(*operands):
        count = len(operands)
        spaces = [pltpu.SMEM if i >= count - scalars else space for i in range(count)]
        return pl.pallas_call(
            kernel,
            out_shape=[jax.ShapeDtypeStruct(shape, dtype) for shape, dtype in outs],
            in_specs=[pl.BlockSpec(memory_space=place) for place in spaces],
            out_specs=[pl.BlockSpec(memory_space=space) for _ in outs],
            scratch_shapes=list(scratch),
            compiler_params=pltpu.CompilerParams(vmem_limit_bytes=VMEM_LIMIT),
            name=kernel.__name__,
        )(*operands)

    return run


def per_device(residual, out_grad, ffn_weights, norm_gain, exponents, sign_bits):
    gain = norm_gain.reshape(36, 128)
    signs = sign_bits.reshape(36, 128)
    table = jnp.asarray(signed_hadamard(), BF16)
    cores = [(0, 1), (1, 0)]
    x_cols, g_cols = residual.T, out_grad.T

    (send,) = call(
        prepare_kernel, [((8, 5, 3, 16, 128), BF16)], scratch=[pltpu.SemaphoreType.DMA((40,))], space=pl.ANY
    )(ffn_weights)
    received = lax.all_to_all(send.reshape(8, 240, 128), AXES, 0, 0, axis_index_groups=near_groups())
    near_x, near_g, _ = lax.optimization_barrier((x_cols, g_cols, send))
    far_x = lax.ppermute(near_x, "c", cores)
    far_g = lax.ppermute(near_g, "c", cores)
    parts, weights, x_aligned, g_aligned, half = call(
        forward_kernel,
        [((4, 2, 56, 512), BF16), ((384, 640), BF16), ((640, 512), BF16), ((640, 512), BF16), ((128, 512), BF16)],
    )(received.reshape(8, 5, 3, 16, 128), x_cols, g_cols, far_x, far_g, gain)

    other_half = lax.ppermute(half, "x", [(0, 1), (1, 0), (2, 3), (3, 2)])
    parts = lax.all_to_all(parts.reshape(4, 112, 512), "x", 0, 0)
    parts, other_half = lax.optimization_barrier((parts, other_half))
    (sums,) = call(sum_kernel, [((2, 56, 512), BF16)])(parts.reshape(4, 2, 56, 512))
    sums = lax.all_gather(sums, "yh", axis=0)
    message, inverse = call(activation_kernel, [((4, 2, 56, 512), BF16), ((8, 512), F32)])(sums)
    acts = lax.all_to_all(message.reshape(4, 112, 512), "x", 0, 0).reshape(4, 2, 56, 512)
    terms, near_resid, far_resid = call(
        gradient_kernel,
        [((32, 64, 128), BF16), ((576, 256), F32), ((576, 256), BF16)],
        scalars=1,
    )(acts, weights, x_aligned, g_aligned, other_half, inverse, gain, signs, table, exponents)
    terms = lax.all_to_all(terms, ("z", "yl"), 0, 0)
    far_resid = lax.ppermute(far_resid, "c", cores)
    share, resid_cols = call(total_kernel, [((32, 64, 128), BF16), ((576, 256), BF16)])(
        terms, g_cols, near_resid, far_resid
    )
    share = lax.all_to_all(share.reshape(256, 8, 128), ("z", "yl", "yh", "x"), 0, 0).reshape(32, 64, 128)
    other = lax.ppermute(share, "c", cores)
    (weight_grads,) = call(restore_kernel, [((3, 32, 4608), BF16)], scalars=1)(
        share, other, signs, table, exponents
    )
    return (resid_cols.T, weight_grads)


def near_groups():
    def flat(z, yl, c, yh, x):
        return (((z * 4 + yl) * 2 + c) * 2 + yh) * 4 + x

    return [
        [flat(z, 3 - yl if yh else yl, c, yh, x) for yh in range(2) for x in range(4)]
        for z in range(8)
        for yl in range(4)
        for c in range(2)
    ]


def solution(mesh):
    fine = Mesh(mesh.devices.reshape(8, 4, 2, 2, 4), AXES)
    rows = P(DP, MP)
    return jax.shard_map(
        per_device,
        mesh=fine,
        in_specs=(rows, rows, P(None, MP, None), P(), P(), P()),
        out_specs=(rows, P(None, MP, None)),
        check_vma=False,
    )
```

time: 145 us -> 128 us (0.88)
  blocking collectives: 81.4 us -> 46.9 us
  starting transfers between devices: 38.3 us -> 53.9 us
  waiting for transfers between devices: 10.6 us -> 13.6 us
  local copies, waits for them, and re-layouts: 5.11 us -> 3.22 us
    all_to_all x2 -> x1, blocking collectives: 48.6 us -> 10.1 us  [per_device(): lax.all_to_all(message.reshape(4, 112, 512), 'x', 0, 0)]
    all_to_all x2 -> x3, starting transfers between devices: 13.8 us -> 27.7 us  [the longest x1 15.4 us: per_device(): terms = lax.all_to_all(terms, ('z', 'yl'), 0, 0)]
    all_gather x0 -> x1, blocking collectives: none -> 10.8 us  [per_device(): sums = lax.all_gather(sums, 'yh', axis=0)]
    ppermute x2 -> x1, starting transfers between devices: 12 us -> 3.36 us  [per_device(): other_half = lax.ppermute(half, 'x', [(0, 1), (1, 0), (2, 3), (3, 2)])]
    all_to_all x1, blocking collectives: 32.7 us -> 26.1 us  [per_device(): lax.all_to_all(share.reshape(256, 8, 128), ('z', 'yl', 'yh', 'x'), 0, 0)]
    ppermute x1, starting transfers between devices: 1.92 us -> 7.56 us  [per_device(): far_resid = lax.ppermute(far_resid, 'c', cores)]
    ppermute x1, starting transfers between devices: 5.79 us -> 8.85 us  [per_device(): other = lax.ppermute(share, 'c', cores)]
    ppermute x1, starting transfers between devices: 1.92 us -> 4.53 us  [per_device(): far_x = lax.ppermute(near_x, 'c', cores)]
  transfers between devices with their start and end apart: 8 -> 8, of which waited for: 5 -> 7; matrix products, arithmetic and copies ran while one was open for 1% -> 0% of each run, Pallas kernels for 0% -> 0%
where the time goes in v3:
time: 128 us
  starting transfers between devices  53.9 us (42%)
  blocking collectives  46.9 us (37%)
  waiting for transfers between devices  13.6 us (11%)
  Pallas kernels  9.13 us (7%)
  local copies, waits for them, and re-layouts  3.22 us (3%)
    all_to_all x1, blocking collectives, per_device(): lax.all_to_all(share.reshape(256, 8, 128), ('z', 'yl', 'yh', 'x'), 0, 0)  26.1 us
    all_to_all x1, starting transfers between devices, per_device(): terms = lax.all_to_all(terms, ('z', 'yl'), 0, 0)  15.4 us
    all_gather x1, blocking collectives, per_device(): sums = lax.all_gather(sums, 'yh', axis=0)  10.8 us
    all_to_all x1, blocking collectives, per_device(): lax.all_to_all(message.reshape(4, 112, 512), 'x', 0, 0)  10.1 us
    pallas_call x7, Pallas kernels, run(): pl.pallas_call(kernel, out_shape=[jax.ShapeDtypeStruct(shape, dtype) for...  9.13 us
    ppermute x1, starting transfers between devices, per_device(): other = lax.ppermute(share, 'c', cores)  8.85 us
    all_to_all x1, starting transfers between devices, per_device(): lax.all_to_all(send.reshape(8, 240, 128), AXES, 0, 0, axis_index_groups=n...  7.9 us
    ppermute x1, starting transfers between devices, per_device(): far_resid = lax.ppermute(far_resid, 'c', cores)  7.56 us
  transfers between devices with their start and end apart: 8, of which 7 were waited for; matrix products, arithmetic and copies ran while one was open for 0% of the time, Pallas kernels for 0%

profile of v3, /device:TPU:1, one launch (start us, length us, event | category | flops | bytes accessed | tf_op | source)
XLA Modules:
  0.0 127.5 jit_solution(16483239578751642531)
XLA Ops:
  0.6 1.2 copy-done.1
  1.8 1.1 prepare_kernel.1
  2.9 0.0 copy-start.2
  2.9 7.9 %all-to-all-start = ((bf16[8,240,128]{2,1,0:T(8,128)(2,1)}), bf16[8,240,128]{2,1,0:T(8,128)(2,1)S(1)}, u32[]{:S(2)}, u32[]{:S(2)}) async-start(bf16[8,240,128]{2,1,0:T(8,128)(2,1)} %bitcast), calls=%async_computation | async-start | bytes 983040 | tf_op jit(solution)/shard_map/all_to_all | solution.py:288
  10.8 4.5 %collective-permute-start = (bf16[576,256]{1,0:T(8,128)(2,1)S(1)}, bf16[576,256]{1,0:T(8,128)(2,1)S(1)}, u32[]{:S(2)}, u32[]{:S(2)}) collective-permute-start(bf16[576,256]{1,0:T(8,128)(2,1)S(1)} %bitcast.25), channel_id=1, source_target_pairs={{0,8},{8,0},{1,9},{9,1},{2,10},{10,2},{3,11},{11,3},{4,12},{12,4},... | collective-permute-start | bytes 884744 | tf_op jit(solution)/shard_map/ppermute | solution.py:290
  15.4 1.9 %collective-permute-start.1 = (bf16[576,256]{1,0:T(8,128)(2,1)S(1)}, bf16[576,256]{1,0:T(8,128)(2,1)S(1)}, u32[]{:S(2)}, u32[]{:S(2)}) collective-permute-start(bf16[576,256]{1,0:T(8,128)(2,1)S(1)} %bitcast.19), channel_id=1, source_target_pairs={{0,8},{8,0},{1,9},{9,1},{2,10},{10,2},{3,11},{11,3},{4,12},{12,4},... | collective-permute-start | bytes 884744 | tf_op jit(solution)/shard_map/ppermute | solution.py:291
  17.3 1.5 %collective-permute-done.1.far_g_ref = bf16[576,256]{1,0:T(8,128)(2,1)S(1)} collective-permute-done((bf16[576,256]{1,0:T(8,128)(2,1)S(1)}, bf16[576,256]{1,0:T(8,128)(2,1)S(1)}, u32[]{:S(2)}, u32[]{:S(2)}) %collective-permute-start.1) | collective-permute-done | bytes 294944 | tf_op jit(solution)/shard_map/ppermute | solution.py:291
  18.9 1.5 %all-to-all-done = bf16[8,240,128]{2,1,0:T(8,128)(2,1)S(1)} async-done(((bf16[8,240,128]{2,1,0:T(8,128)(2,1)}), bf16[8,240,128]{2,1,0:T(8,128)(2,1)S(1)}, u32[]{:S(2)}, u32[]{:S(2)}) %all-to-all-start) | async-done | bytes 491552 | tf_op jit(solution)/shard_map/all_to_all | solution.py:288
  20.3 1.5 %forward_kernel.1 = (bf16[4,2,56,512]{3,2,1,0:T(8,128)(2,1)}, bf16[384,640]{1,0:T(8,128)(2,1)S(1)}, bf16[640,512]{1,0:T(8,128)(2,1)S(1)}, bf16[640,512]{1,0:T(8,128)(2,1)S(1)}, bf16[128,512]{1,0:T(8,128)(2,1)S(1)}) custom-call(bf16[8,5,3,16,128]{4,3,2,1,0:T(8,128)(2,1)S(1)} %bitcast.16, bf16[576,256]{1,0:T(8,128)(2,1)S(1)} %bitcast.26, ...), custom_call_target="tpu_custom_call" | custom-call | tf_op jit(solution)/shard_map/forward_kernel/pallas_call | solution.py:265
  21.9 0.7 copy-done.9
  22.5 4.4 %all-to-all-start.1 = ((bf16[4,112,512]{2,1,0:T(8,128)(2,1)}), bf16[4,112,512]{2,1,0:T(8,128)(2,1)S(1)}, u32[]{:S(2)}, u32[]{:S(2)}) async-start(bf16[4,112,512]{2,1,0:T(8,128)(2,1)} %bitcast.5), calls=%async_computation.1 | async-start | bytes 917504 | tf_op jit(solution)/shard_map/all_to_all | solution.py:298
  26.9 3.4 %collective-permute-start.2 = (bf16[128,512]{1,0:T(8,128)(2,1)S(1)}, bf16[128,512]{1,0:T(8,128)(2,1)S(1)}, u32[]{:S(2)}, u32[]{:S(2)}) collective-permute-start(bf16[128,512]{1,0:T(8,128)(2,1)S(1)} %copy-done.10), channel_id=1, source_target_pairs={{0,1},{1,0},{2,3},{3,2},{4,5},{5,4},{6,7},{7,6},{8,9},{9,8},{10,11... | collective-permute-start | bytes 393224 | tf_op jit(solution)/shard_map/ppermute | solution.py:297
  30.3 3.1 %collective-permute-done.2.half_ref = bf16[128,512]{1,0:T(8,128)(2,1)S(1)} collective-permute-done((bf16[128,512]{1,0:T(8,128)(2,1)S(1)}, bf16[128,512]{1,0:T(8,128)(2,1)S(1)}, u32[]{:S(2)}, u32[]{:S(2)}) %collective-permute-start.2) | collective-permute-done | bytes 131104 | tf_op jit(solution)/shard_map/ppermute | solution.py:297
  33.4 0.1 all-to-all-done.1
  33.5 0.1 sum_kernel.1
  33.6 10.8 %all-gather = bf16[4,56,512]{2,1,0:T(8,128)(2,1)S(1)} all-gather(bf16[2,56,512]{2,1,0:T(8,128)(2,1)S(1)} %sum_kernel.1), channel_id=2, replica_groups=mesh['z'=8,'yl'=4,'c'=2,'yh'=2,'x'=4] {'yh'}, dimensions={0}, use_global_device_ids=true | all-gather | bytes 344064 | tf_op jit(solution)/shard_map/all_gather | solution.py:301
  44.3 0.1 activation_kernel.1
  44.5 0.0 copy-start.3
  44.5 0.0 copy-start.4
  44.5 10.1 %all_to_all.25 = bf16[4,112,512]{2,1,0:T(8,128)(2,1)S(1)} all-to-all(bf16[4,112,512]{2,1,0:T(8,128)(2,1)S(1)} %bitcast.24), channel_id=1, replica_groups=mesh['z'=8,'yl'=4,'c'=2,'yh'=2,'x'=4] {'x'}, dimensions={0} | all-to-all | bytes 917504 | tf_op jit(solution)/shard_map/all_to_all | solution.py:303
  54.5 0.6 copy-done.6
  55.2 3.4 %gradient_kernel.1 = (bf16[32,64,128]{2,1,0:T(8,128)(2,1)}, f32[576,256]{1,0:T(8,128)S(1)}, bf16[576,256]{1,0:T(8,128)(2,1)S(1)}) custom-call(bf16[4,2,56,512]{3,2,1,0:T(8,128)(2,1)S(1)} %bitcast.18, bf16[384,640]{1,0:T(8,128)(2,1)S(1)} %get-tuple-element.24.w_ref, bf16[640,512]{1,0:T(8,128)(2,1)S(1)} %get-tuple-element.25.xa_ref, ...), custom_call_target="tpu_custom_call" | custom-call | tf_op jit(solution)/shard_map/gradient_kernel/pallas_call | solution.py:265
  58.6 0.7 copy-done.7
  59.3 15.4 %all-to-all-start.3 = ((bf16[32,64,128]{2,1,0:T(8,128)(2,1)}), bf16[32,64,128]{2,1,0:T(8,128)(2,1)S(1)}, u32[]{:S(2)}, u32[]{:S(2)}) async-start(bf16[32,64,128]{2,1,0:T(8,128)(2,1)} %get-tuple-element.29), calls=%async_computation.3 | async-start | bytes 1048576 | tf_op jit(solution)/shard_map/all_to_all | solution.py:309
  74.8 7.6 %collective-permute-start.3 = (bf16[576,256]{1,0:T(8,128)(2,1)S(1)}, bf16[576,256]{1,0:T(8,128)(2,1)S(1)}, u32[]{:S(2)}, u32[]{:S(2)}) collective-permute-start(bf16[576,256]{1,0:T(8,128)(2,1)S(1)} %copy-done.8), channel_id=1, source_target_pairs={{0,8},{8,0},{1,9},{9,1},{2,10},{10,2},{3,11},{11,3},{4,12},{12,4},... | collective-permute-start | bytes 884744 | tf_op jit(solution)/shard_map/ppermute | solution.py:310
  82.4 1.2 collective-permute-done.3.far_ref
  83.6 4.6 %all-to-all-done.3.terms_ref = bf16[32,64,128]{2,1,0:T(8,128)(2,1)S(1)} async-done(((bf16[32,64,128]{2,1,0:T(8,128)(2,1)}), bf16[32,64,128]{2,1,0:T(8,128)(2,1)S(1)}, u32[]{:S(2)}, u32[]{:S(2)}) %all-to-all-start.3) | async-done | bytes 524320 | tf_op jit(solution)/shard_map/all_to_all | solution.py:309
  88.2 0.8 total_kernel.1
  89.0 26.1 %all_to_all.26 = bf16[256,8,128]{2,1,0:T(8,128)(2,1)S(1)} all-to-all(bf16[256,8,128]{2,1,0:T(8,128)(2,1)S(1)} %bitcast.23), channel_id=1, replica_groups=mesh['z'=8,'yl'=4,'c'=2,'yh'=2,'x'=4] {'z','yl','yh','x'}, dimensions={0} | all-to-all | bytes 1048576 | tf_op jit(solution)/shard_map/all_to_all | solution.py:314
  115.1 8.8 %collective-permute-start.4 = (bf16[32,64,128]{2,1,0:T(8,128)(2,1)S(1)}, bf16[32,64,128]{2,1,0:T(8,128)(2,1)S(1)}, u32[]{:S(2)}, u32[]{:S(2)}) collective-permute-start(bf16[32,64,128]{2,1,0:T(8,128)(2,1)S(1)} %bitcast.14), channel_id=1, source_target_pairs={{0,8},{8,0},{1,9},{9,1},{2,10},{10,2},{3,11},{11,3},{4,12},{12,4},... | collective-permute-start | bytes 1572872 | tf_op jit(solution)/shard_map/ppermute | solution.py:315
  123.9 1.5 %collective-permute-done.4.far_ref = bf16[32,64,128]{2,1,0:T(8,128)(2,1)S(1)} collective-permute-done((bf16[32,64,128]{2,1,0:T(8,128)(2,1)S(1)}, bf16[32,64,128]{2,1,0:T(8,128)(2,1)S(1)}, u32[]{:S(2)}, u32[]{:S(2)}) %collective-permute-start.4) | collective-permute-done | bytes 524320 | tf_op jit(solution)/shard_map/ppermute | solution.py:315
  125.4 2.1 %restore_kernel.1 = bf16[3,32,4608]{2,1,0:T(8,128)(2,1)} custom-call(bf16[32,64,128]{2,1,0:T(8,128)(2,1)S(1)} %bitcast.15, bf16[32,64,128]{2,1,0:T(8,128)(2,1)S(1)} %collective-permute-done.4.far_ref, s32[36,128]{1,0:T(8,128)S(1)} %bitcast.28, bf16[128,128]{1,0:T(8,128)(2,1)S(1)} %copy-done.3, s32[3]{0:T(128)S(1)} %copy-done.6), custom_call_target="tpu_custom_call" | custom-call | tf_op jit(solution)/shard_map/restore_kernel/pallas_call | solution.py:265
  (16 shorter events, 0.0 us)
Async XLA Ops:
  0.6 1.2 copy-start.1
  2.9 7.9 %copy-start.2 = (bf16[256,576]{0,1:T(8,128)(2,1)S(1)}, bf16[256,576]{0,1:T(8,128)(2,1)}, u32[]{:S(2)}) copy-start(bf16[256,576]{0,1:T(8,128)(2,1)} %param.7) | copy-start | bytes 884740
  2.9 12.5 %copy-start = (bf16[256,576]{0,1:T(8,128)(2,1)S(1)}, bf16[256,576]{0,1:T(8,128)(2,1)}, u32[]{:S(2)}) copy-start(bf16[256,576]{0,1:T(8,128)(2,1)} %param.8) | copy-start | bytes 884740
  2.9 17.4 %copy-start.5 = (f32[4608]{0:T(1024)S(1)}, f32[4608]{0:T(1024)}, u32[]{:S(2)}) copy-start(f32[4608]{0:T(1024)} %param.10) | copy-start | bytes 55300
  2.9 17.4 %all-to-all-start = ((bf16[8,240,128]{2,1,0:T(8,128)(2,1)}), bf16[8,240,128]{2,1,0:T(8,128)(2,1)S(1)}, u32[]{:S(2)}, u32[]{:S(2)}) async-start(bf16[8,240,128]{2,1,0:T(8,128)(2,1)} %bitcast), calls=%async_computation | async-start | bytes 983040 | tf_op jit(solution)/shard_map/all_to_all | solution.py:288
  10.8 6.5 %collective-permute-start = (bf16[576,256]{1,0:T(8,128)(2,1)S(1)}, bf16[576,256]{1,0:T(8,128)(2,1)S(1)}, u32[]{:S(2)}, u32[]{:S(2)}) collective-permute-start(bf16[576,256]{1,0:T(8,128)(2,1)S(1)} %bitcast.25), channel_id=1, source_target_pairs={{0,8},{8,0},{1,9},{9,1},{2,10},{10,2},{3,11},{11,3},{4,12},{12,4},... | collective-permute-start | bytes 884744 | tf_op jit(solution)/shard_map/ppermute | solution.py:290
  15.4 3.5 %collective-permute-start.1 = (bf16[576,256]{1,0:T(8,128)(2,1)S(1)}, bf16[576,256]{1,0:T(8,128)(2,1)S(1)}, u32[]{:S(2)}, u32[]{:S(2)}) collective-permute-start(bf16[576,256]{1,0:T(8,128)(2,1)S(1)} %bitcast.19), channel_id=1, source_target_pairs={{0,8},{8,0},{1,9},{9,1},{2,10},{10,2},{3,11},{11,3},{4,12},{12,4},... | collective-permute-start | bytes 884744 | tf_op jit(solution)/shard_map/ppermute | solution.py:291
  21.9 0.7 copy-start.9
  22.5 4.4 %copy-start.10 = (bf16[128,512]{1,0:T(8,128)(2,1)S(1)}, bf16[128,512]{1,0:T(8,128)(2,1)}, u32[]{:S(2)}) copy-start(bf16[128,512]{1,0:T(8,128)(2,1)} %copy-done.9) | copy-start | bytes 393220
  22.5 11.0 %all-to-all-start.1 = ((bf16[4,112,512]{2,1,0:T(8,128)(2,1)}), bf16[4,112,512]{2,1,0:T(8,128)(2,1)S(1)}, u32[]{:S(2)}, u32[]{:S(2)}) async-start(bf16[4,112,512]{2,1,0:T(8,128)(2,1)} %bitcast.5), calls=%async_computation.1 | async-start | bytes 917504 | tf_op jit(solution)/shard_map/all_to_all | solution.py:298
  26.9 6.5 %collective-permute-start.2 = (bf16[128,512]{1,0:T(8,128)(2,1)S(1)}, bf16[128,512]{1,0:T(8,128)(2,1)S(1)}, u32[]{:S(2)}, u32[]{:S(2)}) collective-permute-start(bf16[128,512]{1,0:T(8,128)(2,1)S(1)} %copy-done.10), channel_id=1, source_target_pairs={{0,1},{1,0},{2,3},{3,2},{4,5},{5,4},{6,7},{7,6},{8,9},{9,8},{10,11... | collective-permute-start | bytes 393224 | tf_op jit(solution)/shard_map/ppermute | solution.py:297
  44.5 10.1 %copy-start.3 = (bf16[128,128]{1,0:T(8,128)(2,1)S(1)}, bf16[128,128]{1,0:T(8,128)(2,1)}, u32[]{:S(2)}) copy-start(bf16[128,128]{1,0:T(8,128)(2,1)} %constant.2.clone.table_ref) | copy-start | bytes 98308
  44.5 10.1 %copy-start.4 = (s32[4608]{0:T(1024)S(1)}, s32[4608]{0:T(1024)}, u32[]{:S(2)}) copy-start(s32[4608]{0:T(1024)} %param.12) | copy-start | bytes 55300
  54.5 0.7 copy-start.6
  58.6 0.7 copy-start.7
  59.3 15.5 %copy-start.8 = (bf16[576,256]{1,0:T(8,128)(2,1)S(1)}, bf16[576,256]{1,0:T(8,128)(2,1)}, u32[]{:S(2)}) copy-start(bf16[576,256]{1,0:T(8,128)(2,1)} %copy-done.7) | copy-start | bytes 884740
  59.3 28.8 %all-to-all-start.3 = ((bf16[32,64,128]{2,1,0:T(8,128)(2,1)}), bf16[32,64,128]{2,1,0:T(8,128)(2,1)S(1)}, u32[]{:S(2)}, u32[]{:S(2)}) async-start(bf16[32,64,128]{2,1,0:T(8,128)(2,1)} %get-tuple-element.29), calls=%async_computation.3 | async-start | bytes 1048576 | tf_op jit(solution)/shard_map/all_to_all | solution.py:309
  74.8 8.8 %collective-permute-start.3 = (bf16[576,256]{1,0:T(8,128)(2,1)S(1)}, bf16[576,256]{1,0:T(8,128)(2,1)S(1)}, u32[]{:S(2)}, u32[]{:S(2)}) collective-permute-start(bf16[576,256]{1,0:T(8,128)(2,1)S(1)} %copy-done.8), channel_id=1, source_target_pairs={{0,8},{8,0},{1,9},{9,1},{2,10},{10,2},{3,11},{11,3},{4,12},{12,4},... | collective-permute-start | bytes 884744 | tf_op jit(solution)/shard_map/ppermute | solution.py:310
  115.1 10.4 %collective-permute-start.4 = (bf16[32,64,128]{2,1,0:T(8,128)(2,1)S(1)}, bf16[32,64,128]{2,1,0:T(8,128)(2,1)S(1)}, u32[]{:S(2)}, u32[]{:S(2)}) collective-permute-start(bf16[32,64,128]{2,1,0:T(8,128)(2,1)S(1)} %bitcast.14), channel_id=1, source_target_pairs={{0,8},{8,0},{1,9},{9,1},{2,10},{10,2},{3,11},{11,3},{4,12},{12,4},... | collective-permute-start | bytes 1572872 | tf_op jit(solution)/shard_map/ppermute | solution.py:315

commit v4 on v3

v4 whole, which is shorter than its diff:
```python
import functools

import jax
import jax.numpy as jnp
import numpy as np
from jax import lax
from jax.experimental import pallas as pl
from jax.experimental.pallas import tpu as pltpu
from jax.sharding import Mesh
from jax.sharding import PartitionSpec as P

F32 = jnp.float32
BF16 = jnp.bfloat16
AXES = ("z", "yl", "c", "yh", "x")
DP = ("z", "yl", "c")
MP = ("yh", "x")
VMEM_LIMIT = 20 * 1024 * 1024
FEATURES = 4608
CONTRACT_LAST = (((1,), (1,)), ((), ()))
CONTRACT_FIRST = (((0,), (0,)), ((), ()))


def signed_hadamard():
    table = np.array([[1.0]], np.float32)
    for _ in range(7):
        table = np.block([[table, table], [table, -table]])
    return table


def gelu_parts(values):
    tanh_input = 0.7978845608 * (values + 0.044715 * values * values * values)
    tanhed = jnp.tanh(tanh_input)
    forward = 0.5 * values * (1.0 + tanhed)
    gelu_slope = 0.5 * (1.0 + tanhed) + 0.5 * values * (1.0 - tanhed * tanhed) * 0.7978845608 * (
        1.0 + 3.0 * 0.044715 * values * values
    )
    return (forward, gelu_slope)


def pieces(values):
    high = values.astype(BF16)
    rest = values - high.astype(F32)
    middle = rest.astype(BF16)
    low = (rest - middle.astype(F32)).astype(BF16)
    return (high, middle, low)


def dot(left, right, dims=(((1,), (0,)), ((), ()))):
    return lax.dot_general(left, right, dims, preferred_element_type=F32)


def places():
    odd = lax.axis_index("x") % 2
    pair = lax.axis_index("yh") * 2 + lax.axis_index("x") // 2
    return (lax.axis_index("c"), odd, pair * 9)


def local_rows(table_ref, first, odd):
    return [table_ref[pl.ds(first + 5 * odd + b, 1), :] for b in range(4)] + [table_ref[pl.ds(first + 4, 1), :]]


def own_rows(odd):
    return (
        pl.ds(pl.multiple_of(odd * 64, 64), 512),
        pl.ds(pl.multiple_of((1 - odd) * 512, 64), 64),
    )


def prepare_kernel(w_ref, send_ref):
    core, _, _ = places()
    rows = pl.ds(pl.multiple_of(core * 16, 16), 16)
    for m in range(8):
        start = 9 * (m // 2)
        for b, block in enumerate([start + 5 * (m % 2) + b for b in range(4)] + [start + 4]):
            for k in range(3):
                send_ref[m, b, k] = w_ref[k, rows, block * 128 : (block + 1) * 128]


def align_kernel(x_ref, g_ref, far_x_ref, far_g_ref, exps_ref, xa_ref, ga_ref, half_ref, tail_ref, scale_ref):
    place = lax.broadcasted_iota(jnp.int32, (8, 128), 0)
    scales = jnp.zeros((8, 128), F32)
    for k in range(3):
        e = exps_ref[k]
        up = jnp.where(e == 3, 8.0, jnp.where(e == 4, 16.0, jnp.where(e == 5, 32.0, 64.0)))
        down = jnp.where(e == 3, 2.0**-9, jnp.where(e == 4, 2.0**-10, jnp.where(e == 5, 2.0**-11, 2.0**-12)))
        scales = jnp.where(place == k, up, jnp.where(place == 3 + k, down, scales))
    scale_ref[...] = scales * float(128.0**-0.5)
    _, odd, _ = places()
    main, half = own_rows(odd)
    mine = pl.ds(pl.multiple_of(512 + odd * 64, 64), 64)
    theirs = pl.ds(pl.multiple_of(576 - odd * 64, 64), 64)
    for part, (to_ref, refs) in enumerate(((xa_ref, (x_ref, far_x_ref)), (ga_ref, (g_ref, far_g_ref)))):
        for side, ref in enumerate(refs):
            tokens = pl.ds(side * 256, 256)
            to_ref[0:512, tokens] = ref[main, :]
            to_ref[mine, tokens] = ref[half, :]
            to_ref[theirs, tokens] = jnp.zeros((64, 256), BF16)
            half_ref[pl.ds(64 * part, 64), tokens] = ref[half, :]
    wide = xa_ref[...].astype(F32)
    tail_ref[...] = stacked_pieces(jnp.sum(wide * wide, axis=0, keepdims=True))


def forward_kernel(recv_ref, xa_ref, ga_ref, tail_ref, gain_ref, part_ref, w_ref):
    _, odd, first = places()
    for j in range(8):
        for b in range(5):
            for k in range(3):
                w_ref[k * 128 + j * 16 : k * 128 + j * 16 + 16, b * 128 : (b + 1) * 128] = recv_ref[j, b, k]
    gained = w_ref[0:256].astype(F32) * jnp.concatenate(local_rows(gain_ref, first, odd), axis=1)
    high = gained.astype(BF16)
    low = (gained - high.astype(F32)).astype(BF16)
    gate_up = (dot(low, xa_ref[...]) + dot(high, xa_ref[...])).astype(BF16)
    down = dot(w_ref[256:384], ga_ref[...]).astype(BF16)
    tail = tail_ref[...]
    for j in range(8):
        x, yh = j % 4, j // 4
        part_ref[x, yh, 0:16, :] = gate_up[j * 16 : j * 16 + 16]
        part_ref[x, yh, 16:32, :] = gate_up[128 + j * 16 : 128 + j * 16 + 16]
        part_ref[x, yh, 32:48, :] = down[j * 16 : j * 16 + 16]
        part_ref[x, yh, 48:56, :] = tail


def stacked_pieces(row):
    place = lax.broadcasted_iota(jnp.int32, (8, 512), 0)
    tail = jnp.zeros((8, 512), F32)
    for i, piece in enumerate(pieces(row)):
        tail = jnp.where(place == i, piece.astype(F32), tail)
    return tail.astype(BF16)


def sum_kernel(parts_ref, _, out_ref, own_ref):
    for yh in range(2):
        total = parts_ref[0, yh].astype(F32)
        for i in range(1, 4):
            total = total + parts_ref[i, yh].astype(F32)
        own_ref[yh] = total[0:48]
        out_ref[yh, 0:48, :] = total[0:48].astype(BF16)
        out_ref[yh, 48:56, :] = stacked_pieces(total[48:49] + total[49:50] + total[50:51])


def activation_kernel(parts_ref, own_ref, out_ref, inv_ref):
    high = lax.axis_index("yh") == 1
    for yh in range(2):
        others = [parts_ref[i, yh, 0:48, :].astype(F32) for i in range(2)]
        total = own_ref[yh] + jnp.where(high, others[0], others[1])
        tails = parts_ref[0, yh, 48:56, :].astype(F32) + parts_ref[1, yh, 48:56, :].astype(F32)
        sums = tails[0:1] + tails[1:2] + tails[2:3]
        inverse = lax.rsqrt(sums / FEATURES + 1e-06)
        inv_ref[...] = jnp.broadcast_to(inverse, (8, 512))
        gate_pre, up_proj, hidden_grad = total[0:16] * inverse, total[16:32] * inverse, total[32:48]
        activated, slope = gelu_parts(gate_pre)
        hidden = (activated * up_proj).astype(BF16)
        gate_grad = (hidden_grad * up_proj * slope).astype(BF16)
        up_grad = (hidden_grad * activated).astype(BF16)
        products = gate_grad.astype(F32) * gate_pre + up_grad.astype(F32) * up_proj
        tail = stacked_pieces(jnp.sum(products, axis=0, keepdims=True) / FEATURES)
        for i in range(4):
            out_ref[i, yh, 0:16, :] = gate_grad
            out_ref[i, yh, 16:32, :] = up_grad
            out_ref[i, yh, 32:48, :] = hidden
            out_ref[i, yh, 48:56, :] = tail


def feature_column(table_ref, first, odd):
    diagonal = lax.broadcasted_iota(jnp.int32, (128, 128), 0) == lax.broadcasted_iota(jnp.int32, (128, 128), 1)
    rows = local_rows(table_ref, first, odd)
    return jnp.concatenate(
        [jnp.sum(jnp.where(diagonal, row.astype(F32), 0.0), axis=1, keepdims=True) for row in rows], axis=0
    )


def gathered_acts(acts_ref, k):
    return jnp.concatenate([acts_ref[j % 4, j // 4, k * 16 : k * 16 + 16, :] for j in range(8)], axis=0)


def gradient_kernel(
    acts_ref, xa_ref, ga_ref, half_ref, inv_ref, gain_ref, sign_ref, table_ref, scale_ref, term_ref
):
    _, odd, first_block = places()
    table = table_ref[...]
    sign = 2.0 * feature_column(sign_ref, first_block, odd) - 1.0
    gain = feature_column(gain_ref, first_block, odd) * sign
    theirs = (lax.broadcasted_iota(jnp.int32, (128, 512), 0) >= 64) == (odd == 0)
    rights = []
    for part, (ref, factor) in enumerate(((xa_ref, inv_ref[0:1, :]), (ga_ref, None))):
        other = half_ref[part * 64 : part * 64 + 64, :].astype(F32)
        shared = jnp.where(theirs, jnp.concatenate([other, other], axis=0), ref[512:640, :].astype(F32))
        values = jnp.concatenate([ref[0:512, :].astype(F32), shared], axis=0)
        rights.append((values * sign if factor is None else values * factor * gain).astype(BF16))
    rights = (rights[0], rights[0], rights[1])
    for k in range(3):
        acts = gathered_acts(acts_ref, k)
        scale = scale_ref[k : k + 1, 0:1]
        terms = jnp.concatenate(
            [
                dot(acts[:, s * 256 : s * 256 + 256], rights[k][:, s * 256 : s * 256 + 256], CONTRACT_LAST)
                for s in range(2)
            ],
            axis=0,
        )
        for first in (0, 256, 512):
            width = min(256, 640 - first)
            block = terms[:, first : first + width]
            high = block.astype(BF16)
            low = (block - high.astype(F32)).astype(BF16)
            part = table[0:width, 0:width]
            rotated = dot(low, part) + dot(high, part)
            quantized = jnp.clip(rotated * scale, -127.0, 127.0).astype(BF16).astype(F32)
            total = quantized[0:128] + quantized[128:256]
            for b in range(first // 128, (first + width) // 128):
                half = total[:, b * 128 - first : b * 128 - first + 128].reshape(8, 2, 8, 128)
                if b < 4:
                    term_ref[k * 8 + b] = half[:, 0].reshape(64, 128).astype(BF16)
                    term_ref[k * 8 + 4 + b] = half[:, 1].reshape(64, 128).astype(BF16)
                else:
                    chosen = jnp.where(odd == 1, half[:, 1], half[:, 0])
                    term_ref[24 + k] = chosen.reshape(64, 128).astype(BF16)
    for s in range(27, 32):
        term_ref[s] = jnp.zeros((64, 128), BF16)


def resid_kernel(acts_ref, w_ref, xa_ref, inv_ref, gain_ref, _, near_ref, far_ref):
    _, odd, first = places()
    gain = feature_column(gain_ref, first, odd)
    inverse = inv_ref[0:1, :]
    tails = acts_ref[0, 0, 48:56, :].astype(F32)
    for j in range(1, 8):
        tails = tails + acts_ref[j % 4, j // 4, 48:56, :].astype(F32)
    row_mean = tails[0:1] + tails[1:2] + tails[2:3]
    pair = jnp.concatenate([gathered_acts(acts_ref, k) for k in range(2)], axis=0)
    normed_grad = dot(w_ref[0:256], pair, CONTRACT_FIRST)
    unit = xa_ref[...].astype(F32) * inverse
    resid = inverse * (normed_grad * gain - unit * row_mean)
    main, half = own_rows(odd)
    shared_half = jnp.where(odd == 1, resid[576:640], resid[512:576])
    near_ref[main, :] = resid[0:512, 0:256]
    near_ref[half, :] = shared_half[:, 0:256]
    far_ref[main, :] = resid[0:512, 256:512].astype(BF16)
    far_ref[half, :] = shared_half[:, 256:512].astype(BF16)


def finish_kernel(g_ref, near_ref, far_ref, out_ref, done_ref):
    out_ref[...] = (g_ref[...].astype(F32) + (near_ref[...] + far_ref[...].astype(F32))).astype(BF16)
    done_ref[...] = jnp.zeros((8, 128), F32)


def total_kernel(terms_ref, _, share_ref):
    totals = []
    for yh in range(2):
        total = terms_ref[yh].astype(F32)
        for i in range(1, 32):
            total = total + terms_ref[2 * i + yh].astype(F32)
        totals.append(total)
    for x in range(4):
        both = jnp.concatenate([total[x * 8 : x * 8 + 8] for total in totals], axis=0).astype(BF16)
        for i in range(32):
            share_ref[i * 4 + x] = both


def received_rows(m):
    start = 8 * (2 * (m % 4) + m // 4)
    return slice(start, start + 8)


def restore_half(q, share_ref, sign_ref, table_ref, scale_ref, out_ref, held, sems):
    table = table_ref[0:128, 0:128]
    copies = []
    for k in range(3):
        factor = scale_ref[3 + k : 4 + k, :]

        def put(block, low_half, high_half):
            sign = (2 * sign_ref[block : block + 1, :] - 1).astype(F32) * factor
            both = jnp.concatenate([low_half, high_half], axis=0) * sign
            held[k, :, block * 128 : (block + 1) * 128] = both.astype(BF16)

        for b in range(4):
            halves = [dot(share_ref[k * 8 + 4 * i + b], table) for i in range(2)]
            for m in range(8):
                rows = received_rows(m)
                put(9 * (m // 2) + 5 * (m % 2) + b, halves[0][rows], halves[1][rows])
        shared = dot(share_ref[24 + k], table)
        for p in range(4):
            put(9 * p + 4, shared[received_rows(2 * p)], shared[received_rows(2 * p + 1)])
        rows = pl.ds(pl.multiple_of(16 * q, 16), 16)
        copy = pltpu.make_async_copy(held.at[k], out_ref.at[k, rows, :], sems.at[k])
        copy.start()
        copies.append(copy)
    for copy in copies:
        copy.wait()


def near_restore_kernel(share_ref, sign_ref, table_ref, scale_ref, out_ref, held, sems):
    restore_half(lax.axis_index("c"), share_ref, sign_ref, table_ref, scale_ref, out_ref, held, sems)


def far_restore_kernel(share_ref, sign_ref, table_ref, scale_ref, _, out_ref, held, sems):
    restore_half(1 - lax.axis_index("c"), share_ref, sign_ref, table_ref, scale_ref, out_ref, held, sems)


def call(kernel, outs, scalars=0, scratch=(), anywhere=(), out_space=pltpu.VMEM, aliases=None, limit=VMEM_LIMIT):
    def run(*operands):
        count = len(operands)
        spaces = [
            pltpu.SMEM if i >= count - scalars else pl.ANY if i in anywhere else pltpu.VMEM for i in range(count)
        ]
        return pl.pallas_call(
            kernel,
            out_shape=[jax.ShapeDtypeStruct(shape, dtype) for shape, dtype in outs],
            in_specs=[pl.BlockSpec(memory_space=place) for place in spaces],
            out_specs=[pl.BlockSpec(memory_space=out_space) for _ in outs],
            scratch_shapes=list(scratch),
            input_output_aliases=aliases or {},
            compiler_params=pltpu.CompilerParams(vmem_limit_bytes=limit),
            cost_estimate=pl.CostEstimate(flops=10**9, bytes_accessed=10**6, transcendentals=0),
            name=kernel.__name__,
        )(*operands)

    return run


def per_device(residual, out_grad, ffn_weights, norm_gain, exponents, sign_bits):
    gain = norm_gain.reshape(36, 128)
    signs = sign_bits.reshape(36, 128)
    table = jnp.asarray(np.kron(np.eye(2), signed_hadamard()), BF16)
    cores = [(0, 1), (1, 0)]
    x_cols, g_cols = residual.T, out_grad.T
    rows = ((640, 512), BF16)

    (send,) = call(prepare_kernel, [((8, 5, 3, 16, 128), BF16)])(ffn_weights)
    received = lax.all_to_all(send.reshape(8, 240, 128), AXES, 0, 0, axis_index_groups=near_groups())
    near_x, near_g, _ = lax.optimization_barrier((x_cols, g_cols, send))
    far_x = lax.ppermute(near_x, "c", cores)
    far_g = lax.ppermute(near_g, "c", cores)
    xa, ga, half, tail, scales = call(
        align_kernel, [rows, rows, ((128, 512), BF16), ((8, 512), BF16), ((8, 128), F32)], scalars=1
    )(x_cols, g_cols, far_x, far_g, exponents)
    parts, weights = call(forward_kernel, [((4, 2, 56, 512), BF16), ((384, 640), BF16)])(
        received.reshape(8, 5, 3, 16, 128), xa, ga, tail, gain
    )

    other_half = lax.ppermute(half, "x", [(0, 1), (1, 0), (2, 3), (3, 2)])
    parts = lax.all_to_all(parts.reshape(4, 112, 512), "x", 0, 0).reshape(4, 2, 56, 512)
    sums, own = call(sum_kernel, [((2, 56, 512), BF16), ((2, 48, 512), F32)], anywhere=(1,))(parts, other_half)
    sums = lax.all_gather(sums, "yh", axis=0)
    message, inverse = call(activation_kernel, [((4, 2, 56, 512), BF16), ((8, 512), F32)])(sums, own)
    acts = lax.all_to_all(message.reshape(4, 112, 512), "x", 0, 0).reshape(4, 2, 56, 512)
    (terms,) = call(gradient_kernel, [((32, 64, 128), BF16)])(
        acts, xa, ga, other_half, inverse, gain, signs, table, scales
    )

    summands = lax.all_to_all(terms.reshape(64, 32, 128), ("z", "yl", "yh"), 0, 0)
    near_resid, far_resid = call(resid_kernel, [((576, 256), F32), ((576, 256), BF16)], anywhere=(5,))(
        acts, weights, xa, inverse, gain, terms
    )
    far_resid = lax.ppermute(far_resid, "c", cores)
    resid_cols, done = call(finish_kernel, [((576, 256), BF16), ((8, 128), F32)])(g_cols, near_resid, far_resid)
    (share,) = call(total_kernel, [((128, 16, 128), BF16)])(summands, done)
    share = lax.all_to_all(share, ("z", "yl", "x"), 0, 0).reshape(32, 64, 128)
    other = lax.ppermute(share, "c", cores)
    scratch = [pltpu.VMEM((3, 16, 4608), BF16), pltpu.SemaphoreType.DMA((3,))]
    out = [((3, 32, 4608), BF16)]
    (half_done,) = call(near_restore_kernel, out, scratch=scratch, out_space=pl.ANY)(share, signs, table, scales)
    (weight_grads,) = call(
        far_restore_kernel, out, scratch=scratch, anywhere=(4,), out_space=pl.ANY, aliases={4: 0}
    )(other, signs, table, scales, half_done)
    return (resid_cols.T, weight_grads)


def near_groups():
    def flat(z, yl, c, yh, x):
        return (((z * 4 + yl) * 2 + c) * 2 + yh) * 4 + x

    return [
        [flat(z, 3 - yl if yh else yl, c, yh, x) for yh in range(2) for x in range(4)]
        for z in range(8)
        for yl in range(4)
        for c in range(2)
    ]


def solution(mesh):
    fine = Mesh(mesh.devices.reshape(8, 4, 2, 2, 4), AXES)
    rows = P(DP, MP)
    return jax.shard_map(
        per_device,
        mesh=fine,
        in_specs=(rows, rows, P(None, MP, None), P(), P(), P()),
        out_specs=(rows, P(None, MP, None)),
        check_vma=False,
    )
```

time: 128 us -> 123 us (0.961)
  blocking collectives: 46.9 us -> 43.6 us
  waiting for transfers between devices: 13.6 us -> 11.5 us
  local copies, waits for them, and re-layouts: 3.22 us -> 1.19 us
  starting transfers between devices: 53.9 us -> 55.7 us
    all_to_all x1, blocking collectives: 26.1 us -> 22.7 us  [per_device(): share = lax.all_to_all(share, ('z', 'yl', 'x'), 0, 0).reshape(32, 64, 128)]
    unnamed x22 -> x14, local copies, waits for them, and re-layouts: 3.22 us -> 1.19 us
    pallas_call x7 -> x11, Pallas kernels: 9.13 us -> 9.27 us  [run(): pl.pallas_call(kernel, out_shape=[jax.ShapeDtypeStruct(shape, dtype) for...]
  transfers between devices with their start and end apart: 8 -> 8, of which waited for: 7 -> 7; matrix products, arithmetic and copies ran while one was open for 0% -> 0% of each run, Pallas kernels for 0% -> 3%
where the time goes in v4:
time: 123 us; the launch traced here: 122 us
  starting transfers between devices  55.7 us (45%)
  blocking collectives  43.6 us (35%)
  waiting for transfers between devices  11.5 us (9%)
  Pallas kernels  9.27 us (8%)
    all_to_all x1, blocking collectives, per_device(): share = lax.all_to_all(share, ('z', 'yl', 'x'), 0, 0).reshape(32, 64, 128)  22.7 us
    all_to_all x1, starting transfers between devices, per_device(): lax.all_to_all(terms.reshape(64, 32, 128), ('z', 'yl', 'yh'), 0, 0)  16.3 us
    all_gather x1, blocking collectives, per_device(): sums = lax.all_gather(sums, 'yh', axis=0)  10.8 us
    all_to_all x1, blocking collectives, per_device(): lax.all_to_all(message.reshape(4, 112, 512), 'x', 0, 0)  10.2 us
    pallas_call x11, Pallas kernels, run(): pl.pallas_call(kernel, out_shape=[jax.ShapeDtypeStruct(shape, dtype) for...  9.27 us
    ppermute x1, starting transfers between devices, per_device(): far_resid = lax.ppermute(far_resid, 'c', cores)  8.8 us
    ppermute x1, starting transfers between devices, per_device(): other = lax.ppermute(share, 'c', cores)  8.68 us
    all_to_all x1, starting transfers between devices, per_device(): lax.all_to_all(send.reshape(8, 240, 128), AXES, 0, 0, axis_index_groups=n...  7.89 us
  transfers between devices with their start and end apart: 8, of which 7 were waited for; matrix products, arithmetic and copies ran while one was open for 0% of the time, Pallas kernels for 3%

profile of v4, /device:TPU:1, one launch (start us, length us, event | category | flops | bytes accessed | tf_op | source)
XLA Modules:
  0.0 122.1 jit_solution(788947726575184441)
XLA Ops:
  0.6 1.2 copy-done
  1.8 0.9 prepare_kernel.1
  2.7 7.9 %all-to-all-start = ((bf16[8,240,128]{2,1,0:T(8,128)(2,1)}), bf16[8,240,128]{2,1,0:T(8,128)(2,1)S(1)}, u32[]{:S(2)}, u32[]{:S(2)}) async-start(bf16[8,240,128]{2,1,0:T(8,128)(2,1)} %bitcast.1), calls=%async_computation | async-start | bytes 983040 | tf_op jit(solution)/shard_map/all_to_all | solution.py:330
  10.6 4.5 %collective-permute-start = (bf16[576,256]{1,0:T(8,128)(2,1)S(1)}, bf16[576,256]{1,0:T(8,128)(2,1)S(1)}, u32[]{:S(2)}, u32[]{:S(2)}) collective-permute-start(bf16[576,256]{1,0:T(8,128)(2,1)S(1)} %bitcast.22), channel_id=1, source_target_pairs={{0,8},{8,0},{1,9},{9,1},{2,10},{10,2},{3,11},{11,3},{4,12},{12,4},... | collective-permute-start | bytes 884744 | tf_op jit(solution)/shard_map/ppermute | solution.py:332
  15.1 1.9 %collective-permute-start.1 = (bf16[576,256]{1,0:T(8,128)(2,1)S(1)}, bf16[576,256]{1,0:T(8,128)(2,1)S(1)}, u32[]{:S(2)}, u32[]{:S(2)}) collective-permute-start(bf16[576,256]{1,0:T(8,128)(2,1)S(1)} %bitcast.24), channel_id=1, source_target_pairs={{0,8},{8,0},{1,9},{9,1},{2,10},{10,2},{3,11},{11,3},{4,12},{12,4},... | collective-permute-start | bytes 884744 | tf_op jit(solution)/shard_map/ppermute | solution.py:333
  17.1 1.5 %collective-permute-done.1.far_g_ref = bf16[576,256]{1,0:T(8,128)(2,1)S(1)} collective-permute-done((bf16[576,256]{1,0:T(8,128)(2,1)S(1)}, bf16[576,256]{1,0:T(8,128)(2,1)S(1)}, u32[]{:S(2)}, u32[]{:S(2)}) %collective-permute-start.1) | collective-permute-done | bytes 294944 | tf_op jit(solution)/shard_map/ppermute | solution.py:333
  18.6 0.7 align_kernel.1
  19.3 0.8 all-to-all-done
  20.1 1.5 %forward_kernel.1 = (bf16[4,2,56,512]{3,2,1,0:T(8,128)(2,1)}, bf16[384,640]{1,0:T(8,128)(2,1)S(1)}) custom-call(bf16[8,5,3,16,128]{4,3,2,1,0:T(8,128)(2,1)S(1)} %bitcast.16, bf16[640,512]{1,0:T(8,128)(2,1)S(1)} %get-tuple-element.21.xa_ref, bf16[640,512]{1,0:T(8,128)(2,1)S(1)} %get-tuple-element.22.ga_ref, bf16[8,512]{1,0:T(8,128)(2,1)S(1)} %get-tuple-element.23.tail_ref, ...), custom_call_target="tpu_custom_call" | custom-call | flops 1000000000 | bytes 1000000 | tf_op jit(solution)/shard_map/forward_kernel/pallas_call | solution.py:306
  21.5 4.2 %all-to-all-start.1 = ((bf16[4,112,512]{2,1,0:T(8,128)(2,1)}), bf16[4,112,512]{2,1,0:T(8,128)(2,1)S(1)}, u32[]{:S(2)}, u32[]{:S(2)}) async-start(bf16[4,112,512]{2,1,0:T(8,128)(2,1)} %bitcast.5), calls=%async_computation.1 | async-start | bytes 917504 | tf_op jit(solution)/shard_map/all_to_all | solution.py:342
  25.8 3.4 %collective-permute-start.2 = (bf16[128,512]{1,0:T(8,128)(2,1)S(1)}, bf16[128,512]{1,0:T(8,128)(2,1)S(1)}, u32[]{:S(2)}, u32[]{:S(2)}) collective-permute-start(bf16[128,512]{1,0:T(8,128)(2,1)S(1)} %get-tuple-element.25), channel_id=1, source_target_pairs={{0,1},{1,0},{2,3},{3,2},{4,5},{5,4},{6,7},{7,6},{8,9},{9,8},{10,11... | collective-permute-start | bytes 393224 | tf_op jit(solution)/shard_map/ppermute | solution.py:341
  29.1 3.1 %collective-permute-done.2._.half_ref = bf16[128,512]{1,0:T(8,128)(2,1)S(1)} collective-permute-done((bf16[128,512]{1,0:T(8,128)(2,1)S(1)}, bf16[128,512]{1,0:T(8,128)(2,1)S(1)}, u32[]{:S(2)}, u32[]{:S(2)}) %collective-permute-start.2) | collective-permute-done | bytes 131104 | tf_op jit(solution)/shard_map/ppermute | solution.py:341
  32.2 0.1 all-to-all-done.1
  32.3 0.1 sum_kernel.1
  32.4 10.8 %all-gather = bf16[4,56,512]{2,1,0:T(8,128)(2,1)S(1)} all-gather(bf16[2,56,512]{2,1,0:T(8,128)(2,1)S(1)} %get-tuple-element.26), channel_id=2, replica_groups=mesh['z'=8,'yl'=4,'c'=2,'yh'=2,'x'=4] {'yh'}, dimensions={0}, use_global_device_ids=true | all-gather | bytes 344064 | tf_op jit(solution)/shard_map/all_gather | solution.py:344
  43.2 0.1 activation_kernel.1
  43.3 0.0 copy-start.4
  43.4 0.0 copy-start.6
  43.4 10.2 %all_to_all.25 = bf16[4,112,512]{2,1,0:T(8,128)(2,1)S(1)} all-to-all(bf16[4,112,512]{2,1,0:T(8,128)(2,1)S(1)} %bitcast.20), channel_id=1, replica_groups=mesh['z'=8,'yl'=4,'c'=2,'yh'=2,'x'=4] {'x'}, dimensions={0} | all-to-all | bytes 917504 | tf_op jit(solution)/shard_map/all_to_all | solution.py:346
  53.6 2.4 %gradient_kernel.1._ = bf16[32,64,128]{2,1,0:T(8,128)(2,1)} custom-call(bf16[4,2,56,512]{3,2,1,0:T(8,128)(2,1)S(1)} %bitcast.18, bf16[640,512]{1,0:T(8,128)(2,1)S(1)} %get-tuple-element.21.xa_ref, bf16[640,512]{1,0:T(8,128)(2,1)S(1)} %get-tuple-element.22.ga_ref, bf16[128,512]{1,0:T(8,128)(2,1)S(1)} %collective-permute-done.2._.half_ref, ...), custom_call_target="tpu_custom_call" | custom-call | flops 1000000000 | bytes 1000000 | tf_op jit(solution)/shard_map/gradient_kernel/pallas_call | solution.py:306
  56.0 16.3 %all-to-all-start.3 = ((bf16[64,32,128]{2,1,0:T(8,128)(2,1)}), bf16[64,32,128]{2,1,0:T(8,128)(2,1)S(1)}, u32[]{:S(2)}, u32[]{:S(2)}) async-start(bf16[64,32,128]{2,1,0:T(8,128)(2,1)} %bitcast.12), calls=%async_computation.3 | async-start | bytes 1048576 | tf_op jit(solution)/shard_map/all_to_all | solution.py:351
  72.3 0.5 resid_kernel.1
  72.8 8.8 %collective-permute-start.3 = (bf16[576,256]{1,0:T(8,128)(2,1)S(1)}, bf16[576,256]{1,0:T(8,128)(2,1)S(1)}, u32[]{:S(2)}, u32[]{:S(2)}) collective-permute-start(bf16[576,256]{1,0:T(8,128)(2,1)S(1)} %get-tuple-element.33), channel_id=1, source_target_pairs={{0,8},{8,0},{1,9},{9,1},{2,10},{10,2},{3,11},{11,3},{4,12},{12,4},... | collective-permute-start | bytes 884744 | tf_op jit(solution)/shard_map/ppermute | solution.py:355
  81.6 1.2 collective-permute-done.3.far_ref
  82.8 0.8 finish_kernel.1
  83.6 4.4 %all-to-all-done.3.terms_ref = bf16[64,32,128]{2,1,0:T(8,128)(2,1)S(1)} async-done(((bf16[64,32,128]{2,1,0:T(8,128)(2,1)}), bf16[64,32,128]{2,1,0:T(8,128)(2,1)S(1)}, u32[]{:S(2)}, u32[]{:S(2)}) %all-to-all-start.3) | async-done | bytes 524320 | tf_op jit(solution)/shard_map/all_to_all | solution.py:351
  88.0 0.1 total_kernel.1
  88.1 22.7 %all_to_all.26 = bf16[128,16,128]{2,1,0:T(8,128)(2,1)S(1)} all-to-all(bf16[128,16,128]{2,1,0:T(8,128)(2,1)S(1)} %total_kernel.1), channel_id=1, replica_groups=mesh['z'=8,'yl'=4,'c'=2,'yh'=2,'x'=4] {'z','yl','x'}, dimensions={0} | all-to-all | bytes 1048576 | tf_op jit(solution)/shard_map/all_to_all | solution.py:358
  110.8 8.7 %collective-permute-start.4 = (bf16[32,64,128]{2,1,0:T(8,128)(2,1)S(1)}, bf16[32,64,128]{2,1,0:T(8,128)(2,1)S(1)}, u32[]{:S(2)}, u32[]{:S(2)}) collective-permute-start(bf16[32,64,128]{2,1,0:T(8,128)(2,1)S(1)} %bitcast.14), channel_id=1, source_target_pairs={{0,8},{8,0},{1,9},{9,1},{2,10},{10,2},{3,11},{11,3},{4,12},{12,4},... | collective-permute-start | bytes 1572872 | tf_op jit(solution)/shard_map/ppermute | solution.py:359
  119.5 1.1 near_restore_kernel.1._
  120.5 0.4 collective-permute-done.4.share_ref
  121.0 1.1 far_restore_kernel.1
  (12 shorter events, 0.0 us)
Async XLA Ops:
  0.6 1.2 copy-start
  2.7 7.9 %copy-start.1 = (bf16[256,576]{0,1:T(8,128)(2,1)S(1)}, bf16[256,576]{0,1:T(8,128)(2,1)}, u32[]{:S(2)}) copy-start(bf16[256,576]{0,1:T(8,128)(2,1)} %param.7) | copy-start | bytes 884740
  2.7 12.5 %copy-start.2 = (bf16[256,576]{0,1:T(8,128)(2,1)S(1)}, bf16[256,576]{0,1:T(8,128)(2,1)}, u32[]{:S(2)}) copy-start(bf16[256,576]{0,1:T(8,128)(2,1)} %param.8) | copy-start | bytes 884740
  2.7 17.4 %all-to-all-start = ((bf16[8,240,128]{2,1,0:T(8,128)(2,1)}), bf16[8,240,128]{2,1,0:T(8,128)(2,1)S(1)}, u32[]{:S(2)}, u32[]{:S(2)}) async-start(bf16[8,240,128]{2,1,0:T(8,128)(2,1)} %bitcast.1), calls=%async_computation | async-start | bytes 983040 | tf_op jit(solution)/shard_map/all_to_all | solution.py:330
  10.5 8.1 %copy-start.5 = (s32[3]{0:T(128)S(1)}, s32[3]{0:T(128)}, u32[]{:S(2)}) copy-start(s32[3]{0:T(128)} %exps_ref.1) | copy-start | bytes 40
  10.6 9.5 %copy-start.3 = (f32[4608]{0:T(1024)S(1)}, f32[4608]{0:T(1024)}, u32[]{:S(2)}) copy-start(f32[4608]{0:T(1024)} %param.10) | copy-start | bytes 55300
  10.6 6.5 %collective-permute-start = (bf16[576,256]{1,0:T(8,128)(2,1)S(1)}, bf16[576,256]{1,0:T(8,128)(2,1)S(1)}, u32[]{:S(2)}, u32[]{:S(2)}) collective-permute-start(bf16[576,256]{1,0:T(8,128)(2,1)S(1)} %bitcast.22), channel_id=1, source_target_pairs={{0,8},{8,0},{1,9},{9,1},{2,10},{10,2},{3,11},{11,3},{4,12},{12,4},... | collective-permute-start | bytes 884744 | tf_op jit(solution)/shard_map/ppermute | solution.py:332
  15.1 3.5 %collective-permute-start.1 = (bf16[576,256]{1,0:T(8,128)(2,1)S(1)}, bf16[576,256]{1,0:T(8,128)(2,1)S(1)}, u32[]{:S(2)}, u32[]{:S(2)}) collective-permute-start(bf16[576,256]{1,0:T(8,128)(2,1)S(1)} %bitcast.24), channel_id=1, source_target_pairs={{0,8},{8,0},{1,9},{9,1},{2,10},{10,2},{3,11},{11,3},{4,12},{12,4},... | collective-permute-start | bytes 884744 | tf_op jit(solution)/shard_map/ppermute | solution.py:333
  21.5 10.8 %all-to-all-start.1 = ((bf16[4,112,512]{2,1,0:T(8,128)(2,1)}), bf16[4,112,512]{2,1,0:T(8,128)(2,1)S(1)}, u32[]{:S(2)}, u32[]{:S(2)}) async-start(bf16[4,112,512]{2,1,0:T(8,128)(2,1)} %bitcast.5), calls=%async_computation.1 | async-start | bytes 917504 | tf_op jit(solution)/shard_map/all_to_all | solution.py:342
  25.8 6.5 %collective-permute-start.2 = (bf16[128,512]{1,0:T(8,128)(2,1)S(1)}, bf16[128,512]{1,0:T(8,128)(2,1)S(1)}, u32[]{:S(2)}, u32[]{:S(2)}) collective-permute-start(bf16[128,512]{1,0:T(8,128)(2,1)S(1)} %get-tuple-element.25), channel_id=1, source_target_pairs={{0,1},{1,0},{2,3},{3,2},{4,5},{5,4},{6,7},{7,6},{8,9},{9,8},{10,11... | collective-permute-start | bytes 393224 | tf_op jit(solution)/shard_map/ppermute | solution.py:341
  43.3 10.2 %copy-start.4 = (s32[4608]{0:T(1024)S(1)}, s32[4608]{0:T(1024)}, u32[]{:S(2)}) copy-start(s32[4608]{0:T(1024)} %param.12) | copy-start | bytes 55300
  43.4 10.2 %copy-start.6 = (bf16[256,256]{1,0:T(8,128)(2,1)S(1)}, bf16[256,256]{1,0:T(8,128)(2,1)}, u32[]{:S(2)}) copy-start(bf16[256,256]{1,0:T(8,128)(2,1)} %constant.2.clone.table_ref) | copy-start | bytes 393220
  56.0 32.0 %all-to-all-start.3 = ((bf16[64,32,128]{2,1,0:T(8,128)(2,1)}), bf16[64,32,128]{2,1,0:T(8,128)(2,1)S(1)}, u32[]{:S(2)}, u32[]{:S(2)}) async-start(bf16[64,32,128]{2,1,0:T(8,128)(2,1)} %bitcast.12), calls=%async_computation.3 | async-start | bytes 1048576 | tf_op jit(solution)/shard_map/all_to_all | solution.py:351
  72.8 10.0 %collective-permute-start.3 = (bf16[576,256]{1,0:T(8,128)(2,1)S(1)}, bf16[576,256]{1,0:T(8,128)(2,1)S(1)}, u32[]{:S(2)}, u32[]{:S(2)}) collective-permute-start(bf16[576,256]{1,0:T(8,128)(2,1)S(1)} %get-tuple-element.33), channel_id=1, source_target_pairs={{0,8},{8,0},{1,9},{9,1},{2,10},{10,2},{3,11},{11,3},{4,12},{12,4},... | collective-permute-start | bytes 884744 | tf_op jit(solution)/shard_map/ppermute | solution.py:355
  110.8 10.2 %collective-permute-start.4 = (bf16[32,64,128]{2,1,0:T(8,128)(2,1)S(1)}, bf16[32,64,128]{2,1,0:T(8,128)(2,1)S(1)}, u32[]{:S(2)}, u32[]{:S(2)}) collective-permute-start(bf16[32,64,128]{2,1,0:T(8,128)(2,1)S(1)} %bitcast.14), channel_id=1, source_target_pairs={{0,8},{8,0},{1,9},{9,1},{2,10},{10,2},{3,11},{11,3},{4,12},{12,4},... | collective-permute-start | bytes 1572872 | tf_op jit(solution)/shard_map/ppermute | solution.py:359

commit v5 on v4

--- a/solution.py
+++ b/solution.py
@@ -66,17 +66,41 @@
     )
 
 
-def prepare_kernel(w_ref, send_ref):
+def prepare_kernel(w_ref, send_ref, held, packed, in_sems, out_sems):
     core, _, _ = places()
     rows = pl.ds(pl.multiple_of(core * 16, 16), 16)
+    loads = [
+        pltpu.make_async_copy(w_ref.at[:, rows, pl.ds(p * 1152, 1152)], held.at[p], in_sems.at[p]) for p in range(4)
+    ]
+    for load in loads:
+        load.start()
+    lane = lax.broadcasted_iota(jnp.int32, (16, 128), 1)
+    stores = []
     for m in range(8):
-        start = 9 * (m // 2)
-        for b, block in enumerate([start + 5 * (m % 2) + b for b in range(4)] + [start + 4]):
+        pair, odd = m // 2, m % 2
+        if odd == 0:
+            loads[pair].wait()
+        for b in range(4):
+            column = (5 * odd + b) * 128
             for k in range(3):
-                send_ref[m, b, k] = w_ref[k, rows, block * 128 : (block + 1) * 128]
-
-
-def align_kernel(x_ref, g_ref, far_x_ref, far_g_ref, exps_ref, xa_ref, ga_ref, half_ref, tail_ref, scale_ref):
+                packed[m, b * 3 + k] = held[pair, k, :, column : column + 128]
+        gate, up, down = [held[pair, k, :, 512:640] for k in range(3)]
+        turned = pltpu.roll(up.astype(F32), 64, 1)
+        packed[m, 12] = jnp.where((lane >= 64) == (odd == 1), gate.astype(F32), turned).astype(BF16)
+        packed[m, 13] = down
+        store = pltpu.make_async_copy(packed.at[m], send_ref.at[m], out_sems.at[m])
+        store.start()
+        stores.append(store)
+    for store in stores:
+        store.wait()
+
+
+def join_kernel(x_ref, g_ref, out_ref):
+    out_ref[0:576, :] = x_ref[...]
+    out_ref[576:1152, :] = g_ref[...]
+
+
+def align_kernel(near_ref, far_ref, exps_ref, xa_ref, ga_ref, half_ref, tail_ref, scale_ref):
     place = lax.broadcasted_iota(jnp.int32, (8, 128), 0)
     scales = jnp.zeros((8, 128), F32)
     for k in range(3):
@@ -86,38 +110,44 @@
         scales = jnp.where(place == k, up, jnp.where(place == 3 + k, down, scales))
     scale_ref[...] = scales * float(128.0**-0.5)
     _, odd, _ = places()
-    main, half = own_rows(odd)
+    main, half = pl.multiple_of(odd * 64, 64), pl.multiple_of((1 - odd) * 512, 64)
     mine = pl.ds(pl.multiple_of(512 + odd * 64, 64), 64)
     theirs = pl.ds(pl.multiple_of(576 - odd * 64, 64), 64)
-    for part, (to_ref, refs) in enumerate(((xa_ref, (x_ref, far_x_ref)), (ga_ref, (g_ref, far_g_ref)))):
-        for side, ref in enumerate(refs):
+    for part, to_ref in enumerate((xa_ref, ga_ref)):
+        for side, ref in enumerate((near_ref, far_ref)):
             tokens = pl.ds(side * 256, 256)
-            to_ref[0:512, tokens] = ref[main, :]
-            to_ref[mine, tokens] = ref[half, :]
+            rows = ref[pl.ds(576 * part + half, 64), :]
+            to_ref[0:512, tokens] = ref[pl.ds(576 * part + main, 512), :]
+            to_ref[mine, tokens] = rows
             to_ref[theirs, tokens] = jnp.zeros((64, 256), BF16)
-            half_ref[pl.ds(64 * part, 64), tokens] = ref[half, :]
+            half_ref[pl.ds(64 * part, 64), tokens] = rows
     wide = xa_ref[...].astype(F32)
     tail_ref[...] = stacked_pieces(jnp.sum(wide * wide, axis=0, keepdims=True))
 
 
-def forward_kernel(recv_ref, xa_ref, ga_ref, tail_ref, gain_ref, part_ref, w_ref):
+def forward_kernel(recv_ref, xa_ref, ga_ref, tail_ref, gain_ref, _, part_ref, w_ref):
     _, odd, first = places()
     for j in range(8):
-        for b in range(5):
-            for k in range(3):
-                w_ref[k * 128 + j * 16 : k * 128 + j * 16 + 16, b * 128 : (b + 1) * 128] = recv_ref[j, b, k]
+        for k in range(3):
+            rows = slice(k * 128 + j * 16, k * 128 + j * 16 + 16)
+            for b in range(4):
+                w_ref[rows, b * 128 : (b + 1) * 128] = recv_ref[j, b * 3 + k]
+        w_ref[j * 16 : j * 16 + 16, 512:640] = recv_ref[j, 12]
+        w_ref[128 + j * 16 : 128 + j * 16 + 16, 512:640] = pltpu.roll(recv_ref[j, 12].astype(F32), 64, 1).astype(BF16)
+        w_ref[256 + j * 16 : 256 + j * 16 + 16, 512:640] = recv_ref[j, 13]
     gained = w_ref[0:256].astype(F32) * jnp.concatenate(local_rows(gain_ref, first, odd), axis=1)
     high = gained.astype(BF16)
     low = (gained - high.astype(F32)).astype(BF16)
     gate_up = (dot(low, xa_ref[...]) + dot(high, xa_ref[...])).astype(BF16)
     down = dot(w_ref[256:384], ga_ref[...]).astype(BF16)
     tail = tail_ref[...]
-    for j in range(8):
-        x, yh = j % 4, j // 4
-        part_ref[x, yh, 0:16, :] = gate_up[j * 16 : j * 16 + 16]
-        part_ref[x, yh, 16:32, :] = gate_up[128 + j * 16 : 128 + j * 16 + 16]
-        part_ref[x, yh, 32:48, :] = down[j * 16 : j * 16 + 16]
-        part_ref[x, yh, 48:56, :] = tail
+    for x in range(4):
+        for yh in range(2):
+            j = 4 * yh + x
+            for k, source in enumerate((gate_up[0:128], gate_up[128:256], down)):
+                start = yh * 48 + k * 16
+                part_ref[x, start : start + 16, :] = source[j * 16 : j * 16 + 16]
+        part_ref[x, 96:104, :] = tail
 
 
 def stacked_pieces(row):
@@ -128,37 +158,42 @@
     return tail.astype(BF16)
 
 
-def sum_kernel(parts_ref, _, out_ref, own_ref):
-    for yh in range(2):
-        total = parts_ref[0, yh].astype(F32)
-        for i in range(1, 4):
-            total = total + parts_ref[i, yh].astype(F32)
-        own_ref[yh] = total[0:48]
-        out_ref[yh, 0:48, :] = total[0:48].astype(BF16)
-        out_ref[yh, 48:56, :] = stacked_pieces(total[48:49] + total[49:50] + total[50:51])
+def sum_kernel(parts_ref, out_ref, own_ref):
+    total = parts_ref[0].astype(F32)
+    for i in range(1, 4):
+        total = total + parts_ref[i].astype(F32)
+    own_ref[...] = total[0:96]
+    out_ref[0:96, :] = total[0:96].astype(BF16)
+    out_ref[96:104, :] = stacked_pieces(total[96:97] + total[97:98] + total[98:99])
 
 
 def activation_kernel(parts_ref, own_ref, out_ref, inv_ref):
     high = lax.axis_index("yh") == 1
+    tails = parts_ref[0, 96:104, :].astype(F32) + parts_ref[1, 96:104, :].astype(F32)
+    sums = tails[0:1] + tails[1:2] + tails[2:3]
+    inverse = lax.rsqrt(sums / FEATURES + 1e-06)
+    inv_ref[...] = jnp.broadcast_to(inverse, (8, 512))
+    others = [parts_ref[i, 0:96, :].astype(F32) for i in range(2)]
+    total = own_ref[...] + jnp.where(high, others[0], others[1])
+    mean = jnp.zeros((1, 512), F32)
     for yh in range(2):
-        others = [parts_ref[i, yh, 0:48, :].astype(F32) for i in range(2)]
-        total = own_ref[yh] + jnp.where(high, others[0], others[1])
-        tails = parts_ref[0, yh, 48:56, :].astype(F32) + parts_ref[1, yh, 48:56, :].astype(F32)
-        sums = tails[0:1] + tails[1:2] + tails[2:3]
-        inverse = lax.rsqrt(sums / FEATURES + 1e-06)
-        inv_ref[...] = jnp.broadcast_to(inverse, (8, 512))
-        gate_pre, up_proj, hidden_grad = total[0:16] * inverse, total[16:32] * inverse, total[32:48]
+        start = yh * 48
+        gate_pre = total[start : start + 16] * inverse
+        up_proj = total[start + 16 : start + 32] * inverse
+        hidden_grad = total[start + 32 : start + 48]
         activated, slope = gelu_parts(gate_pre)
         hidden = (activated * up_proj).astype(BF16)
         gate_grad = (hidden_grad * up_proj * slope).astype(BF16)
         up_grad = (hidden_grad * activated).astype(BF16)
         products = gate_grad.astype(F32) * gate_pre + up_grad.astype(F32) * up_proj
-        tail = stacked_pieces(jnp.sum(products, axis=0, keepdims=True) / FEATURES)
+        mean = mean + jnp.sum(products, axis=0, keepdims=True) / FEATURES
         for i in range(4):
-            out_ref[i, yh, 0:16, :] = gate_grad
-            out_ref[i, yh, 16:32, :] = up_grad
-            out_ref[i, yh, 32:48, :] = hidden
-            out_ref[i, yh, 48:56, :] = tail
+            out_ref[i, start : start + 16, :] = gate_grad
+            out_ref[i, start + 16 : start + 32, :] = up_grad
+            out_ref[i, start + 32 : start + 48, :] = hidden
+    tail = stacked_pieces(mean)
+    for i in range(4):
+        out_ref[i, 96:104, :] = tail
 
 
 def feature_column(table_ref, first, odd):
@@ -170,11 +205,12 @@
 
 
 def gathered_acts(acts_ref, k):
-    return jnp.concatenate([acts_ref[j % 4, j // 4, k * 16 : k * 16 + 16, :] for j in range(8)], axis=0)
+    starts = [(j % 4, j // 4 * 48 + k * 16) for j in range(8)]
+    return jnp.concatenate([acts_ref[x, start : start + 16, :] for x, start in starts], axis=0)
 
 
 def gradient_kernel(
-    acts_ref, xa_ref, ga_ref, half_ref, inv_ref, gain_ref, sign_ref, table_ref, scale_ref, term_ref
+    acts_ref, xa_ref, ga_ref, half_ref, inv_ref, gain_ref, sign_ref, table_ref, scale_ref, out_ref, term_ref, sems
 ):
     _, odd, first_block = places()
     table = table_ref[...]
@@ -188,6 +224,11 @@
         values = jnp.concatenate([ref[0:512, :].astype(F32), shared], axis=0)
         rights.append((values * sign if factor is None else values * factor * gain).astype(BF16))
     rights = (rights[0], rights[0], rights[1])
+    for s in range(27, 32):
+        term_ref[s] = jnp.zeros((64, 128), BF16)
+    copies = [
+        pltpu.make_async_copy(term_ref.at[pl.ds(8 * i, 8)], out_ref.at[pl.ds(8 * i, 8)], sems.at[i]) for i in range(4)
+    ]
     for k in range(3):
         acts = gathered_acts(acts_ref, k)
         scale = scale_ref[k : k + 1, 0:1]
@@ -215,17 +256,19 @@
                 else:
                     chosen = jnp.where(odd == 1, half[:, 1], half[:, 0])
                     term_ref[24 + k] = chosen.reshape(64, 128).astype(BF16)
-    for s in range(27, 32):
-        term_ref[s] = jnp.zeros((64, 128), BF16)
+        copies[k].start()
+    copies[3].start()
+    for copy in copies:
+        copy.wait()
 
 
 def resid_kernel(acts_ref, w_ref, xa_ref, inv_ref, gain_ref, _, near_ref, far_ref):
     _, odd, first = places()
     gain = feature_column(gain_ref, first, odd)
     inverse = inv_ref[0:1, :]
-    tails = acts_ref[0, 0, 48:56, :].astype(F32)
-    for j in range(1, 8):
-        tails = tails + acts_ref[j % 4, j // 4, 48:56, :].astype(F32)
+    tails = acts_ref[0, 96:104, :].astype(F32)
+    for x in range(1, 4):
+        tails = tails + acts_ref[x, 96:104, :].astype(F32)
     row_mean = tails[0:1] + tails[1:2] + tails[2:3]
     pair = jnp.concatenate([gathered_acts(acts_ref, k) for k in range(2)], axis=0)
     normed_grad = dot(w_ref[0:256], pair, CONTRACT_FIRST)
@@ -262,42 +305,34 @@
     return slice(start, start + 8)
 
 
-def restore_half(q, share_ref, sign_ref, table_ref, scale_ref, out_ref, held, sems):
+def restore_kernel(both_ref, sign_ref, table_ref, scale_ref, out_ref, held, sems):
     table = table_ref[0:128, 0:128]
     copies = []
     for k in range(3):
         factor = scale_ref[3 + k : 4 + k, :]
-
-        def put(block, low_half, high_half):
-            sign = (2 * sign_ref[block : block + 1, :] - 1).astype(F32) * factor
-            both = jnp.concatenate([low_half, high_half], axis=0) * sign
-            held[k, :, block * 128 : (block + 1) * 128] = both.astype(BF16)
-
-        for b in range(4):
-            halves = [dot(share_ref[k * 8 + 4 * i + b], table) for i in range(2)]
-            for m in range(8):
-                rows = received_rows(m)
-                put(9 * (m // 2) + 5 * (m % 2) + b, halves[0][rows], halves[1][rows])
-        shared = dot(share_ref[24 + k], table)
-        for p in range(4):
-            put(9 * p + 4, shared[received_rows(2 * p)], shared[received_rows(2 * p + 1)])
-        rows = pl.ds(pl.multiple_of(16 * q, 16), 16)
-        copy = pltpu.make_async_copy(held.at[k], out_ref.at[k, rows, :], sems.at[k])
+        for q in range(2):
+
+            def put(block, low_half, high_half):
+                sign = (2 * sign_ref[block : block + 1, :] - 1).astype(F32) * factor
+                both = jnp.concatenate([low_half, high_half], axis=0) * sign
+                held[k, 16 * q : 16 * q + 16, block * 128 : (block + 1) * 128] = both.astype(BF16)
+
+            for b in range(4):
+                halves = [dot(both_ref[q, k * 8 + 4 * i + b], table) for i in range(2)]
+                for m in range(8):
+                    rows = received_rows(m)
+                    put(9 * (m // 2) + 5 * (m % 2) + b, halves[0][rows], halves[1][rows])
+            shared = dot(both_ref[q, 24 + k], table)
+            for p in range(4):
+                put(9 * p + 4, shared[received_rows(2 * p)], shared[received_rows(2 * p + 1)])
+        copy = pltpu.make_async_copy(held.at[k], out_ref.at[k], sems.at[k])
         copy.start()
         copies.append(copy)
     for copy in copies:
         copy.wait()
 
 
-def near_restore_kernel(share_ref, sign_ref, table_ref, scale_ref, out_ref, held, sems):
-    restore_half(lax.axis_index("c"), share_ref, sign_ref, table_ref, scale_ref, out_ref, held, sems)
-
-
-def far_restore_kernel(share_ref, sign_ref, table_ref, scale_ref, _, out_ref, held, sems):
-    restore_half(1 - lax.axis_index("c"), share_ref, sign_ref, table_ref, scale_ref, out_ref, held, sems)
-
-
-def call(kernel, outs, scalars=0, scratch=(), anywhere=(), out_space=pltpu.VMEM, aliases=None, limit=VMEM_LIMIT):
+def call(kernel, outs, scalars=0, scratch=(), anywhere=(), out_space=pltpu.VMEM, limit=VMEM_LIMIT):
     def run(*operands):
         count = len(operands)
         spaces = [
@@ -309,7 +344,6 @@
             in_specs=[pl.BlockSpec(memory_space=place) for place in spaces],
             out_specs=[pl.BlockSpec(memory_space=out_space) for _ in outs],
             scratch_shapes=list(scratch),
-            input_output_aliases=aliases or {},
             compiler_params=pltpu.CompilerParams(vmem_limit_bytes=limit),
             cost_estimate=pl.CostEstimate(flops=10**9, bytes_accessed=10**6, transcendentals=0),
             name=kernel.__name__,
@@ -326,27 +360,42 @@
     x_cols, g_cols = residual.T, out_grad.T
     rows = ((640, 512), BF16)
 
-    (send,) = call(prepare_kernel, [((8, 5, 3, 16, 128), BF16)])(ffn_weights)
-    received = lax.all_to_all(send.reshape(8, 240, 128), AXES, 0, 0, axis_index_groups=near_groups())
+    (send,) = call(
+        prepare_kernel,
+        [((8, 14, 16, 128), BF16)],
+        scratch=[
+            pltpu.VMEM((4, 3, 16, 1152), BF16),
+            pltpu.VMEM((8, 14, 16, 128), BF16),
+            pltpu.SemaphoreType.DMA((4,)),
+            pltpu.SemaphoreType.DMA((8,)),
+        ],
+        anywhere=(0,),
+        out_space=pl.ANY,
+        limit=60 * 1024 * 1024,
+    )(ffn_weights)
+    received = lax.all_to_all(send.reshape(8, 224, 128), AXES, 0, 0, axis_index_groups=near_groups())
     near_x, near_g, _ = lax.optimization_barrier((x_cols, g_cols, send))
-    far_x = lax.ppermute(near_x, "c", cores)
-    far_g = lax.ppermute(near_g, "c", cores)
+    (near,) = call(join_kernel, [((1152, 256), BF16)])(near_x, near_g)
+    far = lax.ppermute(near, "c", cores)
     xa, ga, half, tail, scales = call(
         align_kernel, [rows, rows, ((128, 512), BF16), ((8, 512), BF16), ((8, 128), F32)], scalars=1
-    )(x_cols, g_cols, far_x, far_g, exponents)
-    parts, weights = call(forward_kernel, [((4, 2, 56, 512), BF16), ((384, 640), BF16)])(
-        received.reshape(8, 5, 3, 16, 128), xa, ga, tail, gain
-    )
-
+    )(near, far, exponents)
     other_half = lax.ppermute(half, "x", [(0, 1), (1, 0), (2, 3), (3, 2)])
-    parts = lax.all_to_all(parts.reshape(4, 112, 512), "x", 0, 0).reshape(4, 2, 56, 512)
-    sums, own = call(sum_kernel, [((2, 56, 512), BF16), ((2, 48, 512), F32)], anywhere=(1,))(parts, other_half)
+    parts, weights = call(forward_kernel, [((4, 104, 512), BF16), ((384, 640), BF16)], anywhere=(5,))(
+        received.reshape(8, 14, 16, 128), xa, ga, tail, gain, other_half
+    )
+
+    parts = lax.all_to_all(parts, "x", 0, 0)
+    sums, own = call(sum_kernel, [((104, 512), BF16), ((96, 512), F32)])(parts)
     sums = lax.all_gather(sums, "yh", axis=0)
-    message, inverse = call(activation_kernel, [((4, 2, 56, 512), BF16), ((8, 512), F32)])(sums, own)
-    acts = lax.all_to_all(message.reshape(4, 112, 512), "x", 0, 0).reshape(4, 2, 56, 512)
-    (terms,) = call(gradient_kernel, [((32, 64, 128), BF16)])(
-        acts, xa, ga, other_half, inverse, gain, signs, table, scales
-    )
+    message, inverse = call(activation_kernel, [((4, 104, 512), BF16), ((8, 512), F32)])(sums, own)
+    acts = lax.all_to_all(message, "x", 0, 0)
+    (terms,) = call(
+        gradient_kernel,
+        [((32, 64, 128), BF16)],
+        scratch=[pltpu.VMEM((32, 64, 128), BF16), pltpu.SemaphoreType.DMA((4,))],
+        out_space=pl.ANY,
+    )(acts, xa, ga, other_half, inverse, gain, signs, table, scales)
 
     summands = lax.all_to_all(terms.reshape(64, 32, 128), ("z", "yl", "yh"), 0, 0)
     near_resid, far_resid = call(resid_kernel, [((576, 256), F32), ((576, 256), BF16)], anywhere=(5,))(
@@ -356,13 +405,13 @@
     resid_cols, done = call(finish_kernel, [((576, 256), BF16), ((8, 128), F32)])(g_cols, near_resid, far_resid)
     (share,) = call(total_kernel, [((128, 16, 128), BF16)])(summands, done)
     share = lax.all_to_all(share, ("z", "yl", "x"), 0, 0).reshape(32, 64, 128)
-    other = lax.ppermute(share, "c", cores)
-    scratch = [pltpu.VMEM((3, 16, 4608), BF16), pltpu.SemaphoreType.DMA((3,))]
-    out = [((3, 32, 4608), BF16)]
-    (half_done,) = call(near_restore_kernel, out, scratch=scratch, out_space=pl.ANY)(share, signs, table, scales)
+    both = lax.all_gather(share[0:27], "c", axis=0)
     (weight_grads,) = call(
-        far_restore_kernel, out, scratch=scratch, anywhere=(4,), out_space=pl.ANY, aliases={4: 0}
-    )(other, signs, table, scales, half_done)
+        restore_kernel,
+        [((3, 32, 4608), BF16)],
+        scratch=[pltpu.VMEM((3, 32, 4608), BF16), pltpu.SemaphoreType.DMA((3,))],
+        out_space=pl.ANY,
+    )(both, signs, table, scales)
     return (resid_cols.T, weight_grads)
 
 

time: 123 us -> 120 us (0.976)
  starting transfers between devices: 55.7 us -> 33.8 us
  blocking collectives: 43.6 us -> 57.9 us
  waiting for transfers between devices: 11.5 us -> 17.8 us
    all_gather x0 -> x1, blocking collectives: none -> 9.02 us  [per_device(): both = lax.all_gather(share[0:27], 'c', axis=0)]
    all_to_all x1 -> x2, blocking collectives: 10.2 us -> 19.1 us  [the longest x1 10.2 us: per_device(): parts = lax.all_to_all(parts, 'x', 0, 0)]
    all_to_all x2 -> x1, starting transfers between devices: 12.1 us -> 3.49 us  [per_device(): lax.all_to_all(send.reshape(8, 224, 128), AXES, 0, 0, axis_index_groups=n...]
    ppermute x3 -> x1, starting transfers between devices: 15.1 us -> 8.79 us  [per_device(): far = lax.ppermute(near, 'c', cores)]
    all_to_all x1, starting transfers between devices: 16.3 us -> 11.1 us  [per_device(): lax.all_to_all(terms.reshape(64, 32, 128), ('z', 'yl', 'yh'), 0, 0)]
    all_to_all x2 -> x1, waiting for transfers between devices: 0.85 us -> 5.63 us  [per_device(): lax.all_to_all(send.reshape(8, 224, 128), AXES, 0, 0, axis_index_groups=n...]
    ppermute x3 -> x1, waiting for transfers between devices: 1.99 us -> 0.01 us  [per_device(): far = lax.ppermute(near, 'c', cores)]
    all_gather x1, blocking collectives: 10.8 us -> 8.92 us  [per_device(): sums = lax.all_gather(sums, 'yh', axis=0)]
  transfers between devices with their start and end apart: 8 -> 5, of which waited for: 7 -> 4; matrix products, arithmetic and copies ran while one was open for 0% -> 0% of each run, Pallas kernels for 3% -> 2%
where the time goes in v5:
time: 120 us; the launch traced here: 119 us
  blocking collectives  57.9 us (48%)
  starting transfers between devices  33.8 us (28%)
  waiting for transfers between devices  17.8 us (15%)
  Pallas kernels  8.86 us (7%)
    all_to_all x1, blocking collectives, per_device(): share = lax.all_to_all(share, ('z', 'yl', 'x'), 0, 0).reshape(32, 64, 128)  20.9 us
    all_to_all x1, starting transfers between devices, per_device(): lax.all_to_all(terms.reshape(64, 32, 128), ('z', 'yl', 'yh'), 0, 0)  11.1 us
    all_to_all x1, blocking collectives, per_device(): parts = lax.all_to_all(parts, 'x', 0, 0)  10.2 us
    all_gather x1, blocking collectives, per_device(): both = lax.all_gather(share[0:27], 'c', axis=0)  9.02 us
    all_gather x1, blocking collectives, per_device(): sums = lax.all_gather(sums, 'yh', axis=0)  8.92 us
    all_to_all x1, blocking collectives, per_device(): acts = lax.all_to_all(message, 'x', 0, 0)  8.91 us
    pallas_call x11, Pallas kernels, run(): pl.pallas_call(kernel, out_shape=[jax.ShapeDtypeStruct(shape, dtype) for...  8.86 us
    ppermute x1, starting transfers between devices, per_device(): far = lax.ppermute(near, 'c', cores)  8.79 us
  transfers between devices with their start and end apart: 5, of which 4 were waited for; matrix products, arithmetic and copies ran while one was open for 0% of the time, Pallas kernels for 2%

profile of v5, /device:TPU:1, one launch (start us, length us, event | category | flops | bytes accessed | tf_op | source)
XLA Modules:
  0.0 119.3 jit_solution(5945455118786314453)
XLA Ops:
  0.6 2.0 %prepare_kernel.1 = bf16[8,14,16,128]{3,2,1,0:T(8,128)(2,1)} custom-call(bf16[3,32,4608]{2,1,0:T(8,128)(2,1)} %w_ref.1), custom_call_target="tpu_custom_call" | custom-call | flops 1000000000 | bytes 1000000 | tf_op jit(solution)/shard_map/prepare_kernel/pallas_call | solution.py:341
  2.7 0.0 copy-done.1
  2.7 0.0 copy-done
  2.8 8.8 %collective-permute-start = (bf16[1152,256]{1,0:T(8,128)(2,1)S(1)}, bf16[1152,256]{1,0:T(8,128)(2,1)S(1)}, u32[]{:S(2)}, u32[]{:S(2)}) collective-permute-start(bf16[1152,256]{1,0:T(8,128)(2,1)S(1)} %join_kernel.1.near_ref), channel_id=1, source_target_pairs={{0,8},{8,0},{1,9},{9,1},{2,10},{10,2},{3,11},{11,3},{4,12},{12,4},... | collective-permute-start | bytes 1769480 | tf_op jit(solution)/shard_map/ppermute | solution.py:379
  11.6 0.0 copy-start.4
  11.6 3.5 %all-to-all-start = ((bf16[8,224,128]{2,1,0:T(8,128)(2,1)}), bf16[8,224,128]{2,1,0:T(8,128)(2,1)S(1)}, u32[]{:S(2)}, u32[]{:S(2)}) async-start(bf16[8,224,128]{2,1,0:T(8,128)(2,1)} %bitcast.1), calls=%async_computation | async-start | bytes 917504 | tf_op jit(solution)/shard_map/all_to_all | solution.py:376
  15.1 0.0 copy-start.2
  15.1 0.0 collective-permute-done.far_ref
  15.1 0.0 copy-done.4
  15.1 0.7 align_kernel.1
  15.8 3.3 %collective-permute-start.1 = (bf16[128,512]{1,0:T(8,128)(2,1)S(1)}, bf16[128,512]{1,0:T(8,128)(2,1)S(1)}, u32[]{:S(2)}, u32[]{:S(2)}) collective-permute-start(bf16[128,512]{1,0:T(8,128)(2,1)S(1)} %get-tuple-element.24), channel_id=1, source_target_pairs={{0,1},{1,0},{2,3},{3,2},{4,5},{5,4},{6,7},{7,6},{8,9},{9,8},{10,11... | collective-permute-start | bytes 393224 | tf_op jit(solution)/shard_map/ppermute | solution.py:383
  19.1 4.7 %collective-permute-done.1._.half_ref = bf16[128,512]{1,0:T(8,128)(2,1)S(1)} collective-permute-done((bf16[128,512]{1,0:T(8,128)(2,1)S(1)}, bf16[128,512]{1,0:T(8,128)(2,1)S(1)}, u32[]{:S(2)}, u32[]{:S(2)}) %collective-permute-start.1) | collective-permute-done | bytes 131104 | tf_op jit(solution)/shard_map/ppermute | solution.py:383
  23.8 5.6 %all-to-all-done = bf16[8,224,128]{2,1,0:T(8,128)(2,1)S(1)} async-done(((bf16[8,224,128]{2,1,0:T(8,128)(2,1)}), bf16[8,224,128]{2,1,0:T(8,128)(2,1)S(1)}, u32[]{:S(2)}, u32[]{:S(2)}) %all-to-all-start) | async-done | bytes 458784 | tf_op jit(solution)/shard_map/all_to_all | solution.py:376
  29.4 0.7 forward_kernel.1
  30.2 10.2 %all_to_all.25.parts_ref = bf16[4,104,512]{2,1,0:T(8,128)(2,1)S(1)} all-to-all(bf16[4,104,512]{2,1,0:T(8,128)(2,1)S(1)} %get-tuple-element.25), channel_id=1, replica_groups=mesh['z'=8,'yl'=4,'c'=2,'yh'=2,'x'=4] {'x'}, dimensions={0} | all-to-all | bytes 851968 | tf_op jit(solution)/shard_map/all_to_all | solution.py:388
  40.4 0.1 sum_kernel.1
  40.5 8.9 %all-gather = bf16[208,512]{1,0:T(8,128)(2,1)S(1)} all-gather(bf16[104,512]{1,0:T(8,128)(2,1)S(1)} %get-tuple-element.26), channel_id=2, replica_groups=mesh['z'=8,'yl'=4,'c'=2,'yh'=2,'x'=4] {'yh'}, dimensions={0}, use_global_device_ids=true | all-gather | bytes 319488 | tf_op jit(solution)/shard_map/all_gather | solution.py:390
  49.4 0.1 activation_kernel.1
  49.5 0.0 copy-start.3
  49.5 0.0 copy-start.5
  49.6 8.9 %all_to_all.26.acts_ref = bf16[4,104,512]{2,1,0:T(8,128)(2,1)S(1)} all-to-all(bf16[4,104,512]{2,1,0:T(8,128)(2,1)S(1)} %get-tuple-element.28), channel_id=1, replica_groups=mesh['z'=8,'yl'=4,'c'=2,'yh'=2,'x'=4] {'x'}, dimensions={0} | all-to-all | bytes 851968 | tf_op jit(solution)/shard_map/all_to_all | solution.py:392
  58.5 2.4 %gradient_kernel.1._ = bf16[32,64,128]{2,1,0:T(8,128)(2,1)} custom-call(bf16[4,104,512]{2,1,0:T(8,128)(2,1)S(1)} %all_to_all.26.acts_ref, bf16[640,512]{1,0:T(8,128)(2,1)S(1)} %get-tuple-element.21.xa_ref, bf16[640,512]{1,0:T(8,128)(2,1)S(1)} %get-tuple-element.22.ga_ref, bf16[128,512]{1,0:T(8,128)(2,1)S(1)} %collective-permute-done.1._.half_ref, ...), custom_call_target="tpu_custom_call" | custom-call | flops 1000000000 | bytes 1000000 | tf_op jit(solution)/shard_map/gradient_kernel/pallas_call | solution.py:341
  60.9 11.1 %all-to-all-start.3 = ((bf16[64,32,128]{2,1,0:T(8,128)(2,1)}), bf16[64,32,128]{2,1,0:T(8,128)(2,1)S(1)}, u32[]{:S(2)}, u32[]{:S(2)}) async-start(bf16[64,32,128]{2,1,0:T(8,128)(2,1)} %bitcast.8), calls=%async_computation.3 | async-start | bytes 1048576 | tf_op jit(solution)/shard_map/all_to_all | solution.py:400
  72.0 0.5 resid_kernel.1
  72.5 7.1 %collective-permute-start.2 = (bf16[576,256]{1,0:T(8,128)(2,1)S(1)}, bf16[576,256]{1,0:T(8,128)(2,1)S(1)}, u32[]{:S(2)}, u32[]{:S(2)}) collective-permute-start(bf16[576,256]{1,0:T(8,128)(2,1)S(1)} %get-tuple-element.33), channel_id=1, source_target_pairs={{0,8},{8,0},{1,9},{9,1},{2,10},{10,2},{3,11},{11,3},{4,12},{12,4},... | collective-permute-start | bytes 884744 | tf_op jit(solution)/shard_map/ppermute | solution.py:404
  79.7 1.2 collective-permute-done.2.far_ref
  80.9 0.8 finish_kernel.1
  81.7 6.2 %all-to-all-done.3.terms_ref = bf16[64,32,128]{2,1,0:T(8,128)(2,1)S(1)} async-done(((bf16[64,32,128]{2,1,0:T(8,128)(2,1)}), bf16[64,32,128]{2,1,0:T(8,128)(2,1)S(1)}, u32[]{:S(2)}, u32[]{:S(2)}) %all-to-all-start.3) | async-done | bytes 524320 | tf_op jit(solution)/shard_map/all_to_all | solution.py:400
  87.9 0.1 total_kernel.1
  88.0 20.9 %all_to_all.27 = bf16[128,16,128]{2,1,0:T(8,128)(2,1)S(1)} all-to-all(bf16[128,16,128]{2,1,0:T(8,128)(2,1)S(1)} %total_kernel.1), channel_id=1, replica_groups=mesh['z'=8,'yl'=4,'c'=2,'yh'=2,'x'=4] {'z','yl','x'}, dimensions={0} | all-to-all | bytes 1048576 | tf_op jit(solution)/shard_map/all_to_all | solution.py:407
  108.9 9.0 %all_gather.15.both_ref = bf16[2,27,64,128]{3,2,1,0:T(8,128)(2,1)S(1)} all-gather(bf16[1,27,64,128]{3,2,1,0:T(8,128)(2,1)S(1)} %bitcast.20), channel_id=1, replica_groups=mesh['z'=8,'yl'=4,'c'=2,'yh'=2,'x'=4] {'c'}, dimensions={0}, use_global_device_ids=true | all-gather | bytes 1327104 | tf_op jit(solution)/shard_map/all_gather | solution.py:408
  117.9 1.4 %restore_kernel.1 = bf16[3,32,4608]{2,1,0:T(8,128)(2,1)} custom-call(bf16[2,27,64,128]{3,2,1,0:T(8,128)(2,1)S(1)} %all_gather.15.both_ref, s32[36,128]{1,0:T(8,128)S(1)} %bitcast.19, bf16[256,256]{1,0:T(8,128)(2,1)S(1)} %copy-done.5, f32[8,128]{1,0:T(8,128)S(1)} %get-tuple-element.31.scale_ref), custom_call_target="tpu_custom_call" | custom-call | flops 1000000000 | bytes 1000000 | tf_op jit(solution)/shard_map/restore_kernel/pallas_call | solution.py:341
  (11 shorter events, 0.1 us)
Async XLA Ops:
  0.6 2.1 %copy-start.1 = (bf16[256,576]{0,1:T(8,128)(2,1)S(1)}, bf16[256,576]{0,1:T(8,128)(2,1)}, u32[]{:S(2)}) copy-start(bf16[256,576]{0,1:T(8,128)(2,1)} %param.8) | copy-start | bytes 884740
  0.6 2.1 %copy-start = (bf16[256,576]{0,1:T(8,128)(2,1)S(1)}, bf16[256,576]{0,1:T(8,128)(2,1)}, u32[]{:S(2)}) copy-start(bf16[256,576]{0,1:T(8,128)(2,1)} %param.7) | copy-start | bytes 884740
  2.8 12.3 %collective-permute-start = (bf16[1152,256]{1,0:T(8,128)(2,1)S(1)}, bf16[1152,256]{1,0:T(8,128)(2,1)S(1)}, u32[]{:S(2)}, u32[]{:S(2)}) collective-permute-start(bf16[1152,256]{1,0:T(8,128)(2,1)S(1)} %join_kernel.1.near_ref), channel_id=1, source_target_pairs={{0,8},{8,0},{1,9},{9,1},{2,10},{10,2},{3,11},{11,3},{4,12},{12,4},... | collective-permute-start | bytes 1769480 | tf_op jit(solution)/shard_map/ppermute | solution.py:379
  11.6 3.5 %copy-start.4 = (s32[3]{0:T(128)S(1)}, s32[3]{0:T(128)}, u32[]{:S(2)}) copy-start(s32[3]{0:T(128)} %exps_ref.1) | copy-start | bytes 40
  11.6 17.9 %all-to-all-start = ((bf16[8,224,128]{2,1,0:T(8,128)(2,1)}), bf16[8,224,128]{2,1,0:T(8,128)(2,1)S(1)}, u32[]{:S(2)}, u32[]{:S(2)}) async-start(bf16[8,224,128]{2,1,0:T(8,128)(2,1)} %bitcast.1), calls=%async_computation | async-start | bytes 917504 | tf_op jit(solution)/shard_map/all_to_all | solution.py:376
  15.1 14.4 %copy-start.2 = (f32[4608]{0:T(1024)S(1)}, f32[4608]{0:T(1024)}, u32[]{:S(2)}) copy-start(f32[4608]{0:T(1024)} %param.10) | copy-start | bytes 55300
  15.8 8.0 %collective-permute-start.1 = (bf16[128,512]{1,0:T(8,128)(2,1)S(1)}, bf16[128,512]{1,0:T(8,128)(2,1)S(1)}, u32[]{:S(2)}, u32[]{:S(2)}) collective-permute-start(bf16[128,512]{1,0:T(8,128)(2,1)S(1)} %get-tuple-element.24), channel_id=1, source_target_pairs={{0,1},{1,0},{2,3},{3,2},{4,5},{5,4},{6,7},{7,6},{8,9},{9,8},{10,11... | collective-permute-start | bytes 393224 | tf_op jit(solution)/shard_map/ppermute | solution.py:383
  30.1 10.3 %copy-start.6 = (bf16[384,640]{1,0:T(8,128)(2,1)}, bf16[384,640]{1,0:T(8,128)(2,1)S(1)}, u32[]{:S(2)}) copy-start(bf16[384,640]{1,0:T(8,128)(2,1)S(1)} %get-tuple-element.29.w_ref) | copy-start | bytes 1474564
  49.5 8.9 %copy-start.3 = (s32[4608]{0:T(1024)S(1)}, s32[4608]{0:T(1024)}, u32[]{:S(2)}) copy-start(s32[4608]{0:T(1024)} %param.12) | copy-start | bytes 55300
  49.5 8.9 %copy-start.5 = (bf16[256,256]{1,0:T(8,128)(2,1)S(1)}, bf16[256,256]{1,0:T(8,128)(2,1)}, u32[]{:S(2)}) copy-start(bf16[256,256]{1,0:T(8,128)(2,1)} %constant.2.clone.table_ref) | copy-start | bytes 393220
  60.9 11.1 %copy-start.7 = (bf16[384,640]{1,0:T(8,128)(2,1)S(1)}, bf16[384,640]{1,0:T(8,128)(2,1)}, u32[]{:S(2)}) copy-start(bf16[384,640]{1,0:T(8,128)(2,1)} %copy-done.6) | copy-start | bytes 1474564
  60.9 27.0 %all-to-all-start.3 = ((bf16[64,32,128]{2,1,0:T(8,128)(2,1)}), bf16[64,32,128]{2,1,0:T(8,128)(2,1)S(1)}, u32[]{:S(2)}, u32[]{:S(2)}) async-start(bf16[64,32,128]{2,1,0:T(8,128)(2,1)} %bitcast.8), calls=%async_computation.3 | async-start | bytes 1048576 | tf_op jit(solution)/shard_map/all_to_all | solution.py:400
  72.5 8.3 %collective-permute-start.2 = (bf16[576,256]{1,0:T(8,128)(2,1)S(1)}, bf16[576,256]{1,0:T(8,128)(2,1)S(1)}, u32[]{:S(2)}, u32[]{:S(2)}) collective-permute-start(bf16[576,256]{1,0:T(8,128)(2,1)S(1)} %get-tuple-element.33), channel_id=1, source_target_pairs={{0,8},{8,0},{1,9},{9,1},{2,10},{10,2},{3,11},{11,3},{4,12},{12,4},... | collective-permute-start | bytes 884744 | tf_op jit(solution)/shard_map/ppermute | solution.py:404

commit v6 on v5

--- a/solution.py
+++ b/solution.py
@@ -95,12 +95,16 @@
         store.wait()
 
 
-def join_kernel(x_ref, g_ref, out_ref):
+def join_kernel(x_ref, g_ref, out_ref, half_ref):
+    _, odd, _ = places()
+    half = pl.ds(pl.multiple_of((1 - odd) * 512, 64), 64)
     out_ref[0:576, :] = x_ref[...]
     out_ref[576:1152, :] = g_ref[...]
-
-
-def align_kernel(near_ref, far_ref, exps_ref, xa_ref, ga_ref, half_ref, tail_ref, scale_ref):
+    half_ref[0:64, :] = x_ref[half, :]
+    half_ref[64:128, :] = g_ref[half, :]
+
+
+def align_kernel(near_ref, far_ref, exps_ref, xa_ref, ga_ref, tail_ref, scale_ref):
     place = lax.broadcasted_iota(jnp.int32, (8, 128), 0)
     scales = jnp.zeros((8, 128), F32)
     for k in range(3):
@@ -116,16 +120,14 @@
     for part, to_ref in enumerate((xa_ref, ga_ref)):
         for side, ref in enumerate((near_ref, far_ref)):
             tokens = pl.ds(side * 256, 256)
-            rows = ref[pl.ds(576 * part + half, 64), :]
             to_ref[0:512, tokens] = ref[pl.ds(576 * part + main, 512), :]
-            to_ref[mine, tokens] = rows
+            to_ref[mine, tokens] = ref[pl.ds(576 * part + half, 64), :]
             to_ref[theirs, tokens] = jnp.zeros((64, 256), BF16)
-            half_ref[pl.ds(64 * part, 64), tokens] = rows
     wide = xa_ref[...].astype(F32)
     tail_ref[...] = stacked_pieces(jnp.sum(wide * wide, axis=0, keepdims=True))
 
 
-def forward_kernel(recv_ref, xa_ref, ga_ref, tail_ref, gain_ref, _, part_ref, w_ref):
+def forward_kernel(recv_ref, xa_ref, ga_ref, tail_ref, gain_ref, _near, _far, part_ref, own_ref, w_ref):
     _, odd, first = places()
     for j in range(8):
         for k in range(3):
@@ -138,15 +140,22 @@
     gained = w_ref[0:256].astype(F32) * jnp.concatenate(local_rows(gain_ref, first, odd), axis=1)
     high = gained.astype(BF16)
     low = (gained - high.astype(F32)).astype(BF16)
-    gate_up = (dot(low, xa_ref[...]) + dot(high, xa_ref[...])).astype(BF16)
-    down = dot(w_ref[256:384], ga_ref[...]).astype(BF16)
+    both = dot(jnp.concatenate([low, high], axis=0), xa_ref[...])
+    gate_up = both[0:256] + both[256:512]
+    down = dot(w_ref[256:384], ga_ref[...])
     tail = tail_ref[...]
+    my_x = lax.axis_index("x")
+    for yh in range(2):
+        for k, source in enumerate((gate_up[0:128], gate_up[128:256], down)):
+            rows = slice(yh * 48 + k * 16, yh * 48 + k * 16 + 16)
+            own = jnp.zeros((16, 512), F32)
+            for x in range(4):
+                j = 4 * yh + x
+                values = source[j * 16 : j * 16 + 16]
+                part_ref[x, rows, :] = values.astype(BF16)
+                own = jnp.where(my_x == x, values, own)
+            own_ref[rows, :] = own
     for x in range(4):
-        for yh in range(2):
-            j = 4 * yh + x
-            for k, source in enumerate((gate_up[0:128], gate_up[128:256], down)):
-                start = yh * 48 + k * 16
-                part_ref[x, start : start + 16, :] = source[j * 16 : j * 16 + 16]
         part_ref[x, 96:104, :] = tail
 
 
@@ -158,13 +167,16 @@
     return tail.astype(BF16)
 
 
-def sum_kernel(parts_ref, out_ref, own_ref):
-    total = parts_ref[0].astype(F32)
-    for i in range(1, 4):
-        total = total + parts_ref[i].astype(F32)
-    own_ref[...] = total[0:96]
-    out_ref[0:96, :] = total[0:96].astype(BF16)
-    out_ref[96:104, :] = stacked_pieces(total[96:97] + total[97:98] + total[98:99])
+def sum_kernel(parts_ref, mine_ref, out_ref, own_ref):
+    my_x = lax.axis_index("x")
+    total = mine_ref[...]
+    tails = jnp.zeros((8, 512), F32)
+    for i in range(4):
+        total = total + jnp.where(my_x == i, 0.0, parts_ref[i, 0:96, :].astype(F32))
+        tails = tails + parts_ref[i, 96:104, :].astype(F32)
+    own_ref[...] = total
+    out_ref[0:96, :] = total.astype(BF16)
+    out_ref[96:104, :] = stacked_pieces(tails[0:1] + tails[1:2] + tails[2:3])
 
 
 def activation_kernel(parts_ref, own_ref, out_ref, inv_ref):
@@ -210,7 +222,7 @@
 
 
 def gradient_kernel(
-    acts_ref, xa_ref, ga_ref, half_ref, inv_ref, gain_ref, sign_ref, table_ref, scale_ref, out_ref, term_ref, sems
+    acts_ref, xa_ref, ga_ref, near_half_ref, far_half_ref, inv_ref, gain_ref, sign_ref, table_ref, scale_ref, out_ref, term_ref, sems
 ):
     _, odd, first_block = places()
     table = table_ref[...]
@@ -219,45 +231,58 @@
     theirs = (lax.broadcasted_iota(jnp.int32, (128, 512), 0) >= 64) == (odd == 0)
     rights = []
     for part, (ref, factor) in enumerate(((xa_ref, inv_ref[0:1, :]), (ga_ref, None))):
-        other = half_ref[part * 64 : part * 64 + 64, :].astype(F32)
+        other = jnp.concatenate(
+            [half_ref[part * 64 : part * 64 + 64, :] for half_ref in (near_half_ref, far_half_ref)], axis=1
+        ).astype(F32)
         shared = jnp.where(theirs, jnp.concatenate([other, other], axis=0), ref[512:640, :].astype(F32))
         values = jnp.concatenate([ref[0:512, :].astype(F32), shared], axis=0)
         rights.append((values * sign if factor is None else values * factor * gain).astype(BF16))
-    rights = (rights[0], rights[0], rights[1])
     for s in range(27, 32):
         term_ref[s] = jnp.zeros((64, 128), BF16)
-    copies = [
-        pltpu.make_async_copy(term_ref.at[pl.ds(8 * i, 8)], out_ref.at[pl.ds(8 * i, 8)], sems.at[i]) for i in range(4)
-    ]
-    for k in range(3):
-        acts = gathered_acts(acts_ref, k)
-        scale = scale_ref[k : k + 1, 0:1]
+    copies = []
+
+    def send(at, count):
+        copy = pltpu.make_async_copy(term_ref.at[pl.ds(at, count)], out_ref.at[pl.ds(at, count)], sems.at[len(copies)])
+        copy.start()
+        copies.append(copy)
+
+    for matrices, right in (((0, 1), rights[0]), ((2,), rights[1])):
+        acts = jnp.concatenate([gathered_acts(acts_ref, k) for k in matrices], axis=0)
+        height = acts.shape[0]
         terms = jnp.concatenate(
             [
-                dot(acts[:, s * 256 : s * 256 + 256], rights[k][:, s * 256 : s * 256 + 256], CONTRACT_LAST)
+                dot(acts[:, s * 256 : s * 256 + 256], right[:, s * 256 : s * 256 + 256], CONTRACT_LAST)
                 for s in range(2)
             ],
             axis=0,
         )
-        for first in (0, 256, 512):
+        for first in (512, 0, 256):
             width = min(256, 640 - first)
             block = terms[:, first : first + width]
             high = block.astype(BF16)
             low = (block - high.astype(F32)).astype(BF16)
             part = table[0:width, 0:width]
             rotated = dot(low, part) + dot(high, part)
-            quantized = jnp.clip(rotated * scale, -127.0, 127.0).astype(BF16).astype(F32)
-            total = quantized[0:128] + quantized[128:256]
-            for b in range(first // 128, (first + width) // 128):
-                half = total[:, b * 128 - first : b * 128 - first + 128].reshape(8, 2, 8, 128)
-                if b < 4:
-                    term_ref[k * 8 + b] = half[:, 0].reshape(64, 128).astype(BF16)
-                    term_ref[k * 8 + 4 + b] = half[:, 1].reshape(64, 128).astype(BF16)
-                else:
-                    chosen = jnp.where(odd == 1, half[:, 1], half[:, 0])
-                    term_ref[24 + k] = chosen.reshape(64, 128).astype(BF16)
-        copies[k].start()
-    copies[3].start()
+            for i, k in enumerate(matrices):
+                scale = scale_ref[k : k + 1, 0:1]
+                total = None
+                for start in (i * 128, height + i * 128):
+                    scaled = jnp.clip(rotated[start : start + 128] * scale, -127.0, 127.0)
+                    quantized = scaled.astype(BF16).astype(F32)
+                    total = quantized if total is None else total + quantized
+                for b in range(first // 128, (first + width) // 128):
+                    half = total[:, b * 128 - first : b * 128 - first + 128].reshape(8, 2, 8, 128)
+                    if b < 4:
+                        term_ref[k * 8 + b] = half[:, 0].reshape(64, 128).astype(BF16)
+                        term_ref[k * 8 + 4 + b] = half[:, 1].reshape(64, 128).astype(BF16)
+                    else:
+                        chosen = jnp.where(odd == 1, half[:, 1], half[:, 0])
+                        term_ref[24 + k] = chosen.reshape(64, 128).astype(BF16)
+                if first < 512:
+                    send(k * 8 + first // 128, 2)
+                    send(k * 8 + 4 + first // 128, 2)
+                elif k == 2:
+                    send(24, 8)
     for copy in copies:
         copy.wait()
 
@@ -317,8 +342,9 @@
                 both = jnp.concatenate([low_half, high_half], axis=0) * sign
                 held[k, 16 * q : 16 * q + 16, block * 128 : (block + 1) * 128] = both.astype(BF16)
 
+            own = dot(both_ref[q, k * 8 : k * 8 + 8].reshape(512, 128), table)
             for b in range(4):
-                halves = [dot(both_ref[q, k * 8 + 4 * i + b], table) for i in range(2)]
+                halves = [own[(4 * i + b) * 64 : (4 * i + b) * 64 + 64] for i in range(2)]
                 for m in range(8):
                     rows = received_rows(m)
                     put(9 * (m // 2) + 5 * (m % 2) + b, halves[0][rows], halves[1][rows])
@@ -375,27 +401,31 @@
     )(ffn_weights)
     received = lax.all_to_all(send.reshape(8, 224, 128), AXES, 0, 0, axis_index_groups=near_groups())
     near_x, near_g, _ = lax.optimization_barrier((x_cols, g_cols, send))
-    (near,) = call(join_kernel, [((1152, 256), BF16)])(near_x, near_g)
+    near, half = call(join_kernel, [((1152, 256), BF16), ((128, 256), BF16)])(near_x, near_g)
     far = lax.ppermute(near, "c", cores)
-    xa, ga, half, tail, scales = call(
-        align_kernel, [rows, rows, ((128, 512), BF16), ((8, 512), BF16), ((8, 128), F32)], scalars=1
-    )(near, far, exponents)
-    other_half = lax.ppermute(half, "x", [(0, 1), (1, 0), (2, 3), (3, 2)])
-    parts, weights = call(forward_kernel, [((4, 104, 512), BF16), ((384, 640), BF16)], anywhere=(5,))(
-        received.reshape(8, 14, 16, 128), xa, ga, tail, gain, other_half
+    near_half = lax.ppermute(half, "x", [(0, 1), (1, 0), (2, 3), (3, 2)])
+    across = [(c * 4 + x, (1 - c) * 4 + (x ^ 1)) for c in range(2) for x in range(4)]
+    far_half = lax.ppermute(half, ("c", "x"), across)
+    xa, ga, tail, scales = call(align_kernel, [rows, rows, ((8, 512), BF16), ((8, 128), F32)], scalars=1)(
+        near, far, exponents
+    )
+    parts, mine, weights = call(
+        forward_kernel, [((4, 104, 512), BF16), ((96, 512), F32), ((384, 640), BF16)], anywhere=(5, 6)
+    )(
+        received.reshape(8, 14, 16, 128), xa, ga, tail, gain, near_half, far_half
     )
 
     parts = lax.all_to_all(parts, "x", 0, 0)
-    sums, own = call(sum_kernel, [((104, 512), BF16), ((96, 512), F32)])(parts)
+    sums, own = call(sum_kernel, [((104, 512), BF16), ((96, 512), F32)])(parts, mine)
     sums = lax.all_gather(sums, "yh", axis=0)
     message, inverse = call(activation_kernel, [((4, 104, 512), BF16), ((8, 512), F32)])(sums, own)
     acts = lax.all_to_all(message, "x", 0, 0)
     (terms,) = call(
         gradient_kernel,
         [((32, 64, 128), BF16)],
-        scratch=[pltpu.VMEM((32, 64, 128), BF16), pltpu.SemaphoreType.DMA((4,))],
+        scratch=[pltpu.VMEM((32, 64, 128), BF16), pltpu.SemaphoreType.DMA((13,))],
         out_space=pl.ANY,
-    )(acts, xa, ga, other_half, inverse, gain, signs, table, scales)
+    )(acts, xa, ga, near_half, far_half, inverse, gain, signs, table, scales)
 
     summands = lax.all_to_all(terms.reshape(64, 32, 128), ("z", "yl", "yh"), 0, 0)
     near_resid, far_resid = call(resid_kernel, [((576, 256), F32), ((576, 256), BF16)], anywhere=(5,))(

time: 120 us -> 120 us (level)
  starting transfers between devices: 33.8 us -> 38.4 us
  waiting for transfers between devices: 17.8 us -> 14.2 us
    all_to_all x1, waiting for transfers between devices: 5.63 us -> 0.01 us  [per_device(): lax.all_to_all(send.reshape(8, 224, 128), AXES, 0, 0, axis_index_groups=n...]
    all_to_all x1, starting transfers between devices: 3.49 us -> 7.9 us  [per_device(): lax.all_to_all(send.reshape(8, 224, 128), AXES, 0, 0, axis_index_groups=n...]
    ppermute x1, starting transfers between devices: 8.79 us -> 4.52 us  [per_device(): far = lax.ppermute(near, 'c', cores)]
    all_to_all x1, starting transfers between devices: 11.1 us -> 14.9 us  [per_device(): lax.all_to_all(terms.reshape(64, 32, 128), ('z', 'yl', 'yh'), 0, 0)]
    all_to_all x1, waiting for transfers between devices: 6.19 us -> 8.73 us  [per_device(): lax.all_to_all(terms.reshape(64, 32, 128), ('z', 'yl', 'yh'), 0, 0)]
    ppermute x1 -> x2, starting transfers between devices: 3.25 us -> 5.49 us  [the longest x1 3.54 us: per_device(): near_half = lax.ppermute(half, 'x', [(0, 1), (1, 0), (2, 3), (3, 2)])]
    ppermute x1, starting transfers between devices: 7.14 us -> 5.59 us  [per_device(): far_resid = lax.ppermute(far_resid, 'c', cores)]
    all_gather x1, blocking collectives: 9.02 us -> 7.75 us  [per_device(): both = lax.all_gather(share[0:27], 'c', axis=0)]
  transfers between devices with their start and end apart: 5 -> 6, of which waited for: 4 -> 3; matrix products, arithmetic and copies ran while one was open for 0% -> 0% of each run, Pallas kernels for 2% -> 2%
where the time goes in v6:
time: 120 us
  blocking collectives  57.4 us (48%)
  starting transfers between devices  38.4 us (32%)
  waiting for transfers between devices  14.2 us (12%)
  Pallas kernels  8.74 us (7%)
    all_to_all x1, blocking collectives, per_device(): share = lax.all_to_all(share, ('z', 'yl', 'x'), 0, 0).reshape(32, 64, 128)  21.3 us
    all_to_all x1, starting transfers between devices, per_device(): lax.all_to_all(terms.reshape(64, 32, 128), ('z', 'yl', 'yh'), 0, 0)  14.9 us
    all_to_all x1, blocking collectives, per_device(): parts = lax.all_to_all(parts, 'x', 0, 0)  11.3 us
    all_to_all x1, blocking collectives, per_device(): acts = lax.all_to_all(message, 'x', 0, 0)  8.91 us
    pallas_call x11, Pallas kernels, run(): pl.pallas_call(kernel, out_shape=[jax.ShapeDtypeStruct(shape, dtype) for...  8.74 us
    all_to_all x1, waiting for transfers between devices, per_device(): lax.all_to_all(terms.reshape(64, 32, 128), ('z', 'yl', 'yh'), 0, 0)  8.73 us
    all_gather x1, blocking collectives, per_device(): sums = lax.all_gather(sums, 'yh', axis=0)  8.24 us
    all_to_all x1, starting transfers between devices, per_device(): lax.all_to_all(send.reshape(8, 224, 128), AXES, 0, 0, axis_index_groups=n...  7.9 us
  transfers between devices with their start and end apart: 6, of which 3 were waited for; matrix products, arithmetic and copies ran while one was open for 0% of the time, Pallas kernels for 2%

profile of v6, /device:TPU:1, one launch (start us, length us, event | category | flops | bytes accessed | tf_op | source)
XLA Modules:
  0.0 119.7 jit_solution(9725772396076958440)
XLA Ops:
  0.6 2.0 %prepare_kernel.1 = bf16[8,14,16,128]{3,2,1,0:T(8,128)(2,1)} custom-call(bf16[3,32,4608]{2,1,0:T(8,128)(2,1)} %w_ref.1), custom_call_target="tpu_custom_call" | custom-call | flops 1000000000 | bytes 1000000 | tf_op jit(solution)/shard_map/prepare_kernel/pallas_call | solution.py:367
  2.6 0.0 copy-start
  2.6 0.0 copy-start.1
  2.6 7.9 %all-to-all-start = ((bf16[8,224,128]{2,1,0:T(8,128)(2,1)}), bf16[8,224,128]{2,1,0:T(8,128)(2,1)S(1)}, u32[]{:S(2)}, u32[]{:S(2)}) async-start(bf16[8,224,128]{2,1,0:T(8,128)(2,1)} %bitcast.21), calls=%async_computation | async-start | bytes 917504 | tf_op jit(solution)/shard_map/all_to_all | solution.py:402
  10.6 0.0 copy-start.4
  10.6 4.5 %collective-permute-start = (bf16[1152,256]{1,0:T(8,128)(2,1)S(1)}, bf16[1152,256]{1,0:T(8,128)(2,1)S(1)}, u32[]{:S(2)}, u32[]{:S(2)}) collective-permute-start(bf16[1152,256]{1,0:T(8,128)(2,1)S(1)} %get-tuple-element.23.near_ref), channel_id=1, source_target_pairs={{0,8},{8,0},{1,9},{9,1},{2,10},{10,2},{3,11},{11,3},{4,12},{12,4},... | collective-permute-start | bytes 1769480 | tf_op jit(solution)/shard_map/ppermute | solution.py:405
  15.1 0.0 copy-start.2
  15.2 3.5 %collective-permute-start.1 = (bf16[128,256]{1,0:T(8,128)(2,1)S(1)}, bf16[128,256]{1,0:T(8,128)(2,1)S(1)}, u32[]{:S(2)}, u32[]{:S(2)}) collective-permute-start(bf16[128,256]{1,0:T(8,128)(2,1)S(1)} %get-tuple-element.27), channel_id=1, source_target_pairs={{0,1},{1,0},{2,3},{3,2},{4,5},{5,4},{6,7},{7,6},{8,9},{9,8},{10,11... | collective-permute-start | bytes 196616 | tf_op jit(solution)/shard_map/ppermute | solution.py:406
  18.7 2.0 %collective-permute-start.2 = (bf16[128,256]{1,0:T(8,128)(2,1)S(1)}, bf16[128,256]{1,0:T(8,128)(2,1)S(1)}, u32[]{:S(2)}, u32[]{:S(2)}) collective-permute-start(bf16[128,256]{1,0:T(8,128)(2,1)S(1)} %get-tuple-element.27), channel_id=1, source_target_pairs={{0,9},{1,8},{2,11},{3,10},{8,1},{9,0},{10,3},{11,2},{4,13},{5,12},... | collective-permute-start | bytes 196616 | tf_op jit(solution)/shard_map/ppermute | solution.py:408
  20.7 0.0 collective-permute-done.far_ref
  20.7 0.7 align_kernel.1
  21.4 0.0 collective-permute-done.1._near.near_half_ref
  21.4 4.3 %collective-permute-done.2._far.far_half_ref = bf16[128,256]{1,0:T(8,128)(2,1)S(1)} collective-permute-done((bf16[128,256]{1,0:T(8,128)(2,1)S(1)}, bf16[128,256]{1,0:T(8,128)(2,1)S(1)}, u32[]{:S(2)}, u32[]{:S(2)}) %collective-permute-start.2) | collective-permute-done | bytes 65568 | tf_op jit(solution)/shard_map/ppermute | solution.py:408
  25.7 0.7 forward_kernel.1
  26.4 11.3 %all_to_all.25.parts_ref = bf16[4,104,512]{2,1,0:T(8,128)(2,1)S(1)} all-to-all(bf16[4,104,512]{2,1,0:T(8,128)(2,1)S(1)} %get-tuple-element.28), channel_id=1, replica_groups=mesh['z'=8,'yl'=4,'c'=2,'yh'=2,'x'=4] {'x'}, dimensions={0} | all-to-all | bytes 851968 | tf_op jit(solution)/shard_map/all_to_all | solution.py:418
  37.7 0.1 sum_kernel.1
  37.8 8.2 %all-gather = bf16[208,512]{1,0:T(8,128)(2,1)S(1)} all-gather(bf16[104,512]{1,0:T(8,128)(2,1)S(1)} %get-tuple-element.30), channel_id=2, replica_groups=mesh['z'=8,'yl'=4,'c'=2,'yh'=2,'x'=4] {'yh'}, dimensions={0}, use_global_device_ids=true | all-gather | bytes 319488 | tf_op jit(solution)/shard_map/all_gather | solution.py:420
  46.0 0.1 activation_kernel.1
  46.1 0.0 copy-start.3
  46.2 0.0 copy-start.5
  46.2 8.9 %all_to_all.26.acts_ref = bf16[4,104,512]{2,1,0:T(8,128)(2,1)S(1)} all-to-all(bf16[4,104,512]{2,1,0:T(8,128)(2,1)S(1)} %get-tuple-element.32), channel_id=1, replica_groups=mesh['z'=8,'yl'=4,'c'=2,'yh'=2,'x'=4] {'x'}, dimensions={0} | all-to-all | bytes 851968 | tf_op jit(solution)/shard_map/all_to_all | solution.py:422
  55.1 2.5 %gradient_kernel.1._ = bf16[32,64,128]{2,1,0:T(8,128)(2,1)} custom-call(bf16[4,104,512]{2,1,0:T(8,128)(2,1)S(1)} %all_to_all.26.acts_ref, bf16[640,512]{1,0:T(8,128)(2,1)S(1)} %get-tuple-element.24.xa_ref, bf16[640,512]{1,0:T(8,128)(2,1)S(1)} %get-tuple-element.25.ga_ref, bf16[128,256]{1,0:T(8,128)(2,1)S(1)} %collective-permute-done.1._near.near_half_ref, ...), custom_call_target="tpu_custom_call" | custom-call | flops 1000000000 | bytes 1000000 | tf_op jit(solution)/shard_map/gradient_kernel/pallas_call | solution.py:367
  57.6 14.9 %all-to-all-start.3 = ((bf16[64,32,128]{2,1,0:T(8,128)(2,1)}), bf16[64,32,128]{2,1,0:T(8,128)(2,1)S(1)}, u32[]{:S(2)}, u32[]{:S(2)}) async-start(bf16[64,32,128]{2,1,0:T(8,128)(2,1)} %bitcast.8), calls=%async_computation.3 | async-start | bytes 1048576 | tf_op jit(solution)/shard_map/all_to_all | solution.py:430
  72.5 0.5 resid_kernel.1
  73.0 5.6 %collective-permute-start.3 = (bf16[576,256]{1,0:T(8,128)(2,1)S(1)}, bf16[576,256]{1,0:T(8,128)(2,1)S(1)}, u32[]{:S(2)}, u32[]{:S(2)}) collective-permute-start(bf16[576,256]{1,0:T(8,128)(2,1)S(1)} %get-tuple-element.37), channel_id=1, source_target_pairs={{0,8},{8,0},{1,9},{9,1},{2,10},{10,2},{3,11},{11,3},{4,12},{12,4},... | collective-permute-start | bytes 884744 | tf_op jit(solution)/shard_map/ppermute | solution.py:434
  78.6 1.2 collective-permute-done.3.far_ref
  79.8 0.8 finish_kernel.1
  80.6 8.7 %all-to-all-done.3.terms_ref = bf16[64,32,128]{2,1,0:T(8,128)(2,1)S(1)} async-done(((bf16[64,32,128]{2,1,0:T(8,128)(2,1)}), bf16[64,32,128]{2,1,0:T(8,128)(2,1)S(1)}, u32[]{:S(2)}, u32[]{:S(2)}) %all-to-all-start.3) | async-done | bytes 524320 | tf_op jit(solution)/shard_map/all_to_all | solution.py:430
  89.4 0.1 total_kernel.1
  89.5 21.3 %all_to_all.27 = bf16[128,16,128]{2,1,0:T(8,128)(2,1)S(1)} all-to-all(bf16[128,16,128]{2,1,0:T(8,128)(2,1)S(1)} %total_kernel.1), channel_id=1, replica_groups=mesh['z'=8,'yl'=4,'c'=2,'yh'=2,'x'=4] {'z','yl','x'}, dimensions={0} | all-to-all | bytes 1048576 | tf_op jit(solution)/shard_map/all_to_all | solution.py:437
  110.8 7.7 %all_gather.15.both_ref = bf16[2,27,64,128]{3,2,1,0:T(8,128)(2,1)S(1)} all-gather(bf16[1,27,64,128]{3,2,1,0:T(8,128)(2,1)S(1)} %bitcast.20), channel_id=1, replica_groups=mesh['z'=8,'yl'=4,'c'=2,'yh'=2,'x'=4] {'c'}, dimensions={0}, use_global_device_ids=true | all-gather | bytes 1327104 | tf_op jit(solution)/shard_map/all_gather | solution.py:438
  118.5 1.2 restore_kernel.1
  (9 shorter events, 0.1 us)
Async XLA Ops:
  2.6 7.9 %copy-start = (bf16[256,576]{0,1:T(8,128)(2,1)S(1)}, bf16[256,576]{0,1:T(8,128)(2,1)}, u32[]{:S(2)}) copy-start(bf16[256,576]{0,1:T(8,128)(2,1)} %param.7) | copy-start | bytes 884740
  2.6 7.9 %copy-start.1 = (bf16[256,576]{0,1:T(8,128)(2,1)S(1)}, bf16[256,576]{0,1:T(8,128)(2,1)}, u32[]{:S(2)}) copy-start(bf16[256,576]{0,1:T(8,128)(2,1)} %param.8) | copy-start | bytes 884740
  2.6 23.1 %all-to-all-start = ((bf16[8,224,128]{2,1,0:T(8,128)(2,1)}), bf16[8,224,128]{2,1,0:T(8,128)(2,1)S(1)}, u32[]{:S(2)}, u32[]{:S(2)}) async-start(bf16[8,224,128]{2,1,0:T(8,128)(2,1)} %bitcast.21), calls=%async_computation | async-start | bytes 917504 | tf_op jit(solution)/shard_map/all_to_all | solution.py:402
  10.6 10.1 %copy-start.4 = (s32[3]{0:T(128)S(1)}, s32[3]{0:T(128)}, u32[]{:S(2)}) copy-start(s32[3]{0:T(128)} %exps_ref.1) | copy-start | bytes 40
  10.6 10.0 %collective-permute-start = (bf16[1152,256]{1,0:T(8,128)(2,1)S(1)}, bf16[1152,256]{1,0:T(8,128)(2,1)S(1)}, u32[]{:S(2)}, u32[]{:S(2)}) collective-permute-start(bf16[1152,256]{1,0:T(8,128)(2,1)S(1)} %get-tuple-element.23.near_ref), channel_id=1, source_target_pairs={{0,8},{8,0},{1,9},{9,1},{2,10},{10,2},{3,11},{11,3},{4,12},{12,4},... | collective-permute-start | bytes 1769480 | tf_op jit(solution)/shard_map/ppermute | solution.py:405
  15.1 10.6 %copy-start.2 = (f32[4608]{0:T(1024)S(1)}, f32[4608]{0:T(1024)}, u32[]{:S(2)}) copy-start(f32[4608]{0:T(1024)} %param.10) | copy-start | bytes 55300
  15.2 6.2 %collective-permute-start.1 = (bf16[128,256]{1,0:T(8,128)(2,1)S(1)}, bf16[128,256]{1,0:T(8,128)(2,1)S(1)}, u32[]{:S(2)}, u32[]{:S(2)}) collective-permute-start(bf16[128,256]{1,0:T(8,128)(2,1)S(1)} %get-tuple-element.27), channel_id=1, source_target_pairs={{0,1},{1,0},{2,3},{3,2},{4,5},{5,4},{6,7},{7,6},{8,9},{9,8},{10,11... | collective-permute-start | bytes 196616 | tf_op jit(solution)/shard_map/ppermute | solution.py:406
  18.7 7.0 %collective-permute-start.2 = (bf16[128,256]{1,0:T(8,128)(2,1)S(1)}, bf16[128,256]{1,0:T(8,128)(2,1)S(1)}, u32[]{:S(2)}, u32[]{:S(2)}) collective-permute-start(bf16[128,256]{1,0:T(8,128)(2,1)S(1)} %get-tuple-element.27), channel_id=1, source_target_pairs={{0,9},{1,8},{2,11},{3,10},{8,1},{9,0},{10,3},{11,2},{4,13},{5,12},... | collective-permute-start | bytes 196616 | tf_op jit(solution)/shard_map/ppermute | solution.py:408
  46.1 8.9 %copy-start.3 = (s32[4608]{0:T(1024)S(1)}, s32[4608]{0:T(1024)}, u32[]{:S(2)}) copy-start(s32[4608]{0:T(1024)} %param.12) | copy-start | bytes 55300
  46.2 8.9 %copy-start.5 = (bf16[256,256]{1,0:T(8,128)(2,1)S(1)}, bf16[256,256]{1,0:T(8,128)(2,1)}, u32[]{:S(2)}) copy-start(bf16[256,256]{1,0:T(8,128)(2,1)} %constant.2.clone.table_ref) | copy-start | bytes 393220
  57.6 31.8 %all-to-all-start.3 = ((bf16[64,32,128]{2,1,0:T(8,128)(2,1)}), bf16[64,32,128]{2,1,0:T(8,128)(2,1)S(1)}, u32[]{:S(2)}, u32[]{:S(2)}) async-start(bf16[64,32,128]{2,1,0:T(8,128)(2,1)} %bitcast.8), calls=%async_computation.3 | async-start | bytes 1048576 | tf_op jit(solution)/shard_map/all_to_all | solution.py:430
  73.0 6.8 %collective-permute-start.3 = (bf16[576,256]{1,0:T(8,128)(2,1)S(1)}, bf16[576,256]{1,0:T(8,128)(2,1)S(1)}, u32[]{:S(2)}, u32[]{:S(2)}) collective-permute-start(bf16[576,256]{1,0:T(8,128)(2,1)S(1)} %get-tuple-element.37), channel_id=1, source_target_pairs={{0,8},{8,0},{1,9},{9,1},{2,10},{10,2},{3,11},{11,3},{4,12},{12,4},... | collective-permute-start | bytes 884744 | tf_op jit(solution)/shard_map/ppermute | solution.py:434

commit v7 on v6

--- a/solution.py
+++ b/solution.py
@@ -95,16 +95,12 @@
         store.wait()
 
 
-def join_kernel(x_ref, g_ref, out_ref, half_ref):
-    _, odd, _ = places()
-    half = pl.ds(pl.multiple_of((1 - odd) * 512, 64), 64)
+def join_kernel(x_ref, g_ref, out_ref):
     out_ref[0:576, :] = x_ref[...]
     out_ref[576:1152, :] = g_ref[...]
-    half_ref[0:64, :] = x_ref[half, :]
-    half_ref[64:128, :] = g_ref[half, :]
-
-
-def align_kernel(near_ref, far_ref, exps_ref, xa_ref, ga_ref, tail_ref, scale_ref):
+
+
+def align_kernel(near_ref, far_ref, exps_ref, xa_ref, ga_ref, half_ref, tail_ref, scale_ref):
     place = lax.broadcasted_iota(jnp.int32, (8, 128), 0)
     scales = jnp.zeros((8, 128), F32)
     for k in range(3):
@@ -121,13 +117,15 @@
         for side, ref in enumerate((near_ref, far_ref)):
             tokens = pl.ds(side * 256, 256)
             to_ref[0:512, tokens] = ref[pl.ds(576 * part + main, 512), :]
-            to_ref[mine, tokens] = ref[pl.ds(576 * part + half, 64), :]
+            rows = ref[pl.ds(576 * part + half, 64), :]
+            half_ref[pl.ds(64 * part, 64), tokens] = rows
+            to_ref[mine, tokens] = rows
             to_ref[theirs, tokens] = jnp.zeros((64, 256), BF16)
     wide = xa_ref[...].astype(F32)
     tail_ref[...] = stacked_pieces(jnp.sum(wide * wide, axis=0, keepdims=True))
 
 
-def forward_kernel(recv_ref, xa_ref, ga_ref, tail_ref, gain_ref, _near, _far, part_ref, own_ref, w_ref):
+def forward_kernel(recv_ref, xa_ref, ga_ref, tail_ref, gain_ref, _, part_ref, own_ref, w_ref):
     _, odd, first = places()
     for j in range(8):
         for k in range(3):
@@ -222,7 +220,7 @@
 
 
 def gradient_kernel(
-    acts_ref, xa_ref, ga_ref, near_half_ref, far_half_ref, inv_ref, gain_ref, sign_ref, table_ref, scale_ref, out_ref, term_ref, sems
+    acts_ref, xa_ref, ga_ref, half_ref, inv_ref, gain_ref, sign_ref, table_ref, scale_ref, out_ref, term_ref, sems
 ):
     _, odd, first_block = places()
     table = table_ref[...]
@@ -231,9 +229,7 @@
     theirs = (lax.broadcasted_iota(jnp.int32, (128, 512), 0) >= 64) == (odd == 0)
     rights = []
     for part, (ref, factor) in enumerate(((xa_ref, inv_ref[0:1, :]), (ga_ref, None))):
-        other = jnp.concatenate(
-            [half_ref[part * 64 : part * 64 + 64, :] for half_ref in (near_half_ref, far_half_ref)], axis=1
-        ).astype(F32)
+        other = half_ref[part * 64 : part * 64 + 64, :].astype(F32)
         shared = jnp.where(theirs, jnp.concatenate([other, other], axis=0), ref[512:640, :].astype(F32))
         values = jnp.concatenate([ref[0:512, :].astype(F32), shared], axis=0)
         rights.append((values * sign if factor is None else values * factor * gain).astype(BF16))
@@ -246,7 +242,7 @@
         copy.start()
         copies.append(copy)
 
-    for matrices, right in (((0, 1), rights[0]), ((2,), rights[1])):
+    for matrices, right in (((2,), rights[1]), ((0, 1), rights[0])):
         acts = jnp.concatenate([gathered_acts(acts_ref, k) for k in matrices], axis=0)
         height = acts.shape[0]
         terms = jnp.concatenate(
@@ -256,7 +252,7 @@
             ],
             axis=0,
         )
-        for first in (512, 0, 256):
+        for first in (0, 256, 512):
             width = min(256, 640 - first)
             block = terms[:, first : first + width]
             high = block.astype(BF16)
@@ -281,7 +277,7 @@
                 if first < 512:
                     send(k * 8 + first // 128, 2)
                     send(k * 8 + 4 + first // 128, 2)
-                elif k == 2:
+                elif k == 1:
                     send(24, 8)
     for copy in copies:
         copy.wait()
@@ -401,18 +397,16 @@
     )(ffn_weights)
     received = lax.all_to_all(send.reshape(8, 224, 128), AXES, 0, 0, axis_index_groups=near_groups())
     near_x, near_g, _ = lax.optimization_barrier((x_cols, g_cols, send))
-    near, half = call(join_kernel, [((1152, 256), BF16), ((128, 256), BF16)])(near_x, near_g)
+    (near,) = call(join_kernel, [((1152, 256), BF16)])(near_x, near_g)
     far = lax.ppermute(near, "c", cores)
-    near_half = lax.ppermute(half, "x", [(0, 1), (1, 0), (2, 3), (3, 2)])
-    across = [(c * 4 + x, (1 - c) * 4 + (x ^ 1)) for c in range(2) for x in range(4)]
-    far_half = lax.ppermute(half, ("c", "x"), across)
-    xa, ga, tail, scales = call(align_kernel, [rows, rows, ((8, 512), BF16), ((8, 128), F32)], scalars=1)(
-        near, far, exponents
-    )
+    xa, ga, half, tail, scales = call(
+        align_kernel, [rows, rows, ((128, 512), BF16), ((8, 512), BF16), ((8, 128), F32)], scalars=1
+    )(near, far, exponents)
+    other_half = lax.ppermute(half, "x", [(0, 1), (1, 0), (2, 3), (3, 2)])
     parts, mine, weights = call(
-        forward_kernel, [((4, 104, 512), BF16), ((96, 512), F32), ((384, 640), BF16)], anywhere=(5, 6)
+        forward_kernel, [((4, 104, 512), BF16), ((96, 512), F32), ((384, 640), BF16)], anywhere=(5,)
     )(
-        received.reshape(8, 14, 16, 128), xa, ga, tail, gain, near_half, far_half
+        received.reshape(8, 14, 16, 128), xa, ga, tail, gain, other_half
     )
 
     parts = lax.all_to_all(parts, "x", 0, 0)
@@ -425,7 +419,7 @@
         [((32, 64, 128), BF16)],
         scratch=[pltpu.VMEM((32, 64, 128), BF16), pltpu.SemaphoreType.DMA((13,))],
         out_space=pl.ANY,
-    )(acts, xa, ga, near_half, far_half, inverse, gain, signs, table, scales)
+    )(acts, xa, ga, other_half, inverse, gain, signs, table, scales)
 
     summands = lax.all_to_all(terms.reshape(64, 32, 128), ("z", "yl", "yh"), 0, 0)
     near_resid, far_resid = call(resid_kernel, [((576, 256), F32), ((576, 256), BF16)], anywhere=(5,))(

time: 120 us -> 120 us (level)
  starting transfers between devices: 38.4 us -> 33.8 us
  waiting for transfers between devices: 14.2 us -> 17.7 us
    all_to_all x1, waiting for transfers between devices: 0.01 us -> 5.63 us  [per_device(): lax.all_to_all(send.reshape(8, 224, 128), AXES, 0, 0, axis_index_groups=n...]
    all_to_all x1, starting transfers between devices: 7.9 us -> 3.49 us  [per_device(): lax.all_to_all(send.reshape(8, 224, 128), AXES, 0, 0, axis_index_groups=n...]
    ppermute x1, starting transfers between devices: 4.52 us -> 8.79 us  [per_device(): far = lax.ppermute(near, 'c', cores)]
    all_to_all x1, starting transfers between devices: 14.9 us -> 11.1 us  [per_device(): lax.all_to_all(terms.reshape(64, 32, 128), ('z', 'yl', 'yh'), 0, 0)]
    all_to_all x1, waiting for transfers between devices: 8.73 us -> 6.16 us  [per_device(): lax.all_to_all(terms.reshape(64, 32, 128), ('z', 'yl', 'yh'), 0, 0)]
    ppermute x2 -> x1, starting transfers between devices: 5.49 us -> 3.25 us  [per_device(): other_half = lax.ppermute(half, 'x', [(0, 1), (1, 0), (2, 3), (3, 2)])]
    ppermute x1, starting transfers between devices: 5.59 us -> 7.16 us  [per_device(): far_resid = lax.ppermute(far_resid, 'c', cores)]
    all_gather x1, blocking collectives: 7.75 us -> 9.14 us  [per_device(): both = lax.all_gather(share[0:27], 'c', axis=0)]
  transfers between devices with their start and end apart: 6 -> 5, of which waited for: 3 -> 4; matrix products, arithmetic and copies ran while one was open for 0% -> 0% of each run, Pallas kernels for 2% -> 2%
where the time goes in v7:
time: 120 us; the launch traced here: 119 us
  blocking collectives  58 us (48%)
  starting transfers between devices  33.8 us (28%)
  waiting for transfers between devices  17.7 us (15%)
  Pallas kernels  8.57 us (7%)
    all_to_all x1, blocking collectives, per_device(): share = lax.all_to_all(share, ('z', 'yl', 'x'), 0, 0).reshape(32, 64, 128)  20.8 us
    all_to_all x1, starting transfers between devices, per_device(): lax.all_to_all(terms.reshape(64, 32, 128), ('z', 'yl', 'yh'), 0, 0)  11.1 us
    all_to_all x1, blocking collectives, per_device(): parts = lax.all_to_all(parts, 'x', 0, 0)  10.3 us
    all_gather x1, blocking collectives, per_device(): both = lax.all_gather(share[0:27], 'c', axis=0)  9.14 us
    all_gather x1, blocking collectives, per_device(): sums = lax.all_gather(sums, 'yh', axis=0)  8.92 us
    all_to_all x1, blocking collectives, per_device(): acts = lax.all_to_all(message, 'x', 0, 0)  8.91 us
    ppermute x1, starting transfers between devices, per_device(): far = lax.ppermute(near, 'c', cores)  8.79 us
    pallas_call x11, Pallas kernels, run(): pl.pallas_call(kernel, out_shape=[jax.ShapeDtypeStruct(shape, dtype) for...  8.57 us
  transfers between devices with their start and end apart: 5, of which 4 were waited for; matrix products, arithmetic and copies ran while one was open for 0% of the time, Pallas kernels for 2%

profile of v7, /device:TPU:1, one launch (start us, length us, event | category | flops | bytes accessed | tf_op | source)
XLA Modules:
  0.0 119.0 jit_solution(11596836570725216826)
XLA Ops:
  0.6 0.0 copy-start.1
  0.6 0.0 copy-start
  0.6 2.0 %prepare_kernel.1 = bf16[8,14,16,128]{3,2,1,0:T(8,128)(2,1)} custom-call(bf16[3,32,4608]{2,1,0:T(8,128)(2,1)} %w_ref.1), custom_call_target="tpu_custom_call" | custom-call | flops 1000000000 | bytes 1000000 | tf_op jit(solution)/shard_map/prepare_kernel/pallas_call | solution.py:363
  2.8 8.8 %collective-permute-start = (bf16[1152,256]{1,0:T(8,128)(2,1)S(1)}, bf16[1152,256]{1,0:T(8,128)(2,1)S(1)}, u32[]{:S(2)}, u32[]{:S(2)}) collective-permute-start(bf16[1152,256]{1,0:T(8,128)(2,1)S(1)} %join_kernel.1.near_ref), channel_id=1, source_target_pairs={{0,8},{8,0},{1,9},{9,1},{2,10},{10,2},{3,11},{11,3},{4,12},{12,4},... | collective-permute-start | bytes 1769480 | tf_op jit(solution)/shard_map/ppermute | solution.py:401
  11.6 0.0 copy-start.4
  11.6 3.5 %all-to-all-start = ((bf16[8,224,128]{2,1,0:T(8,128)(2,1)}), bf16[8,224,128]{2,1,0:T(8,128)(2,1)S(1)}, u32[]{:S(2)}, u32[]{:S(2)}) async-start(bf16[8,224,128]{2,1,0:T(8,128)(2,1)} %bitcast.1), calls=%async_computation | async-start | bytes 917504 | tf_op jit(solution)/shard_map/all_to_all | solution.py:398
  15.1 0.0 copy-start.2
  15.1 0.0 collective-permute-done.far_ref
  15.1 0.7 align_kernel.1
  15.8 3.3 %collective-permute-start.1 = (bf16[128,512]{1,0:T(8,128)(2,1)S(1)}, bf16[128,512]{1,0:T(8,128)(2,1)S(1)}, u32[]{:S(2)}, u32[]{:S(2)}) collective-permute-start(bf16[128,512]{1,0:T(8,128)(2,1)S(1)} %get-tuple-element.25), channel_id=1, source_target_pairs={{0,1},{1,0},{2,3},{3,2},{4,5},{5,4},{6,7},{7,6},{8,9},{9,8},{10,11... | collective-permute-start | bytes 393224 | tf_op jit(solution)/shard_map/ppermute | solution.py:405
  19.1 4.7 %collective-permute-done.1._.half_ref = bf16[128,512]{1,0:T(8,128)(2,1)S(1)} collective-permute-done((bf16[128,512]{1,0:T(8,128)(2,1)S(1)}, bf16[128,512]{1,0:T(8,128)(2,1)S(1)}, u32[]{:S(2)}, u32[]{:S(2)}) %collective-permute-start.1) | collective-permute-done | bytes 131104 | tf_op jit(solution)/shard_map/ppermute | solution.py:405
  23.8 5.6 %all-to-all-done = bf16[8,224,128]{2,1,0:T(8,128)(2,1)S(1)} async-done(((bf16[8,224,128]{2,1,0:T(8,128)(2,1)}), bf16[8,224,128]{2,1,0:T(8,128)(2,1)S(1)}, u32[]{:S(2)}, u32[]{:S(2)}) %all-to-all-start) | async-done | bytes 458784 | tf_op jit(solution)/shard_map/all_to_all | solution.py:398
  29.4 0.7 forward_kernel.1
  30.1 0.0 copy-start.6
  30.1 10.3 %all_to_all.25.parts_ref = bf16[4,104,512]{2,1,0:T(8,128)(2,1)S(1)} all-to-all(bf16[4,104,512]{2,1,0:T(8,128)(2,1)S(1)} %get-tuple-element.26), channel_id=1, replica_groups=mesh['z'=8,'yl'=4,'c'=2,'yh'=2,'x'=4] {'x'}, dimensions={0} | all-to-all | bytes 851968 | tf_op jit(solution)/shard_map/all_to_all | solution.py:412
  40.4 0.1 sum_kernel.1
  40.5 8.9 %all-gather = bf16[208,512]{1,0:T(8,128)(2,1)S(1)} all-gather(bf16[104,512]{1,0:T(8,128)(2,1)S(1)} %get-tuple-element.28), channel_id=2, replica_groups=mesh['z'=8,'yl'=4,'c'=2,'yh'=2,'x'=4] {'yh'}, dimensions={0}, use_global_device_ids=true | all-gather | bytes 319488 | tf_op jit(solution)/shard_map/all_gather | solution.py:414
  49.4 0.1 activation_kernel.1
  49.6 0.0 copy-start.3
  49.6 0.0 copy-start.5
  49.6 8.9 %all_to_all.26.acts_ref = bf16[4,104,512]{2,1,0:T(8,128)(2,1)S(1)} all-to-all(bf16[4,104,512]{2,1,0:T(8,128)(2,1)S(1)} %get-tuple-element.30), channel_id=1, replica_groups=mesh['z'=8,'yl'=4,'c'=2,'yh'=2,'x'=4] {'x'}, dimensions={0} | all-to-all | bytes 851968 | tf_op jit(solution)/shard_map/all_to_all | solution.py:416
  58.5 2.2 %gradient_kernel.1._ = bf16[32,64,128]{2,1,0:T(8,128)(2,1)} custom-call(bf16[4,104,512]{2,1,0:T(8,128)(2,1)S(1)} %all_to_all.26.acts_ref, bf16[640,512]{1,0:T(8,128)(2,1)S(1)} %get-tuple-element.22.xa_ref, bf16[640,512]{1,0:T(8,128)(2,1)S(1)} %get-tuple-element.23.ga_ref, bf16[128,512]{1,0:T(8,128)(2,1)S(1)} %collective-permute-done.1._.half_ref, ...), custom_call_target="tpu_custom_call" | custom-call | flops 1000000000 | bytes 1000000 | tf_op jit(solution)/shard_map/gradient_kernel/pallas_call | solution.py:363
  60.8 11.1 %all-to-all-start.3 = ((bf16[64,32,128]{2,1,0:T(8,128)(2,1)}), bf16[64,32,128]{2,1,0:T(8,128)(2,1)S(1)}, u32[]{:S(2)}, u32[]{:S(2)}) async-start(bf16[64,32,128]{2,1,0:T(8,128)(2,1)} %bitcast.8), calls=%async_computation.3 | async-start | bytes 1048576 | tf_op jit(solution)/shard_map/all_to_all | solution.py:424
  71.9 0.5 resid_kernel.1
  72.4 7.2 %collective-permute-start.2 = (bf16[576,256]{1,0:T(8,128)(2,1)S(1)}, bf16[576,256]{1,0:T(8,128)(2,1)S(1)}, u32[]{:S(2)}, u32[]{:S(2)}) collective-permute-start(bf16[576,256]{1,0:T(8,128)(2,1)S(1)} %get-tuple-element.35), channel_id=1, source_target_pairs={{0,8},{8,0},{1,9},{9,1},{2,10},{10,2},{3,11},{11,3},{4,12},{12,4},... | collective-permute-start | bytes 884744 | tf_op jit(solution)/shard_map/ppermute | solution.py:428
  79.6 1.2 collective-permute-done.2.far_ref
  80.8 0.8 finish_kernel.1
  81.6 6.2 %all-to-all-done.3.terms_ref = bf16[64,32,128]{2,1,0:T(8,128)(2,1)S(1)} async-done(((bf16[64,32,128]{2,1,0:T(8,128)(2,1)}), bf16[64,32,128]{2,1,0:T(8,128)(2,1)S(1)}, u32[]{:S(2)}, u32[]{:S(2)}) %all-to-all-start.3) | async-done | bytes 524320 | tf_op jit(solution)/shard_map/all_to_all | solution.py:424
  87.8 0.1 total_kernel.1
  87.9 20.8 %all_to_all.27 = bf16[128,16,128]{2,1,0:T(8,128)(2,1)S(1)} all-to-all(bf16[128,16,128]{2,1,0:T(8,128)(2,1)S(1)} %total_kernel.1), channel_id=1, replica_groups=mesh['z'=8,'yl'=4,'c'=2,'yh'=2,'x'=4] {'z','yl','x'}, dimensions={0} | all-to-all | bytes 1048576 | tf_op jit(solution)/shard_map/all_to_all | solution.py:431
  108.7 9.1 %all_gather.15.both_ref = bf16[2,27,64,128]{3,2,1,0:T(8,128)(2,1)S(1)} all-gather(bf16[1,27,64,128]{3,2,1,0:T(8,128)(2,1)S(1)} %bitcast.20), channel_id=1, replica_groups=mesh['z'=8,'yl'=4,'c'=2,'yh'=2,'x'=4] {'c'}, dimensions={0}, use_global_device_ids=true | all-gather | bytes 1327104 | tf_op jit(solution)/shard_map/all_gather | solution.py:432
  117.9 1.2 restore_kernel.1
  (11 shorter events, 0.1 us)
Async XLA Ops:
  0.6 2.1 %copy-start.1 = (bf16[256,576]{0,1:T(8,128)(2,1)S(1)}, bf16[256,576]{0,1:T(8,128)(2,1)}, u32[]{:S(2)}) copy-start(bf16[256,576]{0,1:T(8,128)(2,1)} %param.8) | copy-start | bytes 884740
  0.6 2.1 %copy-start = (bf16[256,576]{0,1:T(8,128)(2,1)S(1)}, bf16[256,576]{0,1:T(8,128)(2,1)}, u32[]{:S(2)}) copy-start(bf16[256,576]{0,1:T(8,128)(2,1)} %param.7) | copy-start | bytes 884740
  2.8 12.3 %collective-permute-start = (bf16[1152,256]{1,0:T(8,128)(2,1)S(1)}, bf16[1152,256]{1,0:T(8,128)(2,1)S(1)}, u32[]{:S(2)}, u32[]{:S(2)}) collective-permute-start(bf16[1152,256]{1,0:T(8,128)(2,1)S(1)} %join_kernel.1.near_ref), channel_id=1, source_target_pairs={{0,8},{8,0},{1,9},{9,1},{2,10},{10,2},{3,11},{11,3},{4,12},{12,4},... | collective-permute-start | bytes 1769480 | tf_op jit(solution)/shard_map/ppermute | solution.py:401
  11.6 3.5 %copy-start.4 = (s32[3]{0:T(128)S(1)}, s32[3]{0:T(128)}, u32[]{:S(2)}) copy-start(s32[3]{0:T(128)} %exps_ref.1) | copy-start | bytes 40
  11.6 17.9 %all-to-all-start = ((bf16[8,224,128]{2,1,0:T(8,128)(2,1)}), bf16[8,224,128]{2,1,0:T(8,128)(2,1)S(1)}, u32[]{:S(2)}, u32[]{:S(2)}) async-start(bf16[8,224,128]{2,1,0:T(8,128)(2,1)} %bitcast.1), calls=%async_computation | async-start | bytes 917504 | tf_op jit(solution)/shard_map/all_to_all | solution.py:398
  15.1 14.4 %copy-start.2 = (f32[4608]{0:T(1024)S(1)}, f32[4608]{0:T(1024)}, u32[]{:S(2)}) copy-start(f32[4608]{0:T(1024)} %param.10) | copy-start | bytes 55300
  15.8 8.0 %collective-permute-start.1 = (bf16[128,512]{1,0:T(8,128)(2,1)S(1)}, bf16[128,512]{1,0:T(8,128)(2,1)S(1)}, u32[]{:S(2)}, u32[]{:S(2)}) collective-permute-start(bf16[128,512]{1,0:T(8,128)(2,1)S(1)} %get-tuple-element.25), channel_id=1, source_target_pairs={{0,1},{1,0},{2,3},{3,2},{4,5},{5,4},{6,7},{7,6},{8,9},{9,8},{10,11... | collective-permute-start | bytes 393224 | tf_op jit(solution)/shard_map/ppermute | solution.py:405
  30.1 10.4 %copy-start.6 = (bf16[384,640]{1,0:T(8,128)(2,1)}, bf16[384,640]{1,0:T(8,128)(2,1)S(1)}, u32[]{:S(2)}) copy-start(bf16[384,640]{1,0:T(8,128)(2,1)S(1)} %get-tuple-element.31.w_ref) | copy-start | bytes 1474564
  49.6 8.9 %copy-start.3 = (s32[4608]{0:T(1024)S(1)}, s32[4608]{0:T(1024)}, u32[]{:S(2)}) copy-start(s32[4608]{0:T(1024)} %param.12) | copy-start | bytes 55300
  49.6 8.9 %copy-start.5 = (bf16[256,256]{1,0:T(8,128)(2,1)S(1)}, bf16[256,256]{1,0:T(8,128)(2,1)}, u32[]{:S(2)}) copy-start(bf16[256,256]{1,0:T(8,128)(2,1)} %constant.2.clone.table_ref) | copy-start | bytes 393220
  60.8 11.1 %copy-start.7 = (bf16[384,640]{1,0:T(8,128)(2,1)S(1)}, bf16[384,640]{1,0:T(8,128)(2,1)}, u32[]{:S(2)}) copy-start(bf16[384,640]{1,0:T(8,128)(2,1)} %copy-done.6) | copy-start | bytes 1474564
  60.8 27.0 %all-to-all-start.3 = ((bf16[64,32,128]{2,1,0:T(8,128)(2,1)}), bf16[64,32,128]{2,1,0:T(8,128)(2,1)S(1)}, u32[]{:S(2)}, u32[]{:S(2)}) async-start(bf16[64,32,128]{2,1,0:T(8,128)(2,1)} %bitcast.8), calls=%async_computation.3 | async-start | bytes 1048576 | tf_op jit(solution)/shard_map/all_to_all | solution.py:424
  72.4 8.4 %collective-permute-start.2 = (bf16[576,256]{1,0:T(8,128)(2,1)S(1)}, bf16[576,256]{1,0:T(8,128)(2,1)S(1)}, u32[]{:S(2)}, u32[]{:S(2)}) collective-permute-start(bf16[576,256]{1,0:T(8,128)(2,1)S(1)} %get-tuple-element.35), channel_id=1, source_target_pairs={{0,8},{8,0},{1,9},{9,1},{2,10},{10,2},{3,11},{11,3},{4,12},{12,4},... | collective-permute-start | bytes 884744 | tf_op jit(solution)/shard_map/ppermute | solution.py:428

commit v8 on v7

--- a/solution.py
+++ b/solution.py
@@ -227,12 +227,13 @@
     sign = 2.0 * feature_column(sign_ref, first_block, odd) - 1.0
     gain = feature_column(gain_ref, first_block, odd) * sign
     theirs = (lax.broadcasted_iota(jnp.int32, (128, 512), 0) >= 64) == (odd == 0)
-    rights = []
-    for part, (ref, factor) in enumerate(((xa_ref, inv_ref[0:1, :]), (ga_ref, None))):
+
+    def right_of(part, ref, row, column):
         other = half_ref[part * 64 : part * 64 + 64, :].astype(F32)
         shared = jnp.where(theirs, jnp.concatenate([other, other], axis=0), ref[512:640, :].astype(F32))
         values = jnp.concatenate([ref[0:512, :].astype(F32), shared], axis=0)
-        rights.append((values * sign if factor is None else values * factor * gain).astype(BF16))
+        return ((values if row is None else values * row) * column).astype(BF16)
+
     for s in range(27, 32):
         term_ref[s] = jnp.zeros((64, 128), BF16)
     copies = []
@@ -242,7 +243,9 @@
         copy.start()
         copies.append(copy)
 
-    for matrices, right in (((2,), rights[1]), ((0, 1), rights[0])):
+    send(27, 5)
+    for matrices in ((2,), (0, 1)):
+        right = right_of(1, ga_ref, None, sign) if matrices == (2,) else right_of(0, xa_ref, inv_ref[0:1, :], gain)
         acts = jnp.concatenate([gathered_acts(acts_ref, k) for k in matrices], axis=0)
         height = acts.shape[0]
         terms = jnp.concatenate(
@@ -278,7 +281,7 @@
                     send(k * 8 + first // 128, 2)
                     send(k * 8 + 4 + first // 128, 2)
                 elif k == 1:
-                    send(24, 8)
+                    send(24, 3)
     for copy in copies:
         copy.wait()
 
@@ -417,7 +420,7 @@
     (terms,) = call(
         gradient_kernel,
         [((32, 64, 128), BF16)],
-        scratch=[pltpu.VMEM((32, 64, 128), BF16), pltpu.SemaphoreType.DMA((13,))],
+        scratch=[pltpu.VMEM((32, 64, 128), BF16), pltpu.SemaphoreType.DMA((14,))],
         out_space=pl.ANY,
     )(acts, xa, ga, other_half, inverse, gain, signs, table, scales)
 

time: 120 us -> 120 us (level)
  no operation moved by 1% of the time
where the time goes in v8:
time: 120 us; the launch traced here: 119 us
  blocking collectives  58 us (48%)
  starting transfers between devices  33.8 us (28%)
  waiting for transfers between devices  17.7 us (15%)
  Pallas kernels  8.55 us (7%)
    all_to_all x1, blocking collectives, per_device(): share = lax.all_to_all(share, ('z', 'yl', 'x'), 0, 0).reshape(32, 64, 128)  20.8 us
    all_to_all x1, starting transfers between devices, per_device(): lax.all_to_all(terms.reshape(64, 32, 128), ('z', 'yl', 'yh'), 0, 0)  11.1 us
    all_to_all x1, blocking collectives, per_device(): parts = lax.all_to_all(parts, 'x', 0, 0)  10.3 us
    all_gather x1, blocking collectives, per_device(): both = lax.all_gather(share[0:27], 'c', axis=0)  9.14 us
    all_gather x1, blocking collectives, per_device(): sums = lax.all_gather(sums, 'yh', axis=0)  8.92 us
    all_to_all x1, blocking collectives, per_device(): acts = lax.all_to_all(message, 'x', 0, 0)  8.91 us
    ppermute x1, starting transfers between devices, per_device(): far = lax.ppermute(near, 'c', cores)  8.79 us
    pallas_call x11, Pallas kernels, run(): pl.pallas_call(kernel, out_shape=[jax.ShapeDtypeStruct(shape, dtype) for...  8.55 us
  transfers between devices with their start and end apart: 5, of which 4 were waited for; matrix products, arithmetic and copies ran while one was open for 0% of the time, Pallas kernels for 2%

profile of v8, /device:TPU:1, one launch (start us, length us, event | category | flops | bytes accessed | tf_op | source)
XLA Modules:
  0.0 119.0 jit_solution(2963636363554577501)
XLA Ops:
  0.6 0.0 copy-start.1
  0.6 2.0 %prepare_kernel.1 = bf16[8,14,16,128]{3,2,1,0:T(8,128)(2,1)} custom-call(bf16[3,32,4608]{2,1,0:T(8,128)(2,1)} %w_ref.1), custom_call_target="tpu_custom_call" | custom-call | flops 1000000000 | bytes 1000000 | tf_op jit(solution)/shard_map/prepare_kernel/pallas_call | solution.py:366
  2.8 8.8 %collective-permute-start = (bf16[1152,256]{1,0:T(8,128)(2,1)S(1)}, bf16[1152,256]{1,0:T(8,128)(2,1)S(1)}, u32[]{:S(2)}, u32[]{:S(2)}) collective-permute-start(bf16[1152,256]{1,0:T(8,128)(2,1)S(1)} %join_kernel.1.near_ref), channel_id=1, source_target_pairs={{0,8},{8,0},{1,9},{9,1},{2,10},{10,2},{3,11},{11,3},{4,12},{12,4},... | collective-permute-start | bytes 1769480 | tf_op jit(solution)/shard_map/ppermute | solution.py:404
  11.6 0.0 copy-start.4
  11.6 3.5 %all-to-all-start = ((bf16[8,224,128]{2,1,0:T(8,128)(2,1)}), bf16[8,224,128]{2,1,0:T(8,128)(2,1)S(1)}, u32[]{:S(2)}, u32[]{:S(2)}) async-start(bf16[8,224,128]{2,1,0:T(8,128)(2,1)} %bitcast.1), calls=%async_computation | async-start | bytes 917504 | tf_op jit(solution)/shard_map/all_to_all | solution.py:401
  15.1 0.0 copy-start.2
  15.1 0.0 collective-permute-done.far_ref
  15.1 0.7 align_kernel.1
  15.8 3.3 %collective-permute-start.1 = (bf16[128,512]{1,0:T(8,128)(2,1)S(1)}, bf16[128,512]{1,0:T(8,128)(2,1)S(1)}, u32[]{:S(2)}, u32[]{:S(2)}) collective-permute-start(bf16[128,512]{1,0:T(8,128)(2,1)S(1)} %get-tuple-element.25), channel_id=1, source_target_pairs={{0,1},{1,0},{2,3},{3,2},{4,5},{5,4},{6,7},{7,6},{8,9},{9,8},{10,11... | collective-permute-start | bytes 393224 | tf_op jit(solution)/shard_map/ppermute | solution.py:408
  19.1 4.7 %collective-permute-done.1._.half_ref = bf16[128,512]{1,0:T(8,128)(2,1)S(1)} collective-permute-done((bf16[128,512]{1,0:T(8,128)(2,1)S(1)}, bf16[128,512]{1,0:T(8,128)(2,1)S(1)}, u32[]{:S(2)}, u32[]{:S(2)}) %collective-permute-start.1) | collective-permute-done | bytes 131104 | tf_op jit(solution)/shard_map/ppermute | solution.py:408
  23.8 5.6 %all-to-all-done = bf16[8,224,128]{2,1,0:T(8,128)(2,1)S(1)} async-done(((bf16[8,224,128]{2,1,0:T(8,128)(2,1)}), bf16[8,224,128]{2,1,0:T(8,128)(2,1)S(1)}, u32[]{:S(2)}, u32[]{:S(2)}) %all-to-all-start) | async-done | bytes 458784 | tf_op jit(solution)/shard_map/all_to_all | solution.py:401
  29.4 0.7 forward_kernel.1
  30.1 10.3 %all_to_all.25.parts_ref = bf16[4,104,512]{2,1,0:T(8,128)(2,1)S(1)} all-to-all(bf16[4,104,512]{2,1,0:T(8,128)(2,1)S(1)} %get-tuple-element.26), channel_id=1, replica_groups=mesh['z'=8,'yl'=4,'c'=2,'yh'=2,'x'=4] {'x'}, dimensions={0} | all-to-all | bytes 851968 | tf_op jit(solution)/shard_map/all_to_all | solution.py:415
  40.4 0.1 sum_kernel.1
  40.5 0.0 copy-done.6
  40.5 8.9 %all-gather = bf16[208,512]{1,0:T(8,128)(2,1)S(1)} all-gather(bf16[104,512]{1,0:T(8,128)(2,1)S(1)} %get-tuple-element.28), channel_id=2, replica_groups=mesh['z'=8,'yl'=4,'c'=2,'yh'=2,'x'=4] {'yh'}, dimensions={0}, use_global_device_ids=true | all-gather | bytes 319488 | tf_op jit(solution)/shard_map/all_gather | solution.py:417
  49.4 0.1 activation_kernel.1
  49.6 0.0 copy-start.3
  49.6 0.0 copy-start.5
  49.6 8.9 %all_to_all.26.acts_ref = bf16[4,104,512]{2,1,0:T(8,128)(2,1)S(1)} all-to-all(bf16[4,104,512]{2,1,0:T(8,128)(2,1)S(1)} %get-tuple-element.30), channel_id=1, replica_groups=mesh['z'=8,'yl'=4,'c'=2,'yh'=2,'x'=4] {'x'}, dimensions={0} | all-to-all | bytes 851968 | tf_op jit(solution)/shard_map/all_to_all | solution.py:419
  58.5 0.0 copy-done.3
  58.5 2.2 %gradient_kernel.1._ = bf16[32,64,128]{2,1,0:T(8,128)(2,1)} custom-call(bf16[4,104,512]{2,1,0:T(8,128)(2,1)S(1)} %all_to_all.26.acts_ref, bf16[640,512]{1,0:T(8,128)(2,1)S(1)} %get-tuple-element.22.xa_ref, bf16[640,512]{1,0:T(8,128)(2,1)S(1)} %get-tuple-element.23.ga_ref, bf16[128,512]{1,0:T(8,128)(2,1)S(1)} %collective-permute-done.1._.half_ref, ...), custom_call_target="tpu_custom_call" | custom-call | flops 1000000000 | bytes 1000000 | tf_op jit(solution)/shard_map/gradient_kernel/pallas_call | solution.py:366
  60.8 11.1 %all-to-all-start.3 = ((bf16[64,32,128]{2,1,0:T(8,128)(2,1)}), bf16[64,32,128]{2,1,0:T(8,128)(2,1)S(1)}, u32[]{:S(2)}, u32[]{:S(2)}) async-start(bf16[64,32,128]{2,1,0:T(8,128)(2,1)} %bitcast.8), calls=%async_computation.3 | async-start | bytes 1048576 | tf_op jit(solution)/shard_map/all_to_all | solution.py:427
  71.9 0.5 resid_kernel.1
  72.4 7.2 %collective-permute-start.2 = (bf16[576,256]{1,0:T(8,128)(2,1)S(1)}, bf16[576,256]{1,0:T(8,128)(2,1)S(1)}, u32[]{:S(2)}, u32[]{:S(2)}) collective-permute-start(bf16[576,256]{1,0:T(8,128)(2,1)S(1)} %get-tuple-element.35), channel_id=1, source_target_pairs={{0,8},{8,0},{1,9},{9,1},{2,10},{10,2},{3,11},{11,3},{4,12},{12,4},... | collective-permute-start | bytes 884744 | tf_op jit(solution)/shard_map/ppermute | solution.py:431
  79.6 1.2 collective-permute-done.2.far_ref
  80.8 0.8 finish_kernel.1
  81.6 6.2 %all-to-all-done.3.terms_ref = bf16[64,32,128]{2,1,0:T(8,128)(2,1)S(1)} async-done(((bf16[64,32,128]{2,1,0:T(8,128)(2,1)}), bf16[64,32,128]{2,1,0:T(8,128)(2,1)S(1)}, u32[]{:S(2)}, u32[]{:S(2)}) %all-to-all-start.3) | async-done | bytes 524320 | tf_op jit(solution)/shard_map/all_to_all | solution.py:427
  87.7 0.1 total_kernel.1
  87.9 20.8 %all_to_all.27 = bf16[128,16,128]{2,1,0:T(8,128)(2,1)S(1)} all-to-all(bf16[128,16,128]{2,1,0:T(8,128)(2,1)S(1)} %total_kernel.1), channel_id=1, replica_groups=mesh['z'=8,'yl'=4,'c'=2,'yh'=2,'x'=4] {'z','yl','x'}, dimensions={0} | all-to-all | bytes 1048576 | tf_op jit(solution)/shard_map/all_to_all | solution.py:434
  108.7 9.1 %all_gather.15.both_ref = bf16[2,27,64,128]{3,2,1,0:T(8,128)(2,1)S(1)} all-gather(bf16[1,27,64,128]{3,2,1,0:T(8,128)(2,1)S(1)} %bitcast.20), channel_id=1, replica_groups=mesh['z'=8,'yl'=4,'c'=2,'yh'=2,'x'=4] {'c'}, dimensions={0}, use_global_device_ids=true | all-gather | bytes 1327104 | tf_op jit(solution)/shard_map/all_gather | solution.py:435
  117.8 1.2 restore_kernel.1
  (11 shorter events, 0.1 us)
Async XLA Ops:
  0.6 2.1 %copy-start.1 = (bf16[256,576]{0,1:T(8,128)(2,1)S(1)}, bf16[256,576]{0,1:T(8,128)(2,1)}, u32[]{:S(2)}) copy-start(bf16[256,576]{0,1:T(8,128)(2,1)} %param.8) | copy-start | bytes 884740
  0.6 2.1 %copy-start = (bf16[256,576]{0,1:T(8,128)(2,1)S(1)}, bf16[256,576]{0,1:T(8,128)(2,1)}, u32[]{:S(2)}) copy-start(bf16[256,576]{0,1:T(8,128)(2,1)} %param.7) | copy-start | bytes 884740
  2.8 12.3 %collective-permute-start = (bf16[1152,256]{1,0:T(8,128)(2,1)S(1)}, bf16[1152,256]{1,0:T(8,128)(2,1)S(1)}, u32[]{:S(2)}, u32[]{:S(2)}) collective-permute-start(bf16[1152,256]{1,0:T(8,128)(2,1)S(1)} %join_kernel.1.near_ref), channel_id=1, source_target_pairs={{0,8},{8,0},{1,9},{9,1},{2,10},{10,2},{3,11},{11,3},{4,12},{12,4},... | collective-permute-start | bytes 1769480 | tf_op jit(solution)/shard_map/ppermute | solution.py:404
  11.6 3.5 %copy-start.4 = (s32[3]{0:T(128)S(1)}, s32[3]{0:T(128)}, u32[]{:S(2)}) copy-start(s32[3]{0:T(128)} %exps_ref.1) | copy-start | bytes 40
  11.6 17.9 %all-to-all-start = ((bf16[8,224,128]{2,1,0:T(8,128)(2,1)}), bf16[8,224,128]{2,1,0:T(8,128)(2,1)S(1)}, u32[]{:S(2)}, u32[]{:S(2)}) async-start(bf16[8,224,128]{2,1,0:T(8,128)(2,1)} %bitcast.1), calls=%async_computation | async-start | bytes 917504 | tf_op jit(solution)/shard_map/all_to_all | solution.py:401
  15.1 14.4 %copy-start.2 = (f32[4608]{0:T(1024)S(1)}, f32[4608]{0:T(1024)}, u32[]{:S(2)}) copy-start(f32[4608]{0:T(1024)} %param.10) | copy-start | bytes 55300
  15.8 8.0 %collective-permute-start.1 = (bf16[128,512]{1,0:T(8,128)(2,1)S(1)}, bf16[128,512]{1,0:T(8,128)(2,1)S(1)}, u32[]{:S(2)}, u32[]{:S(2)}) collective-permute-start(bf16[128,512]{1,0:T(8,128)(2,1)S(1)} %get-tuple-element.25), channel_id=1, source_target_pairs={{0,1},{1,0},{2,3},{3,2},{4,5},{5,4},{6,7},{7,6},{8,9},{9,8},{10,11... | collective-permute-start | bytes 393224 | tf_op jit(solution)/shard_map/ppermute | solution.py:408
  30.1 10.4 %copy-start.6 = (bf16[384,640]{1,0:T(8,128)(2,1)}, bf16[384,640]{1,0:T(8,128)(2,1)S(1)}, u32[]{:S(2)}) copy-start(bf16[384,640]{1,0:T(8,128)(2,1)S(1)} %get-tuple-element.31.w_ref) | copy-start | bytes 1474564
  49.6 8.9 %copy-start.3 = (s32[4608]{0:T(1024)S(1)}, s32[4608]{0:T(1024)}, u32[]{:S(2)}) copy-start(s32[4608]{0:T(1024)} %param.12) | copy-start | bytes 55300
  49.6 8.9 %copy-start.5 = (bf16[256,256]{1,0:T(8,128)(2,1)S(1)}, bf16[256,256]{1,0:T(8,128)(2,1)}, u32[]{:S(2)}) copy-start(bf16[256,256]{1,0:T(8,128)(2,1)} %constant.2.clone.table_ref) | copy-start | bytes 393220
  60.7 11.1 %copy-start.7 = (bf16[384,640]{1,0:T(8,128)(2,1)S(1)}, bf16[384,640]{1,0:T(8,128)(2,1)}, u32[]{:S(2)}) copy-start(bf16[384,640]{1,0:T(8,128)(2,1)} %copy-done.6) | copy-start | bytes 1474564
  60.8 27.0 %all-to-all-start.3 = ((bf16[64,32,128]{2,1,0:T(8,128)(2,1)}), bf16[64,32,128]{2,1,0:T(8,128)(2,1)S(1)}, u32[]{:S(2)}, u32[]{:S(2)}) async-start(bf16[64,32,128]{2,1,0:T(8,128)(2,1)} %bitcast.8), calls=%async_computation.3 | async-start | bytes 1048576 | tf_op jit(solution)/shard_map/all_to_all | solution.py:427
  72.4 8.4 %collective-permute-start.2 = (bf16[576,256]{1,0:T(8,128)(2,1)S(1)}, bf16[576,256]{1,0:T(8,128)(2,1)S(1)}, u32[]{:S(2)}, u32[]{:S(2)}) collective-permute-start(bf16[576,256]{1,0:T(8,128)(2,1)S(1)} %get-tuple-element.35), channel_id=1, source_target_pairs={{0,8},{8,0},{1,9},{9,1},{2,10},{10,2},{3,11},{11,3},{4,12},{12,4},... | collective-permute-start | bytes 884744 | tf_op jit(solution)/shard_map/ppermute | solution.py:431
